TPU v7x, 32 devices: a whole 2x2x4 slice. The times are simulated.
32 devices in a mesh: dp: 2 (over x), expert: 16 (over z, y, core).
Axes of the slice: x: 2, y: 2, z: 4, core: 2. Of those that a mesh axis runs over, the one named last changes fastest.
Arguments:
- layer_input: bfloat16 [2, 2, 2048, 2048], P('dp', None, 'expert'), may hold values from -6 to 6
- cotangent: bfloat16 [2, 2, 2048, 2048], P('dp', None, 'expert'), may hold values from -6 to 6
- doc_lengths: int32 [2, 2, 6], P('dp'), may hold values from 1 to 1024, 2048 in all within a row
- routes: int32 [2, 2, 2048, 6], P('dp', None, 'expert'), may hold values from 0 to 15, all different within a row
- attention_gain: bfloat16 [2048], P(('dp', 'expert')), may hold values from 0.099609375 to 1.8984375
- query_weight: bfloat16 [2048, 3072], P(('dp', 'expert')), may hold values from -0.125 to 0.125
- latent_weight: bfloat16 [2048, 576], P(('dp', 'expert')), may hold values from -0.125 to 0.125
- latent_gain: bfloat16 [512], P(('dp', 'expert')), may hold values from 0.099609375 to 1.8984375
- expand_weight: bfloat16 [512, 4096], P(('dp', 'expert')), may hold values from -0.25 to 0.25
- output_weight: bfloat16 [2048, 2048], P(None, ('dp', 'expert')), may hold values from -2 to 2
- feed_gain: bfloat16 [2048], P(('dp', 'expert')), may hold values from 0.099609375 to 1.8984375
- router_weight: bfloat16 [2048, 16], P(('dp', 'expert')), may hold values from -0.0625 to 0.0625
- shared_gate: bfloat16 [2048, 2816], P(('dp', 'expert')), may hold values from -0.125 to 0.125
- shared_up: bfloat16 [2048, 2816], P(('dp', 'expert')), may hold values from -0.125 to 0.125
- shared_down: bfloat16 [2816, 2048], P(('dp', 'expert')), may hold values from -0.109375 to 0.109375
- expert_gate: bfloat16 [16, 2048, 1408], P('expert', 'dp'), may hold values from -0.125 to 0.125
- expert_up: bfloat16 [16, 2048, 1408], P('expert', 'dp'), may hold values from -0.125 to 0.125
- expert_down: bfloat16 [16, 1408, 2048], P('expert', None, 'dp'), may hold values from -2.5 to 2.5
Outputs:
- layer_output: bfloat16 [2, 2, 2048, 2048], P('dp', None, 'expert')
- input_grad: float32 [2, 2, 2048, 2048], P('dp', None, 'expert')
- attention_gain_grad: float32 [2048], P(('dp', 'expert'))
- query_weight_grad: float32 [2048, 3072], P(('dp', 'expert'))
- latent_weight_grad: float32 [2048, 576], P(('dp', 'expert'))
- latent_gain_grad: float32 [512], P(('dp', 'expert'))
- expand_weight_grad: float32 [512, 4096], P(('dp', 'expert'))
- output_weight_grad: float32 [2048, 2048], P(None, ('dp', 'expert'))
- feed_gain_grad: float32 [2048], P(('dp', 'expert'))
- router_weight_grad: float32 [2048, 16], P(('dp', 'expert'))
- shared_gate_grad: float32 [2048, 2816], P(('dp', 'expert'))
- shared_up_grad: float32 [2048, 2816], P(('dp', 'expert'))
- shared_down_grad: float32 [2816, 2048], P(('dp', 'expert'))
- expert_gate_grad: float32 [16, 2048, 1408], P('expert', 'dp')
- expert_up_grad: float32 [16, 2048, 1408], P('expert', 'dp')
- expert_down_grad: float32 [16, 1408, 2048], P('expert', None, 'dp')
Inputs may be any that keep to these rules, and one draw needn't show every extreme that they name: `doc_lengths`: each row holds the lengths of the 6 documents packed in order into one sequence; they sum to 2048. `routes`: each token names 6 different experts, in the order of its gates.
All inputs are finite; a program needn't handle non-finite values.
Results may differ from a plain program's by a relative error of at most 0.02.
Values may be sent and summed in bfloat16 or wider, within the bound.
A program may use at most 320 MiB of HBM per device.

v0:
```python
import math

import jax
import jax.numpy as jnp
from jax import lax
from jax.sharding import PartitionSpec as P

D = 2048
H = 16
NOPE = 128
ROPE = 64
VDIM = 128
LAT = 512
TOP = 6
WINDOW = 1024
MICRO = 2


EPSILON = 1e-06
NEGATIVE = -1e30
HIGHEST_PRECISION = lax.Precision.HIGHEST


def passed_along(x, axis, by):
    size = lax.axis_size(axis)
    pairs = [(i, i + by) for i in range(size) if 0 <= i + by < size]
    return lax.ppermute(x, axis, pairs)


def root_normalize(values, gain):
    inverse = lax.rsqrt(jnp.mean(values * values, axis=-1, keepdims=True) + EPSILON)
    return values * inverse * gain


def normalize_back(values, gain, incoming):
    result, pullback = jax.vjp(root_normalize, values, gain)
    return pullback(incoming)


def silu_product(left, right):
    return jax.nn.silu(left) * right


def silu_back(left, right, incoming):
    result, pullback = jax.vjp(silu_product, left, right)
    return pullback(incoming)


def angles(positions):
    half_width = ROPE // 2
    frequency = jnp.exp(
        jnp.arange(half_width, dtype=jnp.float32) * (-math.log(10000.0) / half_width)
    )
    turned = positions.astype(jnp.float32)[:, None] * frequency[None, :]
    return (jnp.cos(turned), jnp.sin(turned))


def rotate(values, cosine_table, sine_table):
    half_width = values.shape[-1] // 2
    first = values[..., :half_width]
    second = values[..., half_width:]
    return jnp.concatenate(
        [first * cosine_table - second * sine_table, first * sine_table + second * cosine_table],
        axis=-1,
    )


def segment_of(positions, lengths):
    boundary = jnp.cumsum(lengths)
    return jnp.sum((boundary[None, :] <= positions[:, None]).astype(jnp.int32), axis=1)


def slot_table(choices, experts_count, capacity):
    flattened = choices.reshape(-1)
    onehot = (flattened[:, None] == jnp.arange(experts_count, dtype=jnp.int32)[None, :]).astype(
        jnp.int32
    )
    earlier = jnp.cumsum(onehot, axis=0) - onehot
    ranking = jnp.sum(earlier * onehot, axis=1)
    return (flattened * capacity + ranking, ranking < capacity)


def transposed_left(left, right):
    return lax.dot_general(
        left, right, (((0,), (0,)), ((), ())), preferred_element_type=jnp.float32
    )


def transposed_right(left, right):
    return lax.dot_general(
        left, right, (((1,), (1,)), ((), ())), preferred_element_type=jnp.float32
    )


def doubling_plan(reach_blocks):
    shift_plan = []
    covered = 0
    while covered < reach_blocks:
        blocks = min(covered + 1, reach_blocks - covered)
        shift_plan.append((blocks, covered + 1))
        covered = covered + blocks
    return shift_plan


def micro_step(token_rows, cotangent_rows, lengths, choices, gathered, experts_full):
    (
        attention_gain,
        query_weight,
        latent_weight,
        latent_gain,
        expand_weight,
        output_weight,
        feed_gain,
        router_weight,
        shared_gate,
        shared_up,
        shared_down,
    ) = gathered
    expert_gate = experts_full[0][0]
    expert_up = experts_full[1][0]
    expert_down = experts_full[2][0]
    tokens = token_rows.shape[0]
    lane_index = lax.axis_index("expert")
    score_scale = (NOPE + ROPE) ** (-0.5)
    key_width = H * (NOPE + ROPE)
    positions = lane_index * tokens + jnp.arange(tokens, dtype=jnp.int32)
    cosine_table, sine_table = angles(positions)
    head_cosine = cosine_table[:, None, :]
    head_sine = sine_table[:, None, :]
    inputs = token_rows.astype(jnp.float32)
    gain_first = attention_gain.astype(jnp.float32)
    gain_latent = latent_gain.astype(jnp.float32)
    gain_second = feed_gain.astype(jnp.float32)
    hidden = root_normalize(inputs, gain_first).astype(jnp.bfloat16)
    query_heads = jnp.dot(hidden, query_weight, preferred_element_type=jnp.float32).reshape(
        tokens, H, NOPE + ROPE
    )
    latent = jnp.dot(hidden, latent_weight, preferred_element_type=jnp.float32)
    compressed = root_normalize(latent[:, :LAT], gain_latent).astype(jnp.bfloat16)
    expanded = jnp.dot(compressed, expand_weight, preferred_element_type=jnp.float32).reshape(
        tokens, H, NOPE + VDIM
    )
    key_rope = rotate(latent[:, LAT:], cosine_table, sine_table)
    queries = jnp.concatenate(
        [query_heads[..., :NOPE], rotate(query_heads[..., NOPE:], head_cosine, head_sine)], axis=-1
    ).astype(jnp.bfloat16)
    key_heads = jnp.concatenate(
        [expanded[..., :NOPE], jnp.broadcast_to(key_rope[:, None, :], (tokens, H, ROPE))], axis=-1
    ).astype(jnp.bfloat16)
    value_heads = expanded[..., NOPE:].astype(jnp.bfloat16)
    reach_blocks = (WINDOW + tokens - 2) // tokens
    shift_plan = doubling_plan(reach_blocks)
    window = jnp.concatenate(
        [key_heads.reshape(tokens, key_width), value_heads.reshape(tokens, H * VDIM)], axis=1
    )
    for blocks, distance in shift_plan:
        incoming = passed_along(window[window.shape[0] - blocks * tokens :], "expert", distance)
        window = jnp.concatenate([incoming, window], axis=0)
    key_rows = window.shape[0]
    window_keys = window[:, :key_width].reshape(key_rows, H, NOPE + ROPE)
    window_values = window[:, key_width:].reshape(key_rows, H, VDIM)
    key_positions = (lane_index - reach_blocks) * tokens + jnp.arange(key_rows, dtype=jnp.int32)
    distance_grid = positions[:, None] - key_positions[None, :]
    allowed = (
        (key_positions[None, :] >= 0)
        & (distance_grid >= 0)
        & (distance_grid < WINDOW)
        & (segment_of(positions, lengths)[:, None] == segment_of(key_positions, lengths)[None, :])
    )

    def score_table():
        raw_scores = (
            jnp.einsum("qhd,khd->hqk", queries, window_keys, preferred_element_type=jnp.float32)
            * score_scale
        )
        return jnp.where(allowed[None], raw_scores, NEGATIVE)

    scores = score_table()
    highest = jnp.max(scores, axis=-1, keepdims=True)
    log_total = highest + jnp.log(jnp.sum(jnp.exp(scores - highest), axis=-1, keepdims=True))
    weights_low = jnp.exp(scores - log_total).astype(jnp.bfloat16)
    mixture = (
        jnp.einsum("hqk,khd->qhd", weights_low, window_values, preferred_element_type=jnp.float32)
        .reshape(tokens, H * VDIM)
        .astype(jnp.bfloat16)
    )
    residual = inputs + jnp.dot(mixture, output_weight, preferred_element_type=jnp.float32)
    normed = root_normalize(residual, gain_second).astype(jnp.bfloat16)
    gate_projected = jnp.dot(normed, shared_gate, preferred_element_type=jnp.float32)
    up_projected = jnp.dot(normed, shared_up, preferred_element_type=jnp.float32)
    shared_act = silu_product(gate_projected, up_projected).astype(jnp.bfloat16)
    shared_out = jnp.dot(shared_act, shared_down, preferred_element_type=jnp.float32)
    probabilities = jax.nn.softmax(
        jnp.dot(normed, router_weight, preferred_element_type=jnp.float32), axis=-1
    )
    experts_count = router_weight.shape[1]
    capacity = (9 * tokens * TOP + 8 * experts_count - 1) // (8 * experts_count)
    slots_total = experts_count * capacity
    slot_index, slot_kept = slot_table(choices, experts_count, capacity)
    matches = (
        (
            (slot_index[:, None] == jnp.arange(slots_total, dtype=jnp.int32)[None, :])
            & slot_kept[:, None]
        )
        .astype(jnp.float32)
        .reshape(tokens, TOP, slots_total)
    )
    chosen = (
        choices[:, :, None] == jnp.arange(experts_count, dtype=jnp.int32)[None, None, :]
    ).astype(jnp.float32)
    gate_values = jnp.sum(chosen * probabilities[:, None, :], axis=-1)
    picked = jnp.sum(matches, axis=1).astype(jnp.bfloat16)
    blending = jnp.sum(matches * gate_values[:, :, None], axis=1)
    outgoing = (
        transposed_left(picked, normed).astype(jnp.bfloat16).reshape(experts_count, capacity, D)
    )
    arrived = lax.all_to_all(outgoing, "expert", split_axis=0, concat_axis=0, tiled=True).reshape(
        -1, D
    )
    expert_gate_pre = jnp.dot(arrived, expert_gate, preferred_element_type=jnp.float32)
    expert_up_pre = jnp.dot(arrived, expert_up, preferred_element_type=jnp.float32)
    expert_act = silu_product(expert_gate_pre, expert_up_pre).astype(jnp.bfloat16)
    expert_result = (
        jnp.dot(expert_act, expert_down, preferred_element_type=jnp.float32)
        .astype(jnp.bfloat16)
        .reshape(experts_count, capacity, D)
    )
    returned = lax.all_to_all(
        expert_result, "expert", split_axis=0, concat_axis=0, tiled=True
    ).reshape(slots_total, D)
    kept_float = slot_kept.reshape(tokens, TOP).astype(jnp.float32)
    gathered_rows = (
        jnp.take(returned, jnp.where(slot_kept, slot_index, 0), axis=0)
        .reshape(tokens, TOP, D)
        .astype(jnp.float32)
    )
    mixture_out = jnp.sum((gate_values * kept_float)[:, :, None] * gathered_rows, axis=1)
    layer_output = (residual + shared_out + mixture_out).astype(jnp.bfloat16)
    grad_out = cotangent_rows.astype(jnp.float32)
    grad_shared = grad_out.astype(jnp.bfloat16)
    shared_down_grad = transposed_left(shared_act, grad_shared)
    shared_gate_back, shared_up_back = silu_back(
        gate_projected, up_projected, transposed_right(grad_shared, shared_down)
    )
    shared_gate_low = shared_gate_back.astype(jnp.bfloat16)
    shared_up_low = shared_up_back.astype(jnp.bfloat16)
    shared_gate_grad = transposed_left(normed, shared_gate_low)
    shared_up_grad = transposed_left(normed, shared_up_low)
    grad_normed = transposed_right(shared_gate_low, shared_gate) + transposed_right(
        shared_up_low, shared_up
    )
    slot_grad = (
        jnp.einsum("ts,td->sd", blending, grad_out, precision=HIGHEST_PRECISION)
        .astype(jnp.bfloat16)
        .reshape(experts_count, capacity, D)
    )
    sent_grad = lax.all_to_all(
        slot_grad, "expert", split_axis=0, concat_axis=0, tiled=True
    ).reshape(-1, D)
    expert_down_grad = transposed_left(expert_act, sent_grad)
    expert_gate_back, expert_up_back = silu_back(
        expert_gate_pre, expert_up_pre, transposed_right(sent_grad, expert_down)
    )
    expert_gate_low = expert_gate_back.astype(jnp.bfloat16)
    expert_up_low = expert_up_back.astype(jnp.bfloat16)
    expert_gate_grad = transposed_left(arrived, expert_gate_low)
    expert_up_grad = transposed_left(arrived, expert_up_low)
    rows_grad = (
        (
            transposed_right(expert_gate_low, expert_gate)
            + transposed_right(expert_up_low, expert_up)
        )
        .astype(jnp.bfloat16)
        .reshape(experts_count, capacity, D)
    )
    back_rows = lax.all_to_all(
        rows_grad, "expert", split_axis=0, concat_axis=0, tiled=True
    ).reshape(slots_total, D)
    grad_normed = grad_normed + jnp.dot(picked, back_rows, preferred_element_type=jnp.float32)
    gate_grad = jnp.sum(gathered_rows * grad_out[:, None, :], axis=-1) * kept_float
    prob_grad = jnp.sum(chosen * gate_grad[:, :, None], axis=1)
    logit_grad = (
        probabilities * (prob_grad - jnp.sum(prob_grad * probabilities, axis=-1, keepdims=True))
    ).astype(jnp.bfloat16)
    router_weight_grad = transposed_left(normed, logit_grad)
    grad_normed = grad_normed + transposed_right(logit_grad, router_weight)
    residual_extra, feed_gain_grad = normalize_back(residual, gain_second, grad_normed)
    grad_residual = grad_out + residual_extra
    grad_attn_out = grad_residual.astype(jnp.bfloat16)
    output_weight_grad = transposed_left(mixture, grad_attn_out)
    grad_mixture = (
        transposed_right(grad_attn_out, output_weight).astype(jnp.bfloat16).reshape(tokens, H, VDIM)
    )
    probs_again = jnp.exp(score_table() - log_total)
    grad_probs = jnp.einsum(
        "qhd,khd->hqk", grad_mixture, window_values, preferred_element_type=jnp.float32
    )
    grad_scores = (
        probs_again * (grad_probs - jnp.sum(grad_probs * probs_again, axis=-1, keepdims=True))
    ).astype(jnp.bfloat16)
    grad_queries = (
        jnp.einsum("hqk,khd->qhd", grad_scores, window_keys, preferred_element_type=jnp.float32)
        * score_scale
    )
    grad_keys = (
        jnp.einsum("hqk,qhd->khd", grad_scores, queries, preferred_element_type=jnp.float32)
        * score_scale
    )
    grad_values = jnp.einsum(
        "hqk,qhd->khd",
        probs_again.astype(jnp.bfloat16),
        grad_mixture,
        preferred_element_type=jnp.float32,
    )
    grad_window = jnp.concatenate(
        [grad_keys.reshape(key_rows, key_width), grad_values.reshape(key_rows, H * VDIM)], axis=1
    )
    for blocks, distance in reversed(shift_plan):
        leading = grad_window[: blocks * tokens]
        grad_window = grad_window[blocks * tokens :]
        arriving = passed_along(leading.astype(jnp.bfloat16), "expert", -distance).astype(
            leading.dtype
        )
        cut_point = grad_window.shape[0] - blocks * tokens
        grad_window = jnp.concatenate(
            [grad_window[:cut_point], grad_window[cut_point:] + arriving], axis=0
        )
    grad_keys_own = grad_window[:, :key_width].reshape(tokens, H, NOPE + ROPE)
    grad_values_own = grad_window[:, key_width:].reshape(tokens, H, VDIM)
    grad_key_rope = rotate(jnp.sum(grad_keys_own[..., NOPE:], axis=1), cosine_table, -sine_table)
    grad_expanded = (
        jnp.concatenate([grad_keys_own[..., :NOPE], grad_values_own], axis=-1)
        .reshape(tokens, H * (NOPE + VDIM))
        .astype(jnp.bfloat16)
    )
    expand_weight_grad = transposed_left(compressed, grad_expanded)
    latent_part, latent_gain_grad = normalize_back(
        latent[:, :LAT], gain_latent, transposed_right(grad_expanded, expand_weight)
    )
    grad_latent = jnp.concatenate([latent_part, grad_key_rope], axis=1).astype(jnp.bfloat16)
    latent_weight_grad = transposed_left(hidden, grad_latent)
    grad_query_rope = rotate(grad_queries[..., NOPE:], head_cosine, -head_sine)
    grad_query = (
        jnp.concatenate([grad_queries[..., :NOPE], grad_query_rope], axis=-1)
        .reshape(tokens, key_width)
        .astype(jnp.bfloat16)
    )
    query_weight_grad = transposed_left(hidden, grad_query)
    grad_hidden = transposed_right(grad_latent, latent_weight) + transposed_right(
        grad_query, query_weight
    )
    input_extra, attention_gain_grad = normalize_back(inputs, gain_first, grad_hidden)
    input_grad = grad_residual + input_extra
    weight_grads = (
        attention_gain_grad,
        query_weight_grad,
        latent_weight_grad,
        latent_gain_grad,
        expand_weight_grad,
        output_weight_grad,
        feed_gain_grad,
        router_weight_grad,
        shared_gate_grad,
        shared_up_grad,
        shared_down_grad,
    )
    expert_grads = (expert_gate_grad[None], expert_up_grad[None], expert_down_grad[None])
    return (layer_output, input_grad, weight_grads, expert_grads)


def body(
    layer_input,
    cotangent,
    doc_lengths,
    routes,
    attention_gain,
    query_weight,
    latent_weight,
    latent_gain,
    expand_weight,
    output_weight,
    feed_gain,
    router_weight,
    shared_gate,
    shared_up,
    shared_down,
    expert_gate,
    expert_up,
    expert_down,
):
    experts_full = (
        lax.all_gather(expert_gate, "dp", axis=1, tiled=True),
        lax.all_gather(expert_up, "dp", axis=1, tiled=True),
        lax.all_gather(expert_down, "dp", axis=2, tiled=True),
    )
    outputs = []
    input_grads = []
    weight_totals = None
    expert_totals = None
    for micro_index in range(MICRO):
        gathered = (
            lax.all_gather(attention_gain, ("dp", "expert"), axis=0, tiled=True),
            lax.all_gather(query_weight, ("dp", "expert"), axis=0, tiled=True),
            lax.all_gather(latent_weight, ("dp", "expert"), axis=0, tiled=True),
            lax.all_gather(latent_gain, ("dp", "expert"), axis=0, tiled=True),
            lax.all_gather(expand_weight, ("dp", "expert"), axis=0, tiled=True),
            lax.all_gather(output_weight, ("dp", "expert"), axis=1, tiled=True),
            lax.all_gather(feed_gain, ("dp", "expert"), axis=0, tiled=True),
            lax.all_gather(router_weight, ("dp", "expert"), axis=0, tiled=True),
            lax.all_gather(shared_gate, ("dp", "expert"), axis=0, tiled=True),
            lax.all_gather(shared_up, ("dp", "expert"), axis=0, tiled=True),
            lax.all_gather(shared_down, ("dp", "expert"), axis=0, tiled=True),
        )
        layer_output, input_grad, weight_grads, expert_grads = micro_step(
            layer_input[0, micro_index],
            cotangent[0, micro_index],
            doc_lengths[0, micro_index],
            routes[0, micro_index],
            gathered,
            experts_full,
        )
        outputs.append(layer_output)
        input_grads.append(input_grad)
        if weight_totals is None:
            weight_totals = weight_grads
            expert_totals = expert_grads
        else:
            weight_totals = jax.tree.map(jnp.add, weight_totals, weight_grads)
            expert_totals = jax.tree.map(jnp.add, expert_totals, expert_grads)
    weight_sums = (
        lax.psum_scatter(weight_totals[0], ("dp", "expert"), scatter_dimension=0, tiled=True),
        lax.psum_scatter(weight_totals[1], ("dp", "expert"), scatter_dimension=0, tiled=True),
        lax.psum_scatter(weight_totals[2], ("dp", "expert"), scatter_dimension=0, tiled=True),
        lax.psum_scatter(weight_totals[3], ("dp", "expert"), scatter_dimension=0, tiled=True),
        lax.psum_scatter(weight_totals[4], ("dp", "expert"), scatter_dimension=0, tiled=True),
        lax.psum_scatter(weight_totals[5], ("dp", "expert"), scatter_dimension=1, tiled=True),
        lax.psum_scatter(weight_totals[6], ("dp", "expert"), scatter_dimension=0, tiled=True),
        lax.psum_scatter(weight_totals[7], ("dp", "expert"), scatter_dimension=0, tiled=True),
        lax.psum_scatter(weight_totals[8], ("dp", "expert"), scatter_dimension=0, tiled=True),
        lax.psum_scatter(weight_totals[9], ("dp", "expert"), scatter_dimension=0, tiled=True),
        lax.psum_scatter(weight_totals[10], ("dp", "expert"), scatter_dimension=0, tiled=True),
    )
    expert_sums = (
        lax.psum_scatter(
            expert_totals[0].astype(jnp.bfloat16), "dp", scatter_dimension=1, tiled=True
        ).astype(jnp.float32),
        lax.psum_scatter(
            expert_totals[1].astype(jnp.bfloat16), "dp", scatter_dimension=1, tiled=True
        ).astype(jnp.float32),
        lax.psum_scatter(
            expert_totals[2].astype(jnp.bfloat16), "dp", scatter_dimension=2, tiled=True
        ).astype(jnp.float32),
    )
    return (
        jnp.stack(outputs)[None],
        jnp.stack(input_grads)[None],
        weight_sums[0],
        weight_sums[1],
        weight_sums[2],
        weight_sums[3],
        weight_sums[4],
        weight_sums[5],
        weight_sums[6],
        weight_sums[7],
        weight_sums[8],
        weight_sums[9],
        weight_sums[10],
        expert_sums[0],
        expert_sums[1],
        expert_sums[2],
    )


def solution(mesh):
    placed = (
        P("dp", None, "expert", None),
        P("dp", None, "expert", None),
        P("dp", None, None),
        P("dp", None, "expert", None),
        P(("dp", "expert")),
        P(("dp", "expert"), None),
        P(("dp", "expert"), None),
        P(("dp", "expert")),
        P(("dp", "expert"), None),
        P(None, ("dp", "expert")),
        P(("dp", "expert")),
        P(("dp", "expert"), None),
        P(("dp", "expert"), None),
        P(("dp", "expert"), None),
        P(("dp", "expert"), None),
        P("expert", "dp", None),
        P("expert", "dp", None),
        P("expert", None, "dp"),
    )
    return jax.shard_map(
        body,
        mesh=mesh,
        in_specs=placed,
        out_specs=(
            P("dp", None, "expert", None),
            P("dp", None, "expert", None),
            P(("dp", "expert")),
            P(("dp", "expert"), None),
            P(("dp", "expert"), None),
            P(("dp", "expert")),
            P(("dp", "expert"), None),
            P(None, ("dp", "expert")),
            P(("dp", "expert")),
            P(("dp", "expert"), None),
            P(("dp", "expert"), None),
            P(("dp", "expert"), None),
            P(("dp", "expert"), None),
            P("expert", "dp", None),
            P("expert", "dp", None),
            P("expert", None, "dp"),
        ),
        check_vma=False,
    )
```

profile of v0, /device:TPU:0, one launch (start us, length us, event | category | flops | bytes accessed | tf_op | source)
XLA Modules:
  0.0 3958.0 jit_solution(6758860745000510548)
XLA Ops:
  13.5 42.3 %all-reduce.7 = (bf16[2048]{0:T(1024)(128)(2,1)S(1)}, bf16[512]{0:T(512)(128)(2,1)S(1)}, bf16[2048]{0:T(1024)(128)(2,1)S(1)}) all-reduce(bf16[2048]{0:T(1024)(128)(2,1)S(1)} %dynamic-update-slice, bf16[512]{0:T(512)(128)(2,1)S(1)} %dynamic-update-slice.1, ...), channel_id=1, replica_groups=mesh['dp'=2,'expert'=16] {'dp','expert'}, use_global_device_ids=true, to_apply=%add | all-reduce | flops 4608 | bytes 18432
  56.2 15.5 all-gather.12.cloned.1.call-done
  78.7 57.0 %all-gather.14.cloned.1.call-done = bf16[512,4096]{1,0:T(8,128)(2,1)} async-done(((bf16[16,4096]{1,0:T(8,128)(2,1)}), bf16[512,4096]{1,0:T(8,128)(2,1)}) %all-gather.14.cloned.1.call-update) | async-done | bytes 4194320 | tf_op jit(solution)/shard_map/all_gather | solution.py:406
  149.1 21.8 collective-permute-start.2
  170.9 74.8 %collective-permute-done.2 = bf16[256,5120]{0,1:T(8,128)(2,1)} collective-permute-done((bf16[256,5120]{0,1:T(8,128)(2,1)}, bf16[256,5120]{0,1:T(8,128)(2,1)}, u32[]{:S(2)}, u32[]{:S(2)}) %collective-permute-start.2) | collective-permute-done | bytes 2621472 | tf_op jit(solution)/shard_map/ppermute | solution.py:27
  245.7 11.1 maximum_maximum_fusion
  256.8 36.4 collective-permute-start.3
  294.1 179.1 %all-gather = bf16[32,64,16]{1,2,0:T(8,128)(2,1)S(1)} all-gather(bf16[1,64,16]{1,2,0:T(8,128)(2,1)S(1)} %bitcast.492), channel_id=1, replica_groups=mesh['dp'=2,'expert'=16] {'dp','expert'}, dimensions={0}, use_global_device_ids=true | all-gather | bytes 67584 | tf_op jit(solution)/shard_map/all_gather | solution.py:409
  478.6 27.6 collective-permute-done
  525.5 16.2 copy.120
  564.0 10.4 convolution_convert_fusion.9
  594.1 31.0 all-to-all-start.4
  643.3 67.3 %all-to-all-done.4 = bf16[16,54,2048]{2,1,0:T(8,128)(2,1)} async-done(((bf16[16,54,2048]{2,1,0:T(8,128)(2,1)}), bf16[16,54,2048]{2,1,0:T(8,128)(2,1)}, u32[]{:S(2)}, u32[]{:S(2)}) %all-to-all-start.4) | async-done | bytes 3538976 | tf_op jit(solution)/shard_map/all_to_all | solution.py:257
  710.7 49.0 %all-to-all-start = ((bf16[16,54,2048]{2,1,0:T(8,128)(2,1)}), bf16[16,54,2048]{2,1,0:T(8,128)(2,1)}, u32[]{:S(2)}, u32[]{:S(2)}) async-start(bf16[16,54,2048]{2,1,0:T(8,128)(2,1)} %reshape.829), calls=%async_computation | async-start | bytes 7340032 | tf_op jit(solution)/shard_map/all_to_all | solution.py:217
  770.7 40.9 %collective-permute-start.6 = (bf16[256,5120]{0,1:T(8,128)(2,1)}, bf16[256,5120]{0,1:T(8,128)(2,1)}, u32[]{:S(2)}, u32[]{:S(2)}) collective-permute-start(bf16[256,5120]{0,1:T(8,128)(2,1)} %maximum_maximum_fusion.3), channel_id=1, source_target_pairs={{0,2},{1,3},{2,4},{3,5},{4,6},{5,7},{6,8},{7,9},{8,10},{9,11},{10,... | collective-permute-start | bytes 7864328 | tf_op jit(solution)/shard_map/ppermute | solution.py:27
  830.1 109.3 %collective-permute-start.4 = (bf16[128,5120]{0,1:T(8,128)(2,1)}, bf16[128,5120]{0,1:T(8,128)(2,1)}, u32[]{:S(2)}, u32[]{:S(2)}) collective-permute-start(bf16[128,5120]{0,1:T(8,128)(2,1)} %copy-done.83), channel_id=1, source_target_pairs={{0,8},{1,9},{2,10},{3,11},{4,12},{5,13},{6,14},{7,15},{16,24},{17,... | collective-permute-start | bytes 3932168 | tf_op jit(solution)/shard_map/ppermute | solution.py:27
  948.2 23.0 collective-permute-start.7
  976.0 10.5 fusion.13
  991.3 10.4 fusion.25
  1001.7 14.3 fusion.37
  1032.0 101.3 %all-to-all-start.1 = ((bf16[16,54,2048]{2,1,0:T(8,128)(2,1)}), bf16[16,54,2048]{2,1,0:T(8,128)(2,1)}, u32[]{:S(2)}, u32[]{:S(2)}) async-start(bf16[16,54,2048]{2,1,0:T(8,128)(2,1)} %reshape.831), calls=%async_computation.1 | async-start | bytes 7340032 | tf_op jit(solution)/shard_map/all_to_all | solution.py:228
  1159.4 11.6 fusion.21
  1184.9 16.9 all-to-all-done.1
  1201.8 90.8 %all-to-all-start.5 = ((bf16[16,54,2048]{2,1,0:T(8,128)(2,1)}), bf16[16,54,2048]{2,1,0:T(8,128)(2,1)}, u32[]{:S(2)}, u32[]{:S(2)}) async-start(bf16[16,54,2048]{2,1,0:T(8,128)(2,1)} %reshape.846), calls=%async_computation.5 | async-start | bytes 7340032 | tf_op jit(solution)/shard_map/all_to_all | solution.py:276
  1321.6 10.3 multiply_convert_fusion.7
  1382.3 17.6 all-to-all-start.6
  1407.6 60.8 %all-to-all-done.6 = bf16[16,54,2048]{2,1,0:T(8,128)(2,1)} async-done(((bf16[16,54,2048]{2,1,0:T(8,128)(2,1)}), bf16[16,54,2048]{2,1,0:T(8,128)(2,1)}, u32[]{:S(2)}, u32[]{:S(2)}) %all-to-all-start.6) | async-done | bytes 3538976 | tf_op jit(solution)/shard_map/all_to_all | solution.py:257
  1468.5 18.0 all-to-all-start.2
  1489.7 11.2 fusion.11
  1500.9 54.1 %all-to-all-done.2 = bf16[16,54,2048]{2,1,0:T(8,128)(2,1)} async-done(((bf16[16,54,2048]{2,1,0:T(8,128)(2,1)}), bf16[16,54,2048]{2,1,0:T(8,128)(2,1)}, u32[]{:S(2)}, u32[]{:S(2)}) %all-to-all-start.2) | async-done | bytes 3538976 | tf_op jit(solution)/shard_map/all_to_all | solution.py:217
  1567.7 12.0 fusion.40
  1589.6 17.7 all-to-all-start.3
  1622.3 11.1 fusion.229
  1634.3 41.6 %all-to-all-done.3 = bf16[16,54,2048]{2,1,0:T(8,128)(2,1)} async-done(((bf16[16,54,2048]{2,1,0:T(8,128)(2,1)}), bf16[16,54,2048]{2,1,0:T(8,128)(2,1)}, u32[]{:S(2)}, u32[]{:S(2)}) %all-to-all-start.3) | async-done | bytes 3538976 | tf_op jit(solution)/shard_map/all_to_all | solution.py:228
  1690.2 12.4 fusion.8
  1746.3 17.7 all-to-all-start.7
  1764.1 10.8 fusion.231
  1783.9 10.7 multiply_convert_fusion.6
  1808.8 10.7 fusion.10
  1819.7 15.9 all-to-all-done.7
  1848.1 10.8 multiply_reduce_fusion.1
  1872.7 11.3 multiply_reduce_fusion
  1917.9 16.8 fusion
  1942.2 13.9 fusion.1
  1965.3 11.0 fusion.3
  1980.1 18.5 fusion.2
  1998.6 130.9 %collective-permute-done.8 = bf16[128,5120]{0,1:T(8,128)(2,1)} collective-permute-done((bf16[128,5120]{0,1:T(8,128)(2,1)S(1)}, bf16[128,5120]{0,1:T(8,128)(2,1)}, u32[]{:S(2)}, u32[]{:S(2)}) %collective-permute-start.8) | collective-permute-done | bytes 1310752 | tf_op jit(solution)/shard_map/ppermute | solution.py:27
  2132.5 164.3 %collective-permute-done.12 = bf16[128,5120]{0,1:T(8,128)(2,1)} collective-permute-done((bf16[128,5120]{0,1:T(8,128)(2,1)}, bf16[128,5120]{0,1:T(8,128)(2,1)}, u32[]{:S(2)}, u32[]{:S(2)}) %collective-permute-start.12) | collective-permute-done | bytes 1310752 | tf_op jit(solution)/shard_map/ppermute | solution.py:27
  2298.7 10.2 fusion.4
  2314.7 10.4 fusion.5
  2329.6 46.4 %collective-permute-done.14 = bf16[256,5120]{0,1:T(8,128)(2,1)} collective-permute-done((bf16[256,5120]{0,1:T(8,128)(2,1)}, bf16[256,5120]{0,1:T(8,128)(2,1)}, u32[]{:S(2)}, u32[]{:S(2)}) %collective-permute-start.14) | collective-permute-done | bytes 2621472 | tf_op jit(solution)/shard_map/ppermute | solution.py:27
  2381.3 49.5 %collective-permute-done.10 = bf16[256,5120]{0,1:T(8,128)(2,1)S(1)} collective-permute-done((bf16[256,5120]{0,1:T(8,128)(2,1)S(1)}, bf16[256,5120]{0,1:T(8,128)(2,1)S(1)}, u32[]{:S(2)}, u32[]{:S(2)}) %collective-permute-start.10) | collective-permute-done | bytes 2621472 | tf_op jit(solution)/shard_map/ppermute | solution.py:27
  2464.7 15.0 convolution_add_fusion.2
  2490.2 15.0 convolution_add_fusion.1
  2516.0 15.0 convolution_add_fusion
  2559.6 10.5 fusion.125
  2570.1 17.0 convolution_add_fusion.3
  2656.7 10.4 fusion.226
  2682.7 64.5 %all-reduce.6 = (f32[2048]{0:T(1024)S(1)}, f32[512]{0:T(512)S(1)}, f32[2048]{0:T(1024)S(1)}) all-reduce(f32[2048]{0:T(1024)S(1)} %add.398, f32[512]{0:T(512)S(1)} %add.401, f32[2048]{0:T(1024)S(1)} %add.404), channel_id=2, replica_groups=mesh['dp'=2,'expert'=16] {'dp','expert'}, use_global_device_ids=true, to_apply=%region_52.54.clone | all-reduce | flops 4608 | bytes 36864
  2759.6 245.5 %reduce-scatter.22.cloned.1.call-done = f32[64,2816]{1,0:T(8,128)} async-done(((f32[2048,2816]{1,0:T(8,128)}), f32[64,2816]{1,0:T(8,128)}) %reduce-scatter.22.cloned.1.call-update) | async-done | bytes 720912 | tf_op jit(solution)/shard_map/reduce_scatter | solution.py:439
  3005.1 251.7 %reduce-scatter.24.cloned.1.call-done = f32[64,2816]{1,0:T(8,128)} async-done(((f32[2048,2816]{1,0:T(8,128)}), f32[64,2816]{1,0:T(8,128)}) %reduce-scatter.24.cloned.1.call-update) | async-done | bytes 720912 | tf_op jit(solution)/shard_map/reduce_scatter | solution.py:440
  3256.8 251.9 %reduce-scatter.26.cloned.1.call-done = f32[88,2048]{1,0:T(8,128)} async-done(((f32[2816,2048]{1,0:T(8,128)}), f32[88,2048]{1,0:T(8,128)}) %reduce-scatter.26.cloned.1.call-update) | async-done | bytes 720912 | tf_op jit(solution)/shard_map/reduce_scatter | solution.py:441
  3508.7 188.6 %reduce-scatter.20.cloned.1.call-done = f32[2048,64]{0,1:T(8,128)} async-done(((f32[2048,2048]{0,1:T(8,128)}), f32[2048,64]{0,1:T(8,128)}) %reduce-scatter.20.cloned.1.call-update) | async-done | bytes 524304 | tf_op jit(solution)/shard_map/reduce_scatter | solution.py:436
  3697.3 253.4 %reduce-scatter.14.cloned.1.call-done = f32[64,3072]{1,0:T(8,128)} async-done(((f32[2048,3072]{1,0:T(8,128)}), f32[64,3072]{1,0:T(8,128)}) %reduce-scatter.14.cloned.1.call-update) | async-done | bytes 786448 | tf_op jit(solution)/shard_map/reduce_scatter | solution.py:432
  (854 shorter events, 705.4 us)
Async XLA Ops:
  7.2 64.6 %all-gather.12.cloned.1.call-start = ((), (), s32[]{:S(2)}) async-start(), calls=%async_computation.19 | async-start | bytes 2703360 | tf_op jit(solution)/shard_map/all_gather | solution.py:404
  7.9 127.8 %all-gather.14.cloned.1.call-start = ((), (), s32[]{:S(2)}) async-start(), calls=%async_computation.20 | async-start | bytes 4325376 | tf_op jit(solution)/shard_map/all_gather | solution.py:406
  8.7 516.8 %all-gather.16.cloned.1.call-start = ((), (), s32[]{:S(2)}) async-start(), calls=%async_computation.21 | async-start | bytes 12976128 | tf_op jit(solution)/shard_map/all_gather | solution.py:403
  9.4 565.0 %all-gather.18.cloned.1.call-start = ((), (), s32[]{:S(2)}) async-start(), calls=%async_computation.22 | async-start | bytes 8650752 | tf_op jit(solution)/shard_map/all_gather | solution.py:407
  10.0 966.0 %all-gather.30.cloned.1.call-start = ((), (), s32[]{:S(2)}) async-start(), calls=%async_computation.28 | async-start | bytes 8650752 | tf_op jit(solution)/shard_map/all_gather | solution.py:394
  10.6 980.7 %all-gather.28.cloned.1.call-start = ((), (), s32[]{:S(2)}) async-start(), calls=%async_computation.27 | async-start | bytes 8650752 | tf_op jit(solution)/shard_map/all_gather | solution.py:393
  11.2 990.5 %all-gather.26.cloned.1.call-start = ((), (), s32[]{:S(2)}) async-start(), calls=%async_computation.26 | async-start | bytes 8650752 | tf_op jit(solution)/shard_map/all_gather | solution.py:392
  11.9 1295.5 %all-gather.20.cloned.1.call-start = ((), (), s32[]{:S(2)}) async-start(), calls=%async_computation.23 | async-start | bytes 11894784 | tf_op jit(solution)/shard_map/all_gather | solution.py:410
  12.7 1301.8 %all-gather.22.cloned.1.call-start = ((), (), s32[]{:S(2)}) async-start(), calls=%async_computation.24 | async-start | bytes 11894784 | tf_op jit(solution)/shard_map/all_gather | solution.py:411
  55.8 493.6 %copy-start.79 = (f32[2048]{0:T(1024)}, f32[2048]{0:T(1024)S(1)}, u32[]{:S(2)}) copy-start(f32[2048]{0:T(1024)S(1)} %convert_element_type.375) | copy-start | bytes 24580
  55.8 570.0 %copy-start.98 = (f32[512]{0:T(512)}, f32[512]{0:T(512)S(1)}, u32[]{:S(2)}) copy-start(f32[512]{0:T(512)S(1)} %convert_element_type.377) | copy-start | bytes 6148
  55.9 421.4 %copy-start.161 = (f32[32]{0:T(128)}, f32[32]{0:T(128)S(1)}, u32[]{:S(2)}) copy-start(f32[32]{0:T(128)S(1)} %multiply_exponential_fusion) | copy-start | bytes 388
  55.9 421.4 %copy-start.163 = (f32[128]{0:T(128)}, f32[128]{0:T(128)S(1)}, u32[]{:S(2)}) copy-start(f32[128]{0:T(128)S(1)} %fusion.210) | copy-start | bytes 1540
  56.2 485.5 %copy-start.129 = (f32[128]{0:T(128)}, f32[128]{0:T(128)S(1)}, u32[]{:S(2)}) copy-start(f32[128]{0:T(128)S(1)} %fusion.196) | copy-start | bytes 1540
  56.2 493.2 %copy-start.134 = (f32[128]{0:T(128)}, f32[128]{0:T(128)S(1)}, u32[]{:S(2)}) copy-start(f32[128]{0:T(128)S(1)} %fusion.199) | copy-start | bytes 1540
  141.4 4.8 collective-permute-start.1
  149.1 96.6 %collective-permute-start.2 = (bf16[256,5120]{0,1:T(8,128)(2,1)}, bf16[256,5120]{0,1:T(8,128)(2,1)}, u32[]{:S(2)}, u32[]{:S(2)}) collective-permute-start(bf16[256,5120]{0,1:T(8,128)(2,1)} %maximum_maximum_fusion.2), channel_id=1, source_target_pairs={{0,2},{1,3},{2,4},{3,5},{4,6},{5,7},{6,8},{7,9},{8,10},{9,11},{10,... | collective-permute-start | bytes 7864328 | tf_op jit(solution)/shard_map/ppermute | solution.py:27
  170.9 122.3 %copy-start.160 = (s32[1,2,128,6]{2,1,3,0:T(2,128)S(1)}, s32[1,2,128,6]{2,1,3,0:T(2,128)}, u32[]{:S(2)}) copy-start(s32[1,2,128,6]{2,1,3,0:T(2,128)} %param.23) | copy-start | bytes 18436
  170.9 122.8 %copy-start.175 = (s32[1,2,6]{2,1,0:T(2,128)S(1)}, s32[1,2,6]{2,1,0:T(2,128)}, u32[]{:S(2)}) copy-start(s32[1,2,6]{2,1,0:T(2,128)} %param.22) | copy-start | bytes 148
  170.9 123.1 %copy-start.170 = (bf16[64,16]{0,1:T(8,128)(2,1)S(1)}, bf16[64,16]{0,1:T(8,128)(2,1)}, u32[]{:S(2)}) copy-start(bf16[64,16]{0,1:T(8,128)(2,1)} %param.31) | copy-start | bytes 6148
  256.8 249.6 %collective-permute-start.3 = (bf16[512,5120]{0,1:T(8,128)(2,1)}, bf16[512,5120]{0,1:T(8,128)(2,1)}, u32[]{:S(2)}, u32[]{:S(2)}) collective-permute-start(bf16[512,5120]{0,1:T(8,128)(2,1)} %maximum_maximum_fusion), channel_id=1, source_target_pairs={{0,4},{1,5},{2,6},{3,7},{4,8},{5,9},{6,10},{7,11},{8,12},{9,13},{1... | collective-permute-start | bytes 15728648 | tf_op jit(solution)/shard_map/ppermute | solution.py:27
  293.3 289.6 %copy-start.118 = (s32[1,1,128,6]{2,3,1,0:T(8,128)}, s32[1,1,128,6]{2,3,1,0:T(8,128)S(1)}, u32[]{:S(2)}) copy-start(s32[1,1,128,6]{2,3,1,0:T(8,128)S(1)} %copy.177) | copy-start | bytes 9220
  294.1 287.0 %copy-start.104 = (f32[2048]{0:T(1024)}, f32[2048]{0:T(1024)S(1)}, u32[]{:S(2)}) copy-start(f32[2048]{0:T(1024)S(1)} %convert_element_type.390) | copy-start | bytes 24580
  475.7 30.5 collective-permute-start
  582.1 732.4 %copy-start.10 = (bf16[128,2048]{1,0:T(8,128)(2,1)}, bf16[128,2048]{1,0:T(8,128)(2,1)S(1)}, u32[]{:S(2)}) copy-start(bf16[128,2048]{1,0:T(8,128)(2,1)S(1)} %multiply_convert_fusion.11) | copy-start | bytes 1572868
  594.1 116.5 %all-to-all-start.4 = ((bf16[16,54,2048]{2,1,0:T(8,128)(2,1)}), bf16[16,54,2048]{2,1,0:T(8,128)(2,1)}, u32[]{:S(2)}, u32[]{:S(2)}) async-start(bf16[16,54,2048]{2,1,0:T(8,128)(2,1)} %reshape.844), calls=%async_computation.4 | async-start | bytes 7340032 | tf_op jit(solution)/shard_map/all_to_all | solution.py:257
  625.1 696.4 %all-gather.24.cloned.1.call-start = ((), (), s32[]{:S(2)}) async-start(), calls=%async_computation.25 | async-start | bytes 11894784 | tf_op jit(solution)/shard_map/all_gather | solution.py:412
  710.7 275.9 %all-to-all-start = ((bf16[16,54,2048]{2,1,0:T(8,128)(2,1)}), bf16[16,54,2048]{2,1,0:T(8,128)(2,1)}, u32[]{:S(2)}, u32[]{:S(2)}) async-start(bf16[16,54,2048]{2,1,0:T(8,128)(2,1)} %reshape.829), calls=%async_computation | async-start | bytes 7340032 | tf_op jit(solution)/shard_map/all_to_all | solution.py:217
  761.9 4.9 collective-permute-start.5
  770.7 168.7 %collective-permute-start.6 = (bf16[256,5120]{0,1:T(8,128)(2,1)}, bf16[256,5120]{0,1:T(8,128)(2,1)}, u32[]{:S(2)}, u32[]{:S(2)}) collective-permute-start(bf16[256,5120]{0,1:T(8,128)(2,1)} %maximum_maximum_fusion.3), channel_id=1, source_target_pairs={{0,2},{1,3},{2,4},{3,5},{4,6},{5,7},{6,8},{7,9},{8,10},{9,11},{10,... | collective-permute-start | bytes 7864328 | tf_op jit(solution)/shard_map/ppermute | solution.py:27
  829.4 118.8 %copy-start.116 = (s32[128,6]{0,1:T(8,128)}, s32[128,6]{0,1:T(8,128)S(1)}, u32[]{:S(2)}) copy-start(s32[128,6]{0,1:T(8,128)S(1)} %copy.135) | copy-start | bytes 9220
  829.5 523.5 %copy-start.147 = (pred[768]{0:T(1024)(128)(4,1)}, pred[768]{0:T(1024)(128)(4,1)S(1)}, u32[]{:S(2)}) copy-start(pred[768]{0:T(1024)(128)(4,1)S(1)} %get-tuple-element.49) | copy-start | bytes 2308
  830.1 303.2 %collective-permute-start.4 = (bf16[128,5120]{0,1:T(8,128)(2,1)}, bf16[128,5120]{0,1:T(8,128)(2,1)}, u32[]{:S(2)}, u32[]{:S(2)}) collective-permute-start(bf16[128,5120]{0,1:T(8,128)(2,1)} %copy-done.83), channel_id=1, source_target_pairs={{0,8},{1,9},{2,10},{3,11},{4,12},{5,13},{6,14},{7,15},{16,24},{17,... | collective-permute-start | bytes 3932168 | tf_op jit(solution)/shard_map/ppermute | solution.py:27
  948.2 186.6 %collective-permute-start.7 = (bf16[512,5120]{0,1:T(8,128)(2,1)}, bf16[512,5120]{0,1:T(8,128)(2,1)}, u32[]{:S(2)}, u32[]{:S(2)}) collective-permute-start(bf16[512,5120]{0,1:T(8,128)(2,1)} %maximum_maximum_fusion.1), channel_id=1, source_target_pairs={{0,4},{1,5},{2,6},{3,7},{4,8},{5,9},{6,10},{7,11},{8,12},{9,13},{1... | collective-permute-start | bytes 15728648 | tf_op jit(solution)/shard_map/ppermute | solution.py:27
  1032.0 169.9 %all-to-all-start.1 = ((bf16[16,54,2048]{2,1,0:T(8,128)(2,1)}), bf16[16,54,2048]{2,1,0:T(8,128)(2,1)}, u32[]{:S(2)}, u32[]{:S(2)}) async-start(bf16[16,54,2048]{2,1,0:T(8,128)(2,1)} %reshape.831), calls=%async_computation.1 | async-start | bytes 7340032 | tf_op jit(solution)/shard_map/all_to_all | solution.py:228
  1157.6 135.0 %copy-start.102 = (f32[16,128]{1,0:T(8,128)}, f32[16,128]{1,0:T(8,128)S(1)}, u32[]{:S(2)}) copy-start(f32[16,128]{1,0:T(8,128)S(1)} %log_add_fusion) | copy-start | bytes 24580
  1201.8 159.2 %all-to-all-start.5 = ((bf16[16,54,2048]{2,1,0:T(8,128)(2,1)}), bf16[16,54,2048]{2,1,0:T(8,128)(2,1)}, u32[]{:S(2)}, u32[]{:S(2)}) async-start(bf16[16,54,2048]{2,1,0:T(8,128)(2,1)} %reshape.846), calls=%async_computation.5 | async-start | bytes 7340032 | tf_op jit(solution)/shard_map/all_to_all | solution.py:276
  1382.3 86.2 %all-to-all-start.6 = ((bf16[16,54,2048]{2,1,0:T(8,128)(2,1)}), bf16[16,54,2048]{2,1,0:T(8,128)(2,1)}, u32[]{:S(2)}, u32[]{:S(2)}) async-start(bf16[16,54,2048]{2,1,0:T(8,128)(2,1)} %reshape.853), calls=%async_computation.6 | async-start | bytes 7340032 | tf_op jit(solution)/shard_map/all_to_all | solution.py:257
  1468.5 86.5 %all-to-all-start.2 = ((bf16[16,54,2048]{2,1,0:T(8,128)(2,1)}), bf16[16,54,2048]{2,1,0:T(8,128)(2,1)}, u32[]{:S(2)}, u32[]{:S(2)}) async-start(bf16[16,54,2048]{2,1,0:T(8,128)(2,1)} %reshape.840), calls=%async_computation.2 | async-start | bytes 7340032 | tf_op jit(solution)/shard_map/all_to_all | solution.py:217
  1589.6 86.3 %all-to-all-start.3 = ((bf16[16,54,2048]{2,1,0:T(8,128)(2,1)}), bf16[16,54,2048]{2,1,0:T(8,128)(2,1)}, u32[]{:S(2)}, u32[]{:S(2)}) async-start(bf16[16,54,2048]{2,1,0:T(8,128)(2,1)} %reshape.842), calls=%async_computation.3 | async-start | bytes 7340032 | tf_op jit(solution)/shard_map/all_to_all | solution.py:228
  1607.3 1033.1 %reduce-scatter.34.cloned.1.call-start = ((), (), s32[]{:S(2)}) async-start(), calls=%async_computation.39 | async-start | bytes 1081344
  1690.1 951.8 %reduce-scatter.28.cloned.1.call-start = ((), (), s32[]{:S(2)}) async-start(), calls=%async_computation.36 | async-start | bytes 8650752 | tf_op jit(solution)/shard_map/reduce_scatter | solution.py:444
  1702.6 944.0 %reduce-scatter.30.cloned.1.call-start = ((), (), s32[]{:S(2)}) async-start(), calls=%async_computation.37 | async-start | bytes 8650752 | tf_op jit(solution)/shard_map/reduce_scatter | solution.py:447
  1746.3 89.4 %all-to-all-start.7 = ((bf16[16,54,2048]{2,1,0:T(8,128)(2,1)}), bf16[16,54,2048]{2,1,0:T(8,128)(2,1)}, u32[]{:S(2)}, u32[]{:S(2)}) async-start(bf16[16,54,2048]{2,1,0:T(8,128)(2,1)} %reshape.855), calls=%async_computation.7 | async-start | bytes 7340032 | tf_op jit(solution)/shard_map/all_to_all | solution.py:276
  1764.0 887.4 %reduce-scatter.32.cloned.1.call-start = ((), (), s32[]{:S(2)}) async-start(), calls=%async_computation.38 | async-start | bytes 8650752 | tf_op jit(solution)/shard_map/reduce_scatter | solution.py:450
  1819.7 932.9 %reduce-scatter.16.cloned.1.call-start = ((), (), s32[]{:S(2)}) async-start(), calls=%async_computation.30 | async-start | bytes 5406720 | tf_op jit(solution)/shard_map/reduce_scatter | solution.py:433
  1940.8 357.9 %collective-permute-start.13 = (bf16[512,5120]{0,1:T(8,128)(2,1)}, bf16[512,5120]{0,1:T(8,128)(2,1)}, u32[]{:S(2)}, u32[]{:S(2)}) collective-permute-start(bf16[512,5120]{0,1:T(8,128)(2,1)} %slice.368), channel_id=1, source_target_pairs={{4,0},{5,1},{6,2},{7,3},{8,4},{9,5},{10,6},{11,7},{12,8},{13,9},{1... | collective-permute-start | bytes 15728648 | tf_op jit(solution)/shard_map/ppermute | solution.py:27
  1962.7 166.8 %collective-permute-start.8 = (bf16[128,5120]{0,1:T(8,128)(2,1)S(1)}, bf16[128,5120]{0,1:T(8,128)(2,1)}, u32[]{:S(2)}, u32[]{:S(2)}) collective-permute-start(bf16[128,5120]{0,1:T(8,128)(2,1)S(1)} %slice.348), channel_id=1, source_target_pairs={{8,0},{9,1},{10,2},{11,3},{12,4},{13,5},{14,6},{15,7},{24,16},{25,... | collective-permute-start | bytes 3932168 | tf_op jit(solution)/shard_map/ppermute | solution.py:27
  1964.0 350.7 %collective-permute-start.9 = (bf16[512,5120]{0,1:T(8,128)(2,1)}, bf16[512,5120]{0,1:T(8,128)(2,1)}, u32[]{:S(2)}, u32[]{:S(2)}) collective-permute-start(bf16[512,5120]{0,1:T(8,128)(2,1)} %slice.349), channel_id=1, source_target_pairs={{4,0},{5,1},{6,2},{7,3},{8,4},{9,5},{10,6},{11,7},{12,8},{13,9},{1... | collective-permute-start | bytes 15728648 | tf_op jit(solution)/shard_map/ppermute | solution.py:27
  1978.8 318.0 %collective-permute-start.12 = (bf16[128,5120]{0,1:T(8,128)(2,1)}, bf16[128,5120]{0,1:T(8,128)(2,1)}, u32[]{:S(2)}, u32[]{:S(2)}) collective-permute-start(bf16[128,5120]{0,1:T(8,128)(2,1)} %slice.367), channel_id=1, source_target_pairs={{8,0},{9,1},{10,2},{11,3},{12,4},{13,5},{14,6},{15,7},{24,16},{25,... | collective-permute-start | bytes 3932168 | tf_op jit(solution)/shard_map/ppermute | solution.py:27
  1980.1 316.7 %slice-start.10 = ((s8[14155776]{0:T(1024)(128)(4,1)}), s8[4194304]{0:T(1024)(128)(4,1)S(1)}, s32[]{:S(2)}) async-start(s8[14155776]{0:T(1024)(128)(4,1)} %bitcast.406), calls=%async_computation.50 | async-start | bytes 8388608
  1980.1 316.7 %slice-start.11 = ((s8[14155776]{0:T(1024)(128)(4,1)}), s8[4194304]{0:T(1024)(128)(4,1)S(1)}, s32[]{:S(2)}) async-start(s8[14155776]{0:T(1024)(128)(4,1)} %bitcast.406), calls=%async_computation.51 | async-start | bytes 8388608
  1980.1 316.7 %slice-start.12 = ((s8[14155776]{0:T(1024)(128)(4,1)}), s8[4194304]{0:T(1024)(128)(4,1)S(1)}, s32[]{:S(2)}) async-start(s8[14155776]{0:T(1024)(128)(4,1)} %bitcast.406), calls=%async_computation.52 | async-start | bytes 8388608
  1998.5 298.3 %slice-start.13 = ((s8[14155776]{0:T(1024)(128)(4,1)}), s8[1572864]{0:T(1024)(128)(4,1)S(1)}, s32[]{:S(2)}) async-start(s8[14155776]{0:T(1024)(128)(4,1)} %bitcast.406), calls=%async_computation.53 | async-start | bytes 3145728
  2313.4 62.6 %collective-permute-start.14 = (bf16[256,5120]{0,1:T(8,128)(2,1)}, bf16[256,5120]{0,1:T(8,128)(2,1)}, u32[]{:S(2)}, u32[]{:S(2)}) collective-permute-start(bf16[256,5120]{0,1:T(8,128)(2,1)} %slice.536), channel_id=1, source_target_pairs={{2,0},{3,1},{4,2},{5,3},{6,4},{7,5},{8,6},{9,7},{10,8},{11,9},{12,... | collective-permute-start | bytes 7864328 | tf_op jit(solution)/shard_map/ppermute | solution.py:27
  2328.0 102.8 %collective-permute-start.10 = (bf16[256,5120]{0,1:T(8,128)(2,1)S(1)}, bf16[256,5120]{0,1:T(8,128)(2,1)S(1)}, u32[]{:S(2)}, u32[]{:S(2)}) collective-permute-start(bf16[256,5120]{0,1:T(8,128)(2,1)S(1)} %slice.537), channel_id=1, source_target_pairs={{2,0},{3,1},{4,2},{5,3},{6,4},{7,5},{8,6},{9,7},{10,8},{11,9},{12,... | collective-permute-start | bytes 7864328 | tf_op jit(solution)/shard_map/ppermute | solution.py:27
  2380.0 53.4 %collective-permute-start.15 = (bf16[128,5120]{0,1:T(8,128)(2,1)S(1)}, bf16[128,5120]{0,1:T(8,128)(2,1)S(1)}, u32[]{:S(2)}, u32[]{:S(2)}) collective-permute-start(bf16[128,5120]{0,1:T(8,128)(2,1)S(1)} %slice.538), channel_id=1, source_target_pairs={{1,0},{2,1},{3,2},{4,3},{5,4},{6,5},{7,6},{8,7},{9,8},{10,9},{11,1... | collective-permute-start | bytes 3932168 | tf_op jit(solution)/shard_map/ppermute | solution.py:27
  2431.8 4.9 collective-permute-start.11
  2448.1 311.5 %reduce-scatter.18.cloned.1.call-start = ((), (), s32[]{:S(2)}) async-start(), calls=%async_computation.31 | async-start | bytes 8650752 | tf_op jit(solution)/shard_map/reduce_scatter | solution.py:435
  2454.1 551.1 %reduce-scatter.22.cloned.1.call-start = ((), (), s32[]{:S(2)}) async-start(), calls=%async_computation.33 | async-start | bytes 23789568 | tf_op jit(solution)/shard_map/reduce_scatter | solution.py:439
  2479.7 777.1 %reduce-scatter.24.cloned.1.call-start = ((), (), s32[]{:S(2)}) async-start(), calls=%async_computation.34 | async-start | bytes 23789568 | tf_op jit(solution)/shard_map/reduce_scatter | solution.py:440
  2505.2 1003.5 %reduce-scatter.26.cloned.1.call-start = ((), (), s32[]{:S(2)}) async-start(), calls=%async_computation.35 | async-start | bytes 23789568 | tf_op jit(solution)/shard_map/reduce_scatter | solution.py:441
  2531.1 1166.3 %reduce-scatter.20.cloned.1.call-start = ((), (), s32[]{:S(2)}) async-start(), calls=%async_computation.32 | async-start | bytes 17301504 | tf_op jit(solution)/shard_map/reduce_scatter | solution.py:436
  2545.0 1405.7 %reduce-scatter.14.cloned.1.call-start = ((), (), s32[]{:S(2)}) async-start(), calls=%async_computation.29 | async-start | bytes 25952256 | tf_op jit(solution)/shard_map/reduce_scatter | solution.py:432
  (223 other events, 2763.4 us)
Sparse Core Ops, SparseCore 0:
  10.9 60.8 all-gather.11
  74.7 60.9 all-gather.13
  138.6 122.3 all-gather.15
  263.7 111.3 all-gather.17
  376.4 76.6 all-gather.29
  454.5 74.4 all-gather.27
  530.6 74.4 all-gather.25
  607.9 149.7 all-gather.19
  760.5 148.0 all-gather.21
  911.3 162.9 all-gather.23
  1690.2 151.7 reduce-scatter.33
  1844.9 67.3 reduce-scatter.27
  1915.1 71.3 reduce-scatter.29
  1988.8 71.3 reduce-scatter.31
  2448.2 163.3 reduce-scatter.15
  2614.3 145.2 reduce-scatter.17
  2762.4 242.7 reduce-scatter.21
  3007.9 248.9 reduce-scatter.23
  3259.7 248.9 reduce-scatter.25
  3511.4 185.8 reduce-scatter.19
  3704.3 246.3 reduce-scatter.13
where the time goes:
time: 3970 us; the launch traced here: 3960 us
  waiting for transfers between devices  2040 us (51%)
  starting transfers between devices  593 us (15%)
  matrix products  581 us (15%)
  blocking collectives  286 us (7%)
  local copies, waits for them, and re-layouts  241 us (6%)
  other arithmetic  201 us (5%)
    ppermute x16, waiting for transfers between devices, passed_along(): return lax.ppermute(x, axis, pairs)  502 us
    reduce_scatter x1, waiting for transfers between devices, body(): lax.psum_scatter(weight_totals[1], ('dp', 'expert'), scatter_dimension=0,...  253 us
    reduce_scatter x1, waiting for transfers between devices, body(): lax.psum_scatter(weight_totals[10], ('dp', 'expert'), scatter_dimension=0...  252 us
    reduce_scatter x1, waiting for transfers between devices, body(): lax.psum_scatter(weight_totals[9], ('dp', 'expert'), scatter_dimension=0,...  252 us
    ppermute x16, starting transfers between devices, passed_along(): return lax.ppermute(x, axis, pairs)  248 us
    reduce_scatter x1, waiting for transfers between devices, body(): lax.psum_scatter(weight_totals[8], ('dp', 'expert'), scatter_dimension=0,...  246 us
    dot_general x24, matrix products, transposed_left(): lax.dot_general(left, right, (((0,), (0,)), ((), ())), preferred_element_...  194 us
    reduce_scatter x1, waiting for transfers between devices, body(): lax.psum_scatter(weight_totals[5], ('dp', 'expert'), scatter_dimension=1,...  189 us
  transfers between devices with their start and end apart: 45, of which 24 were waited for; matrix products, arithmetic and copies ran while one was open for 23% of the time, Pallas kernels for 0%

commit v1 on v0

v1 whole, which is shorter than its diff:
```python
import math

import jax
import jax.numpy as jnp
from jax import lax
from jax.sharding import PartitionSpec as P

D = 2048
H = 16
NOPE = 128
ROPE = 64
VDIM = 128
LAT = 512
TOP = 6
WINDOW = 1024
MICRO = 2


EPSILON = 1e-06
NEGATIVE = -1e30
HIGHEST_PRECISION = lax.Precision.HIGHEST


def root_normalize(values, gain):
    inverse = lax.rsqrt(jnp.mean(values * values, axis=-1, keepdims=True) + EPSILON)
    return values * inverse * gain


def normalize_back(values, gain, incoming):
    result, pullback = jax.vjp(root_normalize, values, gain)
    return pullback(incoming)


def silu_product(left, right):
    return jax.nn.silu(left) * right


def silu_back(left, right, incoming):
    result, pullback = jax.vjp(silu_product, left, right)
    return pullback(incoming)


def angles(positions):
    half_width = ROPE // 2
    frequency = jnp.exp(
        jnp.arange(half_width, dtype=jnp.float32) * (-math.log(10000.0) / half_width)
    )
    turned = positions.astype(jnp.float32)[:, None] * frequency[None, :]
    return (jnp.cos(turned), jnp.sin(turned))


def rotate(values, cosine_table, sine_table):
    half_width = values.shape[-1] // 2
    first = values[..., :half_width]
    second = values[..., half_width:]
    return jnp.concatenate(
        [first * cosine_table - second * sine_table, first * sine_table + second * cosine_table],
        axis=-1,
    )


def segment_of(positions, lengths):
    boundary = jnp.cumsum(lengths)
    return jnp.sum((boundary[None, :] <= positions[:, None]).astype(jnp.int32), axis=1)


def transposed_left(left, right):
    return lax.dot_general(
        left, right, (((0,), (0,)), ((), ())), preferred_element_type=jnp.float32
    )


def transposed_right(left, right):
    return lax.dot_general(
        left, right, (((1,), (1,)), ((), ())), preferred_element_type=jnp.float32
    )


BOTH = ("dp", "expert")


def gather_all(x):
    return lax.all_gather(x, BOTH, axis=0, tiled=False)


def scatter_all(x):
    return lax.psum_scatter(x, BOTH, scatter_dimension=0, tiled=False)


def gather_plane(x):
    return lax.all_gather(x, "expert", axis=0, tiled=False)


def scatter_plane(x):
    return lax.psum_scatter(x, "expert", scatter_dimension=0, tiled=False)


def low(x):
    return x.astype(jnp.bfloat16)


def dot(a, b):
    return jnp.dot(a, b, preferred_element_type=jnp.float32)


def gather_dp(x, axis):
    size = lax.axis_size("dp")
    if size != 2:
        return lax.all_gather(x, "dp", axis=axis, tiled=True)
    other = lax.ppermute(x, "dp", [(0, 1), (1, 0)])
    first = lax.axis_index("dp") == 0
    return jnp.concatenate(
        [jnp.where(first, x, other), jnp.where(first, other, x)], axis=axis
    )


def scatter_dp(x, axis):
    size = lax.axis_size("dp")
    if size != 2:
        return lax.psum_scatter(low(x), "dp", scatter_dimension=axis, tiled=True).astype(
            jnp.float32
        )
    half = x.shape[axis] // 2
    index = lax.axis_index("dp")
    away = low(lax.dynamic_slice_in_dim(x, (1 - index) * half, half, axis))
    arrived = lax.ppermute(away, "dp", [(0, 1), (1, 0)])
    return lax.dynamic_slice_in_dim(x, index * half, half, axis) + arrived.astype(jnp.float32)


def attention_forward(queries, keys, values, allowed, score_scale):
    raw = jnp.einsum("mqhd,mkhd->mhqk", queries, keys, preferred_element_type=jnp.float32)
    scores = jnp.where(allowed[:, None], raw * score_scale, NEGATIVE)
    highest = jnp.max(scores, axis=-1, keepdims=True)
    log_total = highest + jnp.log(jnp.sum(jnp.exp(scores - highest), axis=-1, keepdims=True))
    weights = low(jnp.exp(scores - log_total))
    mixture = jnp.einsum("mhqk,mkhd->mqhd", weights, values, preferred_element_type=jnp.float32)
    return low(mixture), log_total


def attention_backward(queries, keys, values, allowed, score_scale, log_total, grad_mixture):
    raw = jnp.einsum("mqhd,mkhd->mhqk", queries, keys, preferred_element_type=jnp.float32)
    scores = jnp.where(allowed[:, None], raw * score_scale, NEGATIVE)
    probs = jnp.exp(scores - log_total)
    grad_probs = jnp.einsum(
        "mqhd,mkhd->mhqk", grad_mixture, values, preferred_element_type=jnp.float32
    )
    grad_scores = low(
        probs * (grad_probs - jnp.sum(grad_probs * probs, axis=-1, keepdims=True))
    )
    grad_queries = (
        jnp.einsum("mhqk,mkhd->mqhd", grad_scores, keys, preferred_element_type=jnp.float32)
        * score_scale
    )
    grad_keys = (
        jnp.einsum("mhqk,mqhd->mkhd", grad_scores, queries, preferred_element_type=jnp.float32)
        * score_scale
    )
    grad_values = jnp.einsum(
        "mhqk,mqhd->mkhd", low(probs), grad_mixture, preferred_element_type=jnp.float32
    )
    return grad_queries, grad_keys, grad_values


def body(
    layer_input,
    cotangent,
    doc_lengths,
    routes,
    attention_gain,
    query_weight,
    latent_weight,
    latent_gain,
    expand_weight,
    output_weight,
    feed_gain,
    router_weight,
    shared_gate,
    shared_up,
    shared_down,
    expert_gate,
    expert_up,
    expert_down,
):
    n_dp = lax.axis_size("dp")
    n_expert = lax.axis_size("expert")
    devices = n_dp * n_expert
    lane = lax.axis_index("expert")
    tokens = layer_input.shape[2]
    rows = MICRO * tokens
    experts_count = router_weight.shape[1]
    score_scale = (NOPE + ROPE) ** (-0.5)
    head_width = NOPE + ROPE
    key_width = H * head_width

    expert_gate = gather_dp(expert_gate[0], 0)
    expert_up = gather_dp(expert_up[0], 0)
    expert_down = gather_dp(expert_down[0], 1)
    shard = query_weight.shape[0]
    units = shared_down.shape[0]
    mine = n_dp * units
    both = jnp.stack([shared_gate, shared_up], axis=1).reshape(shard, 2, n_dp, n_expert, units)
    both = both.transpose(3, 0, 1, 2, 4).reshape(n_expert, shard, 2 * mine)
    both = lax.all_to_all(both, "expert", split_axis=0, concat_axis=0, tiled=True)
    shared_in = gather_dp(both.reshape(n_expert * shard, 2 * mine), 0)
    shared_out_weight = gather_dp(shared_down, 0)

    small_latent = latent_gain.shape[0]
    small = jnp.concatenate(
        [
            router_weight,
            attention_gain[:, None],
            feed_gain[:, None],
            jnp.pad(latent_gain, (0, shard - small_latent))[:, None],
        ],
        axis=1,
    )
    small = jnp.pad(small, ((0, 0), (0, 128 - small.shape[1])))
    all_query = gather_all(query_weight).reshape(D, key_width)
    all_latent = gather_all(latent_weight).reshape(D, LAT + ROPE)
    all_expand = gather_all(expand_weight).reshape(LAT, H * (NOPE + VDIM))
    all_output = gather_all(output_weight.T).reshape(D, H * VDIM)
    small = gather_all(small)
    gain_latent = small[:, :small_latent, experts_count + 2].reshape(LAT).astype(jnp.float32)
    small = small.reshape(D, 128)
    all_router = small[:, :experts_count]
    gain_first = small[:, experts_count].astype(jnp.float32)
    gain_second = small[:, experts_count + 1].astype(jnp.float32)

    positions = lane * tokens + jnp.arange(tokens, dtype=jnp.int32)
    cosine_table, sine_table = angles(positions)
    cosine_rows = jnp.tile(cosine_table, (MICRO, 1))
    sine_rows = jnp.tile(sine_table, (MICRO, 1))
    head_cosine = cosine_rows[:, None, :]
    head_sine = sine_rows[:, None, :]
    inputs = layer_input[0].reshape(rows, D).astype(jnp.float32)
    hidden = low(root_normalize(inputs, gain_first))
    latent = dot(hidden, all_latent)
    compressed = low(root_normalize(latent[:, :LAT], gain_latent))
    key_rope = low(rotate(latent[:, LAT:], cosine_rows, sine_rows))
    line = gather_plane(jnp.concatenate([compressed, key_rope], axis=1))
    query_heads = dot(hidden, all_query).reshape(rows, H, head_width)
    queries = low(
        jnp.concatenate(
            [query_heads[..., :NOPE], rotate(query_heads[..., NOPE:], head_cosine, head_sine)],
            axis=-1,
        )
    ).reshape(MICRO, tokens, H, head_width)
    reach = (WINDOW + tokens - 2) // tokens
    span = reach + 1
    key_rows = span * tokens
    line = jnp.concatenate(
        [jnp.zeros((reach,) + line.shape[1:], line.dtype), line], axis=0
    )
    window = lax.dynamic_slice_in_dim(line, lane, span, 0)
    window = window.reshape(span, MICRO, tokens, LAT + ROPE).transpose(1, 0, 2, 3)
    window = window.reshape(MICRO, key_rows, LAT + ROPE)
    window_latent = window[..., :LAT].reshape(MICRO * key_rows, LAT)
    expanded = low(dot(window_latent, all_expand)).reshape(MICRO, key_rows, H, NOPE + VDIM)
    keys = jnp.concatenate(
        [
            expanded[..., :NOPE],
            jnp.broadcast_to(window[:, :, None, LAT:], (MICRO, key_rows, H, ROPE)),
        ],
        axis=-1,
    )
    values = expanded[..., NOPE:]
    key_positions = (lane - reach) * tokens + jnp.arange(key_rows, dtype=jnp.int32)
    apart = positions[:, None] - key_positions[None, :]
    reachable = (key_positions[None, :] >= 0) & (apart >= 0) & (apart < WINDOW)
    allowed = jnp.stack(
        [
            reachable
            & (
                segment_of(positions, doc_lengths[0, m])[:, None]
                == segment_of(key_positions, doc_lengths[0, m])[None, :]
            )
            for m in range(MICRO)
        ]
    )
    mixture, log_total = attention_forward(queries, keys, values, allowed, score_scale)
    mixture = mixture.reshape(rows, H * VDIM)
    residual = inputs + transposed_right(mixture, all_output)
    normed = low(root_normalize(residual, gain_second))

    all_normed = gather_plane(normed).reshape(n_expert * rows, D)
    all_cotangent = gather_plane(cotangent[0].reshape(rows, D)).reshape(n_expert * rows, D)
    all_routes = gather_plane(routes[0].reshape(rows, TOP))
    total_rows = n_expert * rows
    capacity = (9 * tokens * TOP + 8 * experts_count - 1) // (8 * experts_count)
    per_group = max(1, 256 // tokens)
    group_rows = per_group * tokens
    groups = total_rows // group_rows
    slots = -(-per_group * capacity // 16) * 16
    named = jnp.any(all_routes == lane, axis=-1).reshape(-1, tokens).astype(jnp.int32)
    rank = jnp.cumsum(named, axis=1) - named
    kept = (named > 0) & (rank < capacity)
    offset = (jnp.arange(named.shape[0], dtype=jnp.int32) % per_group) * capacity
    place = jnp.where(kept, rank + offset[:, None], -1).reshape(groups, 1, group_rows)
    picked_bool = place == jnp.arange(slots, dtype=jnp.int32)[None, :, None]
    picked = picked_bool.astype(jnp.bfloat16)
    picked_float = picked_bool.astype(jnp.float32)
    probabilities = jax.nn.softmax(dot(all_normed, all_router), axis=-1)
    own_column = jnp.arange(experts_count, dtype=jnp.int32) == lane
    gate_rows = jnp.sum(jnp.where(own_column[None, :], probabilities, 0.0), axis=1)
    gate_slots = jnp.sum(
        picked_float * gate_rows.reshape(groups, 1, group_rows), axis=2
    ).reshape(groups * slots, 1)

    def to_slots(x):
        return low(
            jnp.einsum(
                "gst,gtd->gsd",
                picked,
                x.reshape(groups, group_rows, D),
                preferred_element_type=jnp.float32,
            )
        ).reshape(groups * slots, D)

    def from_slots(x):
        return jnp.einsum(
            "gst,gsd->gtd",
            picked,
            x.reshape(groups, slots, D),
            preferred_element_type=jnp.float32,
        ).reshape(total_rows, D)

    arrived = to_slots(all_normed)
    gate_pre = dot(arrived, expert_gate)
    up_pre = dot(arrived, expert_up)
    expert_act = low(silu_product(gate_pre, up_pre))
    expert_out = low(dot(expert_act, expert_down))
    shared_pre = dot(all_normed, shared_in)
    shared_act = low(silu_product(shared_pre[:, :mine], shared_pre[:, mine:]))
    partial_out = from_slots(low(gate_slots * expert_out.astype(jnp.float32))) + dot(
        shared_act, shared_out_weight
    )
    expert_sum = scatter_plane(low(partial_out).reshape(n_expert, rows, D))
    layer_output = low(residual + expert_sum.astype(jnp.float32))

    arrived_grad = to_slots(all_cotangent)
    gate_dots = jnp.sum(
        expert_out.astype(jnp.float32) * arrived_grad.astype(jnp.float32), axis=1
    ).reshape(groups, slots, 1)
    gate_grad_rows = jnp.sum(picked_float * gate_dots, axis=1).reshape(n_expert, rows)
    gate_grads = lax.all_to_all(
        gate_grad_rows, "expert", split_axis=0, concat_axis=0, tiled=True
    ).T
    slot_grad = low(gate_slots * arrived_grad.astype(jnp.float32))
    expert_down_grad = transposed_left(expert_act, slot_grad)
    gate_back, up_back = silu_back(gate_pre, up_pre, transposed_right(slot_grad, expert_down))
    gate_back = low(gate_back)
    up_back = low(up_back)
    expert_gate_grad = transposed_left(arrived, gate_back)
    expert_up_grad = transposed_left(arrived, up_back)
    rows_grad = low(
        transposed_right(gate_back, expert_gate) + transposed_right(up_back, expert_up)
    )
    shared_back = jnp.concatenate(
        silu_back(
            shared_pre[:, :mine],
            shared_pre[:, mine:],
            transposed_right(all_cotangent, shared_out_weight),
        ),
        axis=1,
    ).astype(jnp.bfloat16)
    partial_normed = from_slots(rows_grad) + transposed_right(shared_back, shared_in)
    grad_normed = scatter_plane(low(partial_normed).reshape(n_expert, rows, D)).astype(
        jnp.float32
    )
    shared_down_grad = scatter_dp(transposed_left(shared_act, all_cotangent), 0)
    shared_in_grad = scatter_dp(transposed_left(all_normed, shared_back), 0)
    shared_in_grad = lax.all_to_all(
        low(shared_in_grad).reshape(n_expert, shard, 2 * mine),
        "expert",
        split_axis=0,
        concat_axis=0,
        tiled=True,
    ).astype(jnp.float32)
    shared_in_grad = (
        shared_in_grad.reshape(n_expert, shard, 2, n_dp, units)
        .transpose(2, 1, 3, 0, 4)
        .reshape(2, shard, n_dp * n_expert * units)
    )
    expert_grads = (
        scatter_dp(expert_gate_grad, 0)[None],
        scatter_dp(expert_up_grad, 0)[None],
        scatter_dp(expert_down_grad, 1)[None],
    )

    own_probs = lax.dynamic_slice_in_dim(probabilities, lane * rows, rows, 0)
    logit_grad = low(
        own_probs * (gate_grads - jnp.sum(gate_grads * own_probs, axis=-1, keepdims=True))
    )
    router_weight_grad = transposed_left(normed, logit_grad)
    grad_normed = grad_normed + transposed_right(logit_grad, all_router)
    residual_extra, feed_gain_grad = normalize_back(residual, gain_second, grad_normed)
    grad_residual = cotangent[0].reshape(rows, D).astype(jnp.float32) + residual_extra

    grad_attn = low(grad_residual)
    output_grad = transposed_left(grad_attn, mixture)
    grad_mixture = low(dot(grad_attn, all_output)).reshape(MICRO, tokens, H, VDIM)
    grad_queries, grad_keys, grad_values = attention_backward(
        queries, keys, values, allowed, score_scale, log_total, grad_mixture
    )
    grad_queries = grad_queries.reshape(rows, H, head_width)
    grad_expanded = low(
        jnp.concatenate([grad_keys[..., :NOPE], grad_values], axis=-1)
    ).reshape(MICRO * key_rows, H * (NOPE + VDIM))
    expand_grad = transposed_left(window_latent, grad_expanded)
    grad_window = jnp.concatenate(
        [
            transposed_right(grad_expanded, all_expand).reshape(MICRO, key_rows, LAT),
            jnp.sum(grad_keys[..., NOPE:], axis=2),
        ],
        axis=-1,
    )
    grad_window = low(grad_window).reshape(MICRO, span, tokens, LAT + ROPE)
    grad_window = grad_window.transpose(1, 0, 2, 3).reshape(span, rows, LAT + ROPE)
    grad_line = lax.dynamic_update_slice_in_dim(
        jnp.zeros((n_expert + reach, rows, LAT + ROPE), jnp.bfloat16), grad_window, lane, 0
    )[reach:]
    grad_line = scatter_plane(grad_line).astype(jnp.float32)
    latent_part, latent_gain_grad = normalize_back(
        latent[:, :LAT], gain_latent, grad_line[:, :LAT]
    )
    grad_key_rope = rotate(grad_line[:, LAT:], cosine_rows, -sine_rows)
    grad_latent = low(jnp.concatenate([latent_part, grad_key_rope], axis=1))
    latent_grad = transposed_left(hidden, grad_latent)
    grad_query = low(
        jnp.concatenate(
            [
                grad_queries[..., :NOPE],
                rotate(grad_queries[..., NOPE:], head_cosine, -head_sine),
            ],
            axis=-1,
        ).reshape(rows, key_width)
    )
    query_grad = transposed_left(hidden, grad_query)
    grad_hidden = transposed_right(grad_latent, all_latent) + transposed_right(
        grad_query, all_query
    )
    input_extra, attention_gain_grad = normalize_back(inputs, gain_first, grad_hidden)
    input_grad = grad_residual + input_extra

    small_grad = jnp.concatenate(
        [
            router_weight_grad,
            attention_gain_grad[:, None],
            feed_gain_grad[:, None],
        ],
        axis=1,
    ).reshape(devices, shard, experts_count + 2)
    latent_column = jnp.pad(
        latent_gain_grad.reshape(devices, small_latent), ((0, 0), (0, shard - small_latent))
    )[:, :, None]
    small_grad = jnp.concatenate([small_grad, latent_column], axis=2)
    small_grad = jnp.pad(small_grad, ((0, 0), (0, 0), (0, 128 - small_grad.shape[2])))
    small_grad = scatter_all(small_grad)
    query_grad = scatter_all(low(query_grad).reshape(devices, shard, key_width))
    latent_grad = scatter_all(low(latent_grad).reshape(devices, shard, LAT + ROPE))
    expand_grad = scatter_all(
        low(expand_grad).reshape(devices, expand_weight.shape[0], expand_weight.shape[1])
    )
    output_grad = scatter_all(low(output_grad).reshape(devices, shard, H * VDIM))
    return (
        layer_output.reshape(1, MICRO, tokens, D),
        input_grad.reshape(1, MICRO, tokens, D),
        small_grad[:, experts_count],
        query_grad.astype(jnp.float32),
        latent_grad.astype(jnp.float32),
        small_grad[:small_latent, experts_count + 2],
        expand_grad.astype(jnp.float32),
        output_grad.astype(jnp.float32).T,
        small_grad[:, experts_count + 1],
        small_grad[:, :experts_count],
        shared_in_grad[0],
        shared_in_grad[1],
        shared_down_grad,
        expert_grads[0],
        expert_grads[1],
        expert_grads[2],
    )


def solution(mesh):
    placed = (
        P("dp", None, "expert", None),
        P("dp", None, "expert", None),
        P("dp", None, None),
        P("dp", None, "expert", None),
        P(("dp", "expert")),
        P(("dp", "expert"), None),
        P(("dp", "expert"), None),
        P(("dp", "expert")),
        P(("dp", "expert"), None),
        P(None, ("dp", "expert")),
        P(("dp", "expert")),
        P(("dp", "expert"), None),
        P(("dp", "expert"), None),
        P(("dp", "expert"), None),
        P(("dp", "expert"), None),
        P("expert", "dp", None),
        P("expert", "dp", None),
        P("expert", None, "dp"),
    )
    return jax.shard_map(
        body,
        mesh=mesh,
        in_specs=placed,
        out_specs=(
            P("dp", None, "expert", None),
            P("dp", None, "expert", None),
            P(("dp", "expert")),
            P(("dp", "expert"), None),
            P(("dp", "expert"), None),
            P(("dp", "expert")),
            P(("dp", "expert"), None),
            P(None, ("dp", "expert")),
            P(("dp", "expert")),
            P(("dp", "expert"), None),
            P(("dp", "expert"), None),
            P(("dp", "expert"), None),
            P(("dp", "expert"), None),
            P("expert", "dp", None),
            P("expert", "dp", None),
            P("expert", None, "dp"),
        ),
        check_vma=False,
    )
```

time: 3970 us -> 2200 us (0.55)
  waiting for transfers between devices: 2040 us -> 1220 us
  starting transfers between devices: 593 us -> 23.3 us
  blocking collectives: 286 us -> 84.3 us
  matrix products: 581 us -> 486 us
  other arithmetic: 201 us -> 116 us
    reduce_scatter x10 -> x8, waiting for transfers between devices: 1200 us -> 747 us  [the longest x5 413 us: scatter_all(): return lax.psum_scatter(x, BOTH, scatter_dimension=0, tiled=False)]
    all_to_all x8 -> x3, starting transfers between devices: 343 us -> 11.4 us  [the longest x1 4.29 us: body(): lax.all_to_all(low(shared_in_grad).reshape(n_expert, shard, 2 * mine), 'e...]
    all_to_all x8 -> x3, waiting for transfers between devices: 260 us -> 6.69 us  [the longest x1 6.68 us: body(): lax.all_to_all(gate_grad_rows, 'expert', split_axis=0, concat_axis=0, til...]
    ppermute x16 -> x10, starting transfers between devices: 248 us -> 10.9 us  [the longest x5 6.07 us: gather_dp(): other = lax.ppermute(x, 'dp', [(0, 1), (1, 0)])]
    ppermute x16 -> x10, waiting for transfers between devices: 502 us -> 283 us  [the longest x5 154 us: gather_dp(): other = lax.ppermute(x, 'dp', [(0, 1), (1, 0)])]
    all_gather x10 -> x7, waiting for transfers between devices: 72.6 us -> 180 us  [the longest x4 104 us: gather_all(): return lax.all_gather(x, BOTH, axis=0, tiled=False)]
    unnamed x2 -> x0, blocking collectives: 107 us -> none
    dot_general x24 -> x10, matrix products: 194 us -> 96.6 us  [transposed_left(): lax.dot_general(left, right, (((0,), (0,)), ((), ())), preferred_element_...]
  transfers between devices with their start and end apart: 45 -> 28, of which waited for: 24 -> 16; matrix products, arithmetic and copies ran while one was open for 23% -> 21% of each run, Pallas kernels for 0% -> 0%
where the time goes in v1:
time: 2200 us; the launch traced here: 2190 us
  waiting for transfers between devices  1220 us (55%)
  matrix products  486 us (22%)
  local copies, waits for them, and re-layouts  241 us (11%)
  other arithmetic  116 us (5%)
  blocking collectives  84.3 us (4%)
  starting transfers between devices  23.3 us (1%)
    reduce_scatter x5, waiting for transfers between devices, scatter_all(): return lax.psum_scatter(x, BOTH, scatter_dimension=0, tiled=False)  413 us
    reduce_scatter x3, waiting for transfers between devices, scatter_plane(): return lax.psum_scatter(x, 'expert', scatter_dimension=0, tiled=False)  334 us
    ppermute x5, waiting for transfers between devices, gather_dp(): other = lax.ppermute(x, 'dp', [(0, 1), (1, 0)])  154 us
    ppermute x5, waiting for transfers between devices, scatter_dp(): arrived = lax.ppermute(away, 'dp', [(0, 1), (1, 0)])  129 us
    dot_general x10, matrix products, transposed_right(): lax.dot_general(left, right, (((1,), (1,)), ((), ())), preferred_element_...  128 us
    dot_general x10, matrix products, dot(): return jnp.dot(a, b, preferred_element_type=jnp.float32)  126 us
    all_gather x4, waiting for transfers between devices, gather_all(): return lax.all_gather(x, BOTH, axis=0, tiled=False)  104 us
    dot_general x10, matrix products, transposed_left(): lax.dot_general(left, right, (((0,), (0,)), ((), ())), preferred_element_...  96.6 us
  transfers between devices with their start and end apart: 28, of which 16 were waited for; matrix products, arithmetic and copies ran while one was open for 21% of the time, Pallas kernels for 0%

profile of v1, /device:TPU:0, one launch (start us, length us, event | category | flops | bytes accessed | tf_op | source)
XLA Modules:
  0.0 2186.8 jit_solution(15867244590242842078)
XLA Ops:
  9.5 45.0 %all-gather = bf16[2048,128]{1,0:T(8,128)(2,1)S(1)} all-gather(bf16[64,128]{1,0:T(8,128)(2,1)S(1)} %pad.18), channel_id=2, replica_groups=mesh['dp'=2,'expert'=16] {'dp','expert'}, dimensions={0}, use_global_device_ids=true | all-gather | bytes 540672 | tf_op jit(solution)/shard_map/all_gather | solution.py:83
  58.7 13.0 all-gather.17.cloned.1.call-done
  79.9 51.5 %all-gather.19.cloned.1.call-done = bf16[4096,576]{0,1:T(8,128)(2,1)} async-done(((bf16[256,576]{0,1:T(8,128)(2,1)}), bf16[4096,576]{0,1:T(8,128)(2,1)}) %all-gather.19.cloned.1.call-update) | async-done | bytes 4718608 | tf_op jit(solution)/shard_map/all_gather | solution.py:91
  142.5 7.1 copy.140
  154.3 40.3 %all-gather.21.cloned.1.call-done = bf16[512,4096]{1,0:T(8,128)(2,1)} async-done(((bf16[16,4096]{1,0:T(8,128)(2,1)}), bf16[512,4096]{1,0:T(8,128)(2,1)}) %all-gather.21.cloned.1.call-update) | async-done | bytes 4194320 | tf_op jit(solution)/shard_map/all_gather | solution.py:83
  194.5 16.0 convolution_convert_fusion
  210.6 11.5 copy.181
  222.1 7.8 fusion.100
  229.8 12.9 copy.173
  242.7 13.2 copy.172
  255.9 35.9 %all-gather.23.cloned.1.call-done = bf16[2048,3072]{1,0:T(8,128)(2,1)} async-done(((bf16[64,3072]{1,0:T(8,128)(2,1)}), bf16[2048,3072]{1,0:T(8,128)(2,1)}) %all-gather.23.cloned.1.call-update) | async-done | bytes 12582928 | tf_op jit(solution)/shard_map/all_gather | solution.py:83
  291.9 16.8 copy.142
  308.7 6.8 fusion.108
  318.9 10.7 fusion.102
  329.6 9.4 exponential_reduce_fusion
  339.6 13.3 fusion.45
  355.2 15.2 all-gather.25.cloned.1.call-done
  394.3 39.4 %all_gather.60 = s32[16,256,6]{1,2,0:T(8,128)S(1)} all-gather(s32[1,256,6]{1,2,0:T(8,128)S(1)} %copy.149), channel_id=1, replica_groups=mesh['dp'=2,'expert'=16] {'expert'}, dimensions={0}, use_global_device_ids=true | all-gather | bytes 104448 | tf_op jit(solution)/shard_map/all_gather | solution.py:91
  435.8 78.3 %collective-permute-done.4 = bf16[88,2048]{1,0:T(8,128)(2,1)S(1)} collective-permute-done((bf16[88,2048]{1,0:T(8,128)(2,1)S(1)}, bf16[88,2048]{1,0:T(8,128)(2,1)S(1)}, u32[]{:S(2)}, u32[]{:S(2)}) %collective-permute-start.4) | collective-permute-done | bytes 360480 | tf_op jit(solution)/shard_map/ppermute | solution.py:110
  515.0 75.7 %collective-permute-done.3 = bf16[1024,352]{0,1:T(8,128)(2,1)S(1)} collective-permute-done((bf16[1024,352]{0,1:T(8,128)(2,1)S(1)}, bf16[1024,352]{0,1:T(8,128)(2,1)S(1)}, u32[]{:S(2)}, u32[]{:S(2)}) %collective-permute-start.3) | collective-permute-done | bytes 720928 | tf_op jit(solution)/shard_map/ppermute | solution.py:110
  606.6 11.1 convolution_convert_fusion.6
  617.7 24.5 %all-gather.27.cloned.1.call-done = bf16[4096,2048]{1,0:T(8,128)(2,1)} async-done(((bf16[256,2048]{1,0:T(8,128)(2,1)}), bf16[4096,2048]{1,0:T(8,128)(2,1)}) %all-gather.27.cloned.1.call-update) | async-done | bytes 16777232 | tf_op jit(solution)/shard_map/all_gather | solution.py:91
  642.2 10.2 fusion.103
  653.3 11.2 convolution_convert_fusion.7
  664.5 15.9 fusion.17
  680.4 20.4 multiply_convert_fusion.2
  700.8 17.2 fusion.4
  719.5 10.3 fusion.3
  729.8 24.4 %fusion.9 = (bf16[1792,1408]{1,0:T(8,128)(2,1)}, bf16[1792,1408]{1,0:T(8,128)(2,1)}) fusion(f32[1792,1408]{1,0:T(8,128)} %fusion.17, f32[1792,1408]{1,0:T(8,128)} %get-tuple-element.78, bf16[1792,2048]{1,0:T(8,128)(2,1)S(1)} %get-tuple-element.67, bf16[1408,1024]{1,0:T(8,128)(2,1)} %get-tuple-element.40, bf16[1408,1024]{1,0:T(8,128)(2,1)S(1)} %copy-done.25), kind=kOutput, calls=%fused_computation.28 | convolution fusion | flops 10381623296 | bytes 43384832 | tf_op jit(solution)/shard_map/dot_general | solution.py:74
  754.2 17.6 fusion.15
  771.8 19.1 add_convert_fusion
  790.9 16.5 fusion.40
  807.4 9.8 fusion.52
  817.3 11.7 fusion.20
  829.0 20.0 fusion
  849.1 23.2 %fusion.41 = f32[16,256,2048]{2,1,0:T(8,128)} fusion(bf16[16,112,2048]{2,1,0:T(8,128)(2,1)} %bitcast.306, s32[16,256]{1,0:T(8,128)S(1)} %fusion.71), kind=kOutput, calls=%fused_computation.117 | convolution fusion | flops 1879506944 | bytes 40910848 | tf_op jit(solution)/shard_map/gst,gsd->gtd/dot_general | solution.py:320
  872.3 20.0 fusion.1
  904.6 121.7 %reduce-scatter.11.cloned.1.call-done = bf16[1,256,2048]{2,1,0:T(8,128)(2,1)} async-done(((bf16[16,256,2048]{2,1,0:T(8,128)(2,1)}), bf16[1,256,2048]{2,1,0:T(8,128)(2,1)}) %reduce-scatter.11.cloned.1.call-update) | async-done | bytes 1048592 | tf_op jit(solution)/shard_map/reduce_scatter | solution.py:95
  1030.2 177.7 %reduce-scatter.9.cloned.1.call-done = bf16[1,256,2048]{2,1,0:T(8,128)(2,1)} async-done(((bf16[16,256,2048]{2,1,0:T(8,128)(2,1)}), bf16[1,256,2048]{2,1,0:T(8,128)(2,1)}) %reduce-scatter.9.cloned.1.call-update) | async-done | bytes 1048592 | tf_op jit(solution)/shard_map/reduce_scatter | solution.py:95
  1219.8 10.3 fusion.11
  1230.1 17.1 multiply_reduce_fusion
  1247.2 13.2 multiply_convert_fusion
  1260.4 11.7 multiply_bitcast_fusion
  1276.8 7.2 slice.246
  1284.7 9.1 pad_maximum_fusion
  1293.8 24.7 %copy.158 = bf16[2,1152,16,256]{3,2,1,0:T(8,128)(2,1)} copy(bf16[2,1152,16,256]{1,3,2,0:T(8,128)(2,1)} %pad_maximum_fusion) | data formatting | bytes 37748736 | tf_op jit(solution)/shard_map/concatenate | solution.py:407
  1318.7 28.8 %convert_element_type.360 = bf16[2,9,128,4096]{3,2,1,0:T(8,128)(2,1)} reshape(bf16[2,1152,16,256]{3,2,1,0:T(8,128)(2,1)} %copy.158) | data formatting | bytes 37748736 | tf_op jit(solution)/shard_map/convert_element_type | solution.py:99
  1347.5 15.6 fusion.36
  1377.9 13.5 copy.185
  1391.5 12.2 convolution_convert_fusion.5
  1405.2 10.7 multiply_bitcast_fusion.1
  1418.0 34.5 %reduce-scatter.13.cloned.1.call-done = bf16[1,256,576]{1,2,0:T(8,128)(2,1)} async-done(((bf16[16,256,576]{1,2,0:T(8,128)(2,1)}), bf16[1,256,576]{1,2,0:T(8,128)(2,1)}) %reduce-scatter.13.cloned.1.call-update) | async-done | bytes 294928 | tf_op jit(solution)/shard_map/reduce_scatter | solution.py:95
  1455.6 6.7 fusion.109
  1473.9 6.9 convolution_convert_fusion.3
  1481.3 9.8 convolution_convert_fusion.1
  1491.2 10.6 fusion.39
  1505.0 14.8 fusion.113
  1527.0 18.1 fusion.111
  1550.5 16.5 fusion.112
  1586.9 129.5 %collective-permute-done.6 = bf16[88,2048]{1,0:T(8,128)(2,1)} collective-permute-done((bf16[88,2048]{1,0:T(8,128)(2,1)S(1)}, bf16[88,2048]{1,0:T(8,128)(2,1)}, u32[]{:S(2)}, u32[]{:S(2)}) %collective-permute-start.6) | collective-permute-done | bytes 360480 | tf_op jit(solution)/shard_map/ppermute | solution.py:126
  1735.5 7.7 add_bitcast_fusion
  1762.1 111.0 %reduce-scatter.19.cloned.1.call-done = bf16[1,64,576]{2,1,0:T(8,128)(2,1)} async-done(((bf16[32,64,576]{2,1,0:T(8,128)(2,1)}), bf16[1,64,576]{2,1,0:T(8,128)(2,1)}) %reduce-scatter.19.cloned.1.call-update) | async-done | bytes 73744 | tf_op jit(solution)/shard_map/reduce_scatter | solution.py:87
  1874.7 145.9 %reduce-scatter.23.cloned.1.call-done = bf16[1,64,2048]{2,1,0:T(8,128)(2,1)} async-done(((bf16[32,64,2048]{2,1,0:T(8,128)(2,1)}), bf16[1,64,2048]{2,1,0:T(8,128)(2,1)}) %reduce-scatter.23.cloned.1.call-update) | async-done | bytes 262160 | tf_op jit(solution)/shard_map/reduce_scatter | solution.py:87
  2022.4 155.8 %reduce-scatter.17.cloned.1.call-done = bf16[1,64,3072]{2,1,0:T(8,128)(2,1)} async-done(((bf16[32,64,3072]{2,1,0:T(8,128)(2,1)}), bf16[1,64,3072]{2,1,0:T(8,128)(2,1)}) %reduce-scatter.17.cloned.1.call-update) | async-done | bytes 393232 | tf_op jit(solution)/shard_map/reduce_scatter | solution.py:87
  (379 shorter events, 227.2 us)
Async XLA Ops:
  7.2 64.6 %all-gather.17.cloned.1.call-start = ((), (), s32[]{:S(2)}) async-start(), calls=%async_computation.20 | async-start | bytes 2703360 | tf_op jit(solution)/shard_map/all_gather | solution.py:83
  7.9 123.5 %all-gather.19.cloned.1.call-start = ((), (), s32[]{:S(2)}) async-start(), calls=%async_computation.21 | async-start | bytes 5013504 | tf_op jit(solution)/shard_map/all_gather | solution.py:91
  54.4 587.8 %copy-start.7 = (bf16[2048,128]{1,0:T(8,128)(2,1)}, bf16[2048,128]{1,0:T(8,128)(2,1)S(1)}, u32[]{:S(2)}) copy-start(bf16[2048,128]{1,0:T(8,128)(2,1)S(1)} %all-gather) | copy-start | bytes 1572868
  54.7 20.8 copy-start.55
  55.5 321.5 %copy-start.52 = (f32[2048]{0:T(1024)}, f32[2048]{0:T(1024)S(1)}, u32[]{:S(2)}) copy-start(f32[2048]{0:T(1024)S(1)} %get-tuple-element.22) | copy-start | bytes 24580
  57.0 17.7 copy-start.60
  57.2 21.7 copy-start.71
  58.7 249.9 %copy-start.11 = (bf16[1,2,128,2048]{3,2,1,0:T(8,128)(2,1)}, bf16[1,2,128,2048]{3,2,1,0:T(8,128)(2,1)S(1)}, u32[]{:S(2)}) copy-start(bf16[1,2,128,2048]{3,2,1,0:T(8,128)(2,1)S(1)} %fusion.34) | copy-start | bytes 3145732
  74.7 59.5 %copy-start.62 = (f32[256]{0:T(256)}, f32[256]{0:T(256)S(1)}, u32[]{:S(2)}) copy-start(f32[256]{0:T(256)S(1)} %fusion.79) | copy-start | bytes 3076
  74.7 59.5 %copy-start.37 = (f32[2,128,32]{1,0,2:T(2,128)}, f32[2,128,32]{1,0,2:T(2,128)S(1)}, u32[]{:S(2)}) copy-start(f32[2,128,32]{1,0,2:T(2,128)S(1)} %tile.20) | copy-start | bytes 98308
  75.4 58.9 %copy-start.39 = (f32[2,128,32]{1,0,2:T(2,128)}, f32[2,128,32]{1,0,2:T(2,128)S(1)}, u32[]{:S(2)}) copy-start(f32[2,128,32]{1,0,2:T(2,128)S(1)} %tile.8) | copy-start | bytes 98308
  76.3 118.2 %all-gather.21.cloned.1.call-start = ((), (), s32[]{:S(2)}) async-start(), calls=%async_computation.22 | async-start | bytes 4325376 | tf_op jit(solution)/shard_map/all_gather | solution.py:83
  77.1 214.8 %all-gather.23.cloned.1.call-start = ((), (), s32[]{:S(2)}) async-start(), calls=%async_computation.23 | async-start | bytes 12976128 | tf_op jit(solution)/shard_map/all_gather | solution.py:83
  77.6 292.8 %all-gather.25.cloned.1.call-start = ((), (), s32[]{:S(2)}) async-start(), calls=%async_computation.24 | async-start | bytes 8650752 | tf_op jit(solution)/shard_map/all_gather | solution.py:83
  78.2 528.3 %all-gather.15.cloned.1.call-start = ((), (), s32[]{:S(2)}) async-start(), calls=%async_computation.12 | async-start | bytes 17825792 | tf_op jit(solution)/shard_map/all_gather | solution.py:91
  78.8 563.4 %all-gather.27.cloned.1.call-start = ((), (), s32[]{:S(2)}) async-start(), calls=%async_computation.25 | async-start | bytes 17825792 | tf_op jit(solution)/shard_map/all_gather | solution.py:91
  78.9 236.6 %copy-start.46 = (f32[4,8,2,128]{3,1,2,0:T(8,128)}, f32[4,8,2,128]{3,1,2,0:T(8,128)S(1)}, u32[]{:S(2)}) copy-start(f32[4,8,2,128]{3,1,2,0:T(8,128)S(1)} %copy.229) | copy-start | bytes 98308
  339.6 30.9 %copy-start.5 = (bf16[1,2,128,2048]{3,2,1,0:T(8,128)(2,1)S(1)}, bf16[1,2,128,2048]{3,2,1,0:T(8,128)(2,1)}, u32[]{:S(2)}) copy-start(bf16[1,2,128,2048]{3,2,1,0:T(8,128)(2,1)} %param.18) | copy-start | bytes 3145732
  355.2 21.2 copy-start.21
  379.0 212.9 %collective-permute-start.2 = (bf16[1408,1024]{1,0:T(8,128)(2,1)}, bf16[1408,1024]{1,0:T(8,128)(2,1)}, u32[]{:S(2)}, u32[]{:S(2)}) collective-permute-start(bf16[1408,1024]{1,0:T(8,128)(2,1)} %bitcast.351), channel_id=1, source_target_pairs={{0,16},{16,0},{1,17},{17,1},{2,18},{18,2},{3,19},{19,3},{4,20},{20... | collective-permute-start | bytes 8650760 | tf_op jit(solution)/shard_map/ppermute | solution.py:110
  387.4 46.4 %all-to-all-start = ((bf16[16,64,352]{2,1,0:T(8,128)(2,1)}), bf16[16,64,352]{2,1,0:T(8,128)(2,1)S(1)}, u32[]{:S(2)}, u32[]{:S(2)}) async-start(bf16[16,64,352]{2,1,0:T(8,128)(2,1)} %reshape.802), calls=%async_computation | async-start | bytes 1572864 | tf_op jit(solution)/shard_map/all_to_all | solution.py:203
  391.0 635.3 %reduce-scatter.11.cloned.1.call-start = ((), (), s32[]{:S(2)}) async-start(), calls=%async_computation.13 | async-start | bytes 17825792 | tf_op jit(solution)/shard_map/reduce_scatter | solution.py:95
  391.1 205.7 %collective-permute-start.1 = (bf16[1024,1408]{1,0:T(8,128)(2,1)}, bf16[1024,1408]{1,0:T(8,128)(2,1)}, u32[]{:S(2)}, u32[]{:S(2)}) collective-permute-start(bf16[1024,1408]{1,0:T(8,128)(2,1)} %bitcast.352), channel_id=1, source_target_pairs={{0,16},{16,0},{1,17},{17,1},{2,18},{18,2},{3,19},{19,3},{4,20},{20... | collective-permute-start | bytes 8650760 | tf_op jit(solution)/shard_map/ppermute | solution.py:110
  392.3 121.8 %collective-permute-start.4 = (bf16[88,2048]{1,0:T(8,128)(2,1)S(1)}, bf16[88,2048]{1,0:T(8,128)(2,1)S(1)}, u32[]{:S(2)}, u32[]{:S(2)}) collective-permute-start(bf16[88,2048]{1,0:T(8,128)(2,1)S(1)} %copy-done.45), channel_id=1, source_target_pairs={{0,16},{16,0},{1,17},{17,1},{2,18},{18,2},{3,19},{19,3},{4,20},{20... | collective-permute-start | bytes 1081352 | tf_op jit(solution)/shard_map/ppermute | solution.py:110
  393.2 208.6 %collective-permute-start = (bf16[1024,1408]{1,0:T(8,128)(2,1)}, bf16[1024,1408]{1,0:T(8,128)(2,1)}, u32[]{:S(2)}, u32[]{:S(2)}) collective-permute-start(bf16[1024,1408]{1,0:T(8,128)(2,1)} %bitcast.353), channel_id=1, source_target_pairs={{0,16},{16,0},{1,17},{17,1},{2,18},{18,2},{3,19},{19,3},{4,20},{20... | collective-permute-start | bytes 8650760 | tf_op jit(solution)/shard_map/ppermute | solution.py:110
  434.1 156.6 %collective-permute-start.3 = (bf16[1024,352]{0,1:T(8,128)(2,1)S(1)}, bf16[1024,352]{0,1:T(8,128)(2,1)S(1)}, u32[]{:S(2)}, u32[]{:S(2)}) collective-permute-start(bf16[1024,352]{0,1:T(8,128)(2,1)S(1)} %copy.153), channel_id=1, source_target_pairs={{0,16},{16,0},{1,17},{17,1},{2,18},{18,2},{3,19},{19,3},{4,20},{20... | collective-permute-start | bytes 2162696 | tf_op jit(solution)/shard_map/ppermute | solution.py:110
  435.7 156.2 %copy-start.22 = (bf16[1,1408,1024]{2,1,0:T(8,128)(2,1)S(1)}, bf16[1,1408,1024]{2,1,0:T(8,128)(2,1)}, u32[]{:S(2)}) copy-start(bf16[1,1408,1024]{2,1,0:T(8,128)(2,1)} %param.35) | copy-start | bytes 8650756
  664.5 36.3 %slice-start = ((s8[7340032]{0:T(1024)(128)(4,1)}), s8[4194304]{0:T(1024)(128)(4,1)S(1)}, s32[]{:S(2)}) async-start(s8[7340032]{0:T(1024)(128)(4,1)} %bitcast.304), calls=%async_computation.26 | async-start | bytes 8388608
  680.4 20.4 slice-start.1
  729.8 24.4 %copy-start.18 = (bf16[1792,2048]{1,0:T(8,128)(2,1)}, bf16[1792,2048]{1,0:T(8,128)(2,1)S(1)}, u32[]{:S(2)}) copy-start(bf16[1792,2048]{1,0:T(8,128)(2,1)S(1)} %get-tuple-element.67) | copy-start | bytes 22020100
  849.1 358.9 %reduce-scatter.9.cloned.1.call-start = ((), (), s32[]{:S(2)}) async-start(), calls=%async_computation.11 | async-start | bytes 17825792 | tf_op jit(solution)/shard_map/reduce_scatter | solution.py:95
  849.1 23.2 %copy-start.31 = (bf16[4096,176]{0,1:T(8,128)(2,1)S(1)}, bf16[4096,176]{0,1:T(8,128)(2,1)}, u32[]{:S(2)}) copy-start(bf16[4096,176]{0,1:T(8,128)(2,1)} %get-tuple-element.38) | copy-start | bytes 4325380
  892.3 134.0 %copy-start.4 = (f32[256,2048]{1,0:T(8,128)S(1)}, f32[256,2048]{1,0:T(8,128)}, u32[]{:S(2)}) copy-start(f32[256,2048]{1,0:T(8,128)} %copy-done.3) | copy-start | bytes 6291460
  892.3 134.0 %copy-start.8 = (bf16[2048,128]{1,0:T(8,128)(2,1)S(1)}, bf16[2048,128]{1,0:T(8,128)(2,1)}, u32[]{:S(2)}) copy-start(bf16[2048,128]{1,0:T(8,128)(2,1)} %copy-done.7) | copy-start | bytes 1572868
  892.3 134.0 %copy-start.53 = (f32[2048]{0:T(1024)S(1)}, f32[2048]{0:T(1024)}, u32[]{:S(2)}) copy-start(f32[2048]{0:T(1024)} %copy-done.52) | copy-start | bytes 24580
  892.3 134.0 %copy-start.59 = (f32[256]{0:T(256)S(1)}, f32[256]{0:T(256)}, u32[]{:S(2)}) copy-start(f32[256]{0:T(256)} %copy-done.58) | copy-start | bytes 3076
  892.3 137.9 %copy-start.70 = (f32[256]{0:T(256)S(1)}, f32[256]{0:T(256)}, u32[]{:S(2)}) copy-start(f32[256]{0:T(256)} %copy-done.69) | copy-start | bytes 3076
  893.6 10.2 all-to-all-start.1
  897.1 555.4 %reduce-scatter.13.cloned.1.call-start = ((), (), s32[]{:S(2)}) async-start(), calls=%async_computation.14 | async-start | bytes 5013504 | tf_op jit(solution)/shard_map/reduce_scatter | solution.py:95
  903.8 307.9 %copy-start.48 = (f32[16,1,256]{2,1,0:T(1,128)}, f32[16,1,256]{2,1,0:T(1,128)S(1)}, u32[]{:S(2)}) copy-start(f32[16,1,256]{2,1,0:T(1,128)S(1)} %all-to-all-done.1) | copy-start | bytes 49156
  904.6 307.2 %copy-start.64 = (f32[256]{0:T(256)}, f32[256]{0:T(256)S(1)}, u32[]{:S(2)}) copy-start(f32[256]{0:T(256)S(1)} %fusion.72) | copy-start | bytes 3076
  1377.8 379.0 %reduce-scatter.21.cloned.1.call-start = ((), (), s32[]{:S(2)}) async-start(), calls=%async_computation.18 | async-start | bytes 4325376 | tf_op jit(solution)/shard_map/reduce_scatter | solution.py:87
  1403.7 354.7 %reduce-scatter.15.cloned.1.call-start = ((), (), s32[]{:S(2)}) async-start(), calls=%async_computation.15 | async-start | bytes 2162688 | tf_op jit(solution)/shard_map/reduce_scatter | solution.py:87
  1415.9 37.6 %copy-start.38 = (f32[2,128,32]{1,0,2:T(2,128)S(1)}, f32[2,128,32]{1,0,2:T(2,128)}, u32[]{:S(2)}) copy-start(f32[2,128,32]{1,0,2:T(2,128)} %copy-done.37) | copy-start | bytes 98308
  1415.9 37.6 %copy-start.40 = (f32[2,128,32]{1,0,2:T(2,128)S(1)}, f32[2,128,32]{1,0,2:T(2,128)}, u32[]{:S(2)}) copy-start(f32[2,128,32]{1,0,2:T(2,128)} %copy-done.39) | copy-start | bytes 98308
  1415.9 37.7 %copy-start.47 = (f32[4,8,2,128]{3,1,2,0:T(8,128)S(1)}, f32[4,8,2,128]{3,1,2,0:T(8,128)}, u32[]{:S(2)}) copy-start(f32[4,8,2,128]{3,1,2,0:T(8,128)} %copy-done.46) | copy-start | bytes 98308
  1416.2 38.9 %copy-start.10 = (f32[256,576]{0,1:T(8,128)S(1)}, f32[256,576]{0,1:T(8,128)}, u32[]{:S(2)}) copy-start(f32[256,576]{0,1:T(8,128)} %copy-done.9) | copy-start | bytes 1769476
  1416.2 38.9 %copy-start.56 = (f32[512]{0:T(512)S(1)}, f32[512]{0:T(512)}, u32[]{:S(2)}) copy-start(f32[512]{0:T(512)} %copy-done.55) | copy-start | bytes 6148
  1416.2 38.9 %copy-start.63 = (f32[256]{0:T(256)S(1)}, f32[256]{0:T(256)}, u32[]{:S(2)}) copy-start(f32[256]{0:T(256)} %copy-done.62) | copy-start | bytes 3076
  1416.2 39.1 %copy-start.67 = (f32[256]{0:T(256)S(1)}, f32[256]{0:T(256)}, u32[]{:S(2)}) copy-start(f32[256]{0:T(256)} %copy-done.66) | copy-start | bytes 3076
  1467.1 406.1 %reduce-scatter.19.cloned.1.call-start = ((), (), s32[]{:S(2)}) async-start(), calls=%async_computation.17 | async-start | bytes 2703360 | tf_op jit(solution)/shard_map/reduce_scatter | solution.py:87
  1473.8 546.8 %reduce-scatter.23.cloned.1.call-start = ((), (), s32[]{:S(2)}) async-start(), calls=%async_computation.19 | async-start | bytes 8650752 | tf_op jit(solution)/shard_map/reduce_scatter | solution.py:87
  1480.8 697.3 %reduce-scatter.17.cloned.1.call-start = ((), (), s32[]{:S(2)}) async-start(), calls=%async_computation.16 | async-start | bytes 12976128 | tf_op jit(solution)/shard_map/reduce_scatter | solution.py:87
  1503.6 67.9 %collective-permute-start.5 = (bf16[1024,352]{0,1:T(8,128)(2,1)}, bf16[1024,352]{0,1:T(8,128)(2,1)S(1)}, u32[]{:S(2)}, u32[]{:S(2)}) collective-permute-start(bf16[1024,352]{0,1:T(8,128)(2,1)} %dynamic-slice_convert_fusion.3), channel_id=1, source_target_pairs={{0,16},{16,0},{1,17},{17,1},{2,18},{18,2},{3,19},{19,3},{4,20},{20... | collective-permute-start | bytes 2162696 | tf_op jit(solution)/shard_map/ppermute | solution.py:126
  1519.8 30.7 %slice-start.9 = ((s8[7340032]{0:T(1024)(128)(4,1)}), s8[4194304]{0:T(1024)(128)(4,1)S(1)}, s32[]{:S(2)}) async-start(s8[7340032]{0:T(1024)(128)(4,1)} %bitcast.320), calls=%async_computation.35 | async-start | bytes 8388608
  1521.9 28.6 %slice-start.10 = ((s8[7340032]{0:T(1024)(128)(4,1)}), s8[3145728]{0:T(1024)(128)(4,1)S(1)}, s32[]{:S(2)}) async-start(s8[7340032]{0:T(1024)(128)(4,1)} %bitcast.320), calls=%async_computation.36 | async-start | bytes 6291456
  1521.9 213.6 %collective-permute-start.9 = (bf16[1408,1024]{1,0:T(8,128)(2,1)}, bf16[1408,1024]{1,0:T(8,128)(2,1)}, u32[]{:S(2)}, u32[]{:S(2)}) collective-permute-start(bf16[1408,1024]{1,0:T(8,128)(2,1)} %dynamic-slice_convert_fusion), channel_id=1, source_target_pairs={{0,16},{16,0},{1,17},{17,1},{2,18},{18,2},{3,19},{19,3},{4,20},{20... | collective-permute-start | bytes 8650760 | tf_op jit(solution)/shard_map/ppermute | solution.py:126
  1545.1 21.9 %slice-start.2 = ((s8[16777216]{0:T(1024)(128)(4,1)}), s8[4194304]{0:T(1024)(128)(4,1)S(1)}, s32[]{:S(2)}) async-start(s8[16777216]{0:T(1024)(128)(4,1)} %bitcast.308), calls=%async_computation.28 | async-start | bytes 8388608
  1549.8 17.2 slice-start.5
  1549.8 17.2 copy-start.32
  1549.8 193.4 %collective-permute-start.7 = (bf16[1024,1408]{1,0:T(8,128)(2,1)}, bf16[1024,1408]{1,0:T(8,128)(2,1)}, u32[]{:S(2)}, u32[]{:S(2)}) collective-permute-start(bf16[1024,1408]{1,0:T(8,128)(2,1)} %dynamic-slice_convert_fusion.2), channel_id=1, source_target_pairs={{0,16},{16,0},{1,17},{17,1},{2,18},{18,2},{3,19},{19,3},{4,20},{20... | collective-permute-start | bytes 8650760 | tf_op jit(solution)/shard_map/ppermute | solution.py:126
  1574.8 143.7 %all-to-all-start.2 = ((bf16[16,64,352]{2,1,0:T(8,128)(2,1)}), bf16[16,64,352]{2,1,0:T(8,128)(2,1)}, u32[]{:S(2)}, u32[]{:S(2)}) async-start(bf16[16,64,352]{2,1,0:T(8,128)(2,1)} %bitcast.349), calls=%async_computation.10 | async-start | bytes 1572864 | tf_op jit(solution)/shard_map/all_to_all | solution.py:372
  1583.7 166.2 %collective-permute-start.8 = (bf16[1024,1408]{1,0:T(8,128)(2,1)}, bf16[1024,1408]{1,0:T(8,128)(2,1)}, u32[]{:S(2)}, u32[]{:S(2)}) collective-permute-start(bf16[1024,1408]{1,0:T(8,128)(2,1)} %dynamic-slice_convert_fusion.1), channel_id=1, source_target_pairs={{0,16},{16,0},{1,17},{17,1},{2,18},{18,2},{3,19},{19,3},{4,20},{20... | collective-permute-start | bytes 8650760 | tf_op jit(solution)/shard_map/ppermute | solution.py:126
  1586.6 129.8 %collective-permute-start.6 = (bf16[88,2048]{1,0:T(8,128)(2,1)S(1)}, bf16[88,2048]{1,0:T(8,128)(2,1)}, u32[]{:S(2)}, u32[]{:S(2)}) collective-permute-start(bf16[88,2048]{1,0:T(8,128)(2,1)S(1)} %dynamic-slice_convert_fusion.4), channel_id=1, source_target_pairs={{0,16},{16,0},{1,17},{17,1},{2,18},{18,2},{3,19},{19,3},{4,20},{20... | collective-permute-start | bytes 1081352 | tf_op jit(solution)/shard_map/ppermute | solution.py:126
  (53 other events, 454.5 us)
Sparse Core Ops, SparseCore 0:
  10.9 60.7 all-gather.16
  76.4 54.9 all-gather.18
  134.3 60.2 all-gather.20
  197.3 94.5 all-gather.22
  294.6 75.8 all-gather.24
  372.5 142.4 all-gather.14
  517.1 125.0 all-gather.26
  849.2 177.0 reduce-scatter.10
  1030.4 177.5 reduce-scatter.8
  1377.9 74.5 reduce-scatter.12
  1454.9 143.6 reduce-scatter.20
  1600.8 136.3 reduce-scatter.14
  1739.4 133.7 reduce-scatter.18
  1875.3 145.2 reduce-scatter.22
  2026.5 151.6 reduce-scatter.16

commit v2 on v1

--- a/solution.py
+++ b/solution.py
@@ -1,8 +1,12 @@
+import functools
+import itertools
 import math
 
 import jax
 import jax.numpy as jnp
 from jax import lax
+from jax.experimental import pallas as pl
+from jax.experimental.pallas import tpu as pltpu
 from jax.sharding import PartitionSpec as P
 
 D = 2048
@@ -76,15 +80,428 @@
     )
 
 
-BOTH = ("dp", "expert")
-
-
-def gather_all(x):
-    return lax.all_gather(x, BOTH, axis=0, tiled=False)
-
-
-def scatter_all(x):
-    return lax.psum_scatter(x, BOTH, scatter_dimension=0, tiled=False)
+MESH_ID = pl.DeviceIdType.MESH
+ANYWHERE = pl.BlockSpec(memory_space=pl.ANY)
+
+
+def dims_of():
+    n_expert = lax.axis_size("expert")
+    core = 2 if n_expert % 2 == 0 else 1
+    z = 4 if n_expert % (4 * core) == 0 else 1
+    return {"x": lax.axis_size("dp"), "z": z, "y": n_expert // (z * core), "c": core}
+
+
+def place_of(sizes):
+    e = lax.axis_index("expert")
+    return {
+        "x": lax.axis_index("dp"),
+        "z": e // (sizes["y"] * sizes["c"]),
+        "y": (e // sizes["c"]) % sizes["y"],
+        "c": e % sizes["c"],
+    }
+
+
+def expert_of(sizes, at):
+    return (at["z"] * sizes["y"] + at["y"]) * sizes["c"] + at["c"]
+
+
+def device_of(sizes, at):
+    return (at["x"], expert_of(sizes, at))
+
+
+def slot_of(sizes, at, whole):
+    e = expert_of(sizes, at)
+    if whole:
+        return at["x"] * (sizes["z"] * sizes["y"] * sizes["c"]) + e
+    return e
+
+
+def nearest(p, k, size):
+    if k == 0:
+        return p
+    if size == 2:
+        return 1 - p
+    if size == 4:
+        return (1 + p % 2, (2 + 3 * p) % 5, 3 - 3 * (p // 2))[k - 1]
+    return (p + k) % size
+
+
+WEIGHT = {"z": 10, "y": 10, "x": 10, "c": 2}
+
+
+def visits(order, sizes):
+    every = itertools.product(*[range(sizes[d]) for d in order])
+    return sorted(every, key=lambda ks: (sum(k * WEIGHT[d] for k, d in zip(ks, order)), ks))
+
+
+def when(condition, action):
+    if condition is True:
+        action()
+    else:
+        pl.when(condition)(action)
+
+
+def greet(names, sizes, at):
+    barrier = pltpu.get_barrier_semaphore()
+    around = []
+    for d in names:
+        for step in (1, -1):
+            if sizes[d] == 2 and step == 1:
+                around.append((True, dict(at, **{d: 1 - at[d]})))
+            elif sizes[d] > 2:
+                there = at[d] < sizes[d] - 1 if step == 1 else at[d] > 0
+                around.append((there, dict(at, **{d: at[d] + step})))
+    for there, to in around:
+        when(
+            there,
+            lambda to=to: pl.semaphore_signal(
+                barrier, inc=1, device_id=device_of(sizes, to), device_id_type=MESH_ID
+            ),
+        )
+    pl.semaphore_wait(barrier, sum(1 if there is True else there.astype(jnp.int32) for there, _ in around))
+
+
+def ways(ks, j, order, sizes, at, where):
+    d = order[j]
+    size = sizes[d]
+    if size == 1 or any(ks[j + 1 :]):
+        return
+    p, q = at[d], where[d]
+    if size == 2:
+        if ks[j] == 0:
+            yield 0, True, dict(at, **{d: 1 - p})
+        return
+    if ks[j] == 0:
+        yield 0, p < size - 1, dict(at, **{d: p + 1})
+        yield 1, p > 0, dict(at, **{d: p - 1})
+    else:
+        yield 0, (q < p) & (p < size - 1), dict(at, **{d: p + 1})
+        yield 1, (q > p) & (p > 0), dict(at, **{d: p - 1})
+
+
+def count_sends(order, sizes):
+    total = 0
+    zero = {d: 0 for d in order}
+    for ks in visits(order, sizes):
+        for j in range(len(order)):
+            total += len(list(ways(ks, j, order, sizes, zero, zero)))
+    return total
+
+
+def gather_kernel(items, whole, sizes, *refs):
+    arrays = items[-1][0] + 1
+    count = len(items)
+    orders = [order for _, _, order in items]
+    ins = [part_of(refs[a], chunk) for a, chunk, _ in items]
+    outs = [functools.partial(slot_part, refs[arrays + a], chunk) for a, chunk, _ in items]
+    own_sem = refs[2 * arrays]
+    sends = refs[2 * arrays + 1 : 2 * arrays + 1 + count]
+    recvs = refs[2 * arrays + 1 + count :]
+    at = place_of(sizes)
+    names = sorted({d for order in orders for d in order})
+    greet(names, sizes, at)
+    me = slot_of(sizes, at, whole)
+    keep = []
+    for a in range(count):
+        own = pltpu.make_async_copy(ins[a], outs[a](me), own_sem.at[a])
+        own.start()
+        keep.append(own)
+    started = []
+    plan = []
+    for a, order in enumerate(orders):
+        for rank, ks in enumerate(visits(order, sizes)):
+            weight = sum(k * WEIGHT[d] for k, d in zip(ks, order))
+            plan.append((weight, rank, a, ks))
+    plan.sort(key=lambda item: item[:3])
+    number = [0] * count
+    for _, _, a, ks in plan:
+        order = orders[a]
+        where = dict(at)
+        for d, k in zip(order, ks):
+            where[d] = nearest(at[d], k, sizes[d])
+        slot = slot_of(sizes, where, whole)
+        here = outs[a](slot)
+        if any(ks):
+            pltpu.make_async_copy(here, here, recvs[a].at[slot]).wait()
+            source = here
+        else:
+            source = ins[a]
+        for j in reversed(range(len(order))):
+            for _, there, to in ways(ks, j, order, sizes, at, where):
+                copy = pltpu.make_async_remote_copy(
+                    src_ref=source,
+                    dst_ref=here,
+                    send_sem=sends[a].at[number[a]],
+                    recv_sem=recvs[a].at[slot],
+                    device_id=device_of(sizes, to),
+                    device_id_type=MESH_ID,
+                )
+                number[a] += 1
+                when(there, copy.start)
+                started.append((there, copy))
+    for there, copy in started:
+        when(there, copy.wait_send)
+    for own in keep:
+        own.wait()
+
+
+def part_of(ref, chunk):
+    return ref if chunk is None else ref.at[chunk]
+
+
+def slot_part(ref, chunk, slot):
+    return ref.at[slot] if chunk is None else ref.at[slot, chunk]
+
+
+def items_of(orders, shapes):
+    items = []
+    for a, (order, shape) in enumerate(zip(orders, shapes)):
+        if len(shape) == 2:
+            items.append((a, None, order))
+        else:
+            for chunk in range(shape[0]):
+                items.append((a, chunk, order[chunk] if isinstance(order, list) else order))
+    return items
+
+
+def gather(arrays, orders, whole, identity):
+    sizes = dims_of()
+    total = (sizes["x"] if whole else 1) * lax.axis_size("expert")
+    items = items_of(orders, [a.shape for a in arrays])
+    sent = total * sum(a.size * a.dtype.itemsize for a in arrays)
+    return pl.pallas_call(
+        functools.partial(gather_kernel, items, whole, sizes),
+        out_shape=[jax.ShapeDtypeStruct((total,) + a.shape, a.dtype) for a in arrays],
+        in_specs=[ANYWHERE] * len(arrays),
+        out_specs=[ANYWHERE] * len(arrays),
+        scratch_shapes=[pltpu.SemaphoreType.DMA((len(items),))]
+        + [pltpu.SemaphoreType.DMA((count_sends(order, sizes),)) for _, _, order in items]
+        + [pltpu.SemaphoreType.DMA((total,)) for _ in items],
+        compiler_params=pltpu.CompilerParams(collective_id=identity, has_side_effects=True),
+        cost_estimate=pl.CostEstimate(flops=0, bytes_accessed=sent * 6, transcendentals=0),
+    )(*arrays)
+
+
+def box_of(j, order, sizes, where, extra):
+    base = 0
+    for i in range(j):
+        base += math.prod(sizes[d] for d in order[:i]) * boxes_along(sizes[order[i]])
+    inner = 0
+    for d in order[:j]:
+        inner = inner * sizes[d] + where[d]
+    wide = boxes_along(sizes[order[j]])
+    last = 0 if wide == 1 else (sizes[order[j]] if extra else where[order[j]])
+    return base + inner * wide + last
+
+
+def boxes_along(size):
+    return {1: 0, 2: 1}.get(size, size + 1)
+
+
+def boxes(order, sizes):
+    return sum(
+        math.prod(sizes[d] for d in order[:i]) * boxes_along(sizes[order[i]])
+        for i in range(len(order))
+    )
+
+
+def staged_of(order, sizes, where):
+    inner = 0
+    for d in order[:-1]:
+        inner = inner * sizes[d] + where[d]
+    return inner
+
+
+def add_up(target, terms, dtype):
+    rows = target.shape[0]
+    step = 16 if rows % 16 == 0 else rows
+
+    def one(i, carry):
+        part = pl.ds(pl.multiple_of(i * step, step), step)
+        total = terms[0][part, :].astype(jnp.float32)
+        for term in terms[1:]:
+            total = total + term[part, :].astype(jnp.float32)
+        target[part, :] = total.astype(dtype)
+        return carry
+
+    lax.fori_loop(0, rows // step, one, 0)
+
+
+def scatter_kernel(items, whole, sizes, *refs):
+    arrays = items[-1][0] + 1
+    count = len(items)
+    orders = [order for _, _, order in items]
+    ins = [functools.partial(slot_part, refs[a], chunk) for a, chunk, _ in items]
+    outs = [part_of(refs[arrays + a], chunk) for a, chunk, _ in items]
+    refs = refs[2 * arrays :]
+    staged, landed, sends, recvs, loads = [
+        refs[i * count : (i + 1) * count] for i in range(5)
+    ]
+    at = place_of(sizes)
+    names = sorted({d for order in orders for d in order})
+    plan = []
+    for a, order in enumerate(orders):
+        for rank, ks in enumerate(visits(order, sizes)):
+            weight = sum(k * WEIGHT[d] for k, d in zip(ks, order))
+            plan.append((weight, rank, a, ks))
+    plan.sort(key=lambda item: item[:3], reverse=True)
+    slots = {}
+    for _, _, a, ks in plan:
+        order = orders[a]
+        where = dict(at)
+        for d, k in zip(order, ks):
+            where[d] = nearest(at[d], k, sizes[d])
+        slots[a, ks] = (where, slot_of(sizes, where, whole))
+    for _, _, a, ks in plan:
+        if ks[-1] == 0:
+            where, slot = slots[a, ks]
+            index = staged_of(orders[a], sizes, where)
+            pltpu.make_async_copy(
+                ins[a](slot), staged[a].at[index], loads[a].at[index]
+            ).start()
+    greet(names, sizes, at)
+    started = []
+    number = [0] * count
+
+    def send(a, source, box, to, there):
+        copy = pltpu.make_async_remote_copy(
+            src_ref=source,
+            dst_ref=landed[a].at[box],
+            send_sem=sends[a].at[number[a]],
+            recv_sem=recvs[a].at[box],
+            device_id=device_of(sizes, to),
+            device_id_type=MESH_ID,
+        )
+        number[a] += 1
+        when(there, copy.start)
+        started.append((there, copy))
+
+    for _, _, a, ks in plan:
+        if ks[-1]:
+            order = orders[a]
+            where, slot = slots[a, ks]
+            j = len(order) - 1
+            to = dict(at, **{order[j]: 1 - at[order[j]]})
+            send(a, ins[a](slot), box_of(j, order, sizes, where, False), to, True)
+    for _, _, a, ks in plan:
+        if ks[-1]:
+            continue
+        order = orders[a]
+        where, slot = slots[a, ks]
+        index = staged_of(order, sizes, where)
+        mine = staged[a].at[index]
+        pltpu.make_async_copy(ins[a](slot), mine, loads[a].at[index]).wait()
+        leaves = max([j for j in range(len(order)) if ks[j]], default=-1)
+        terms = [mine]
+        loose = []
+        for j in reversed(range(len(order))):
+            d = order[j]
+            if j < leaves or sizes[d] == 1:
+                break
+            if sizes[d] == 2:
+                if ks[j] == 0:
+                    box = box_of(j, order, sizes, where, False)
+                    terms.append((box, True))
+                continue
+            p, q = at[d], where[d]
+            if j == leaves:
+                far = ((q > p) & (p > 0)) | ((q < p) & (p < sizes[d] - 1))
+                terms.append((box_of(j, order, sizes, where, False), far))
+            else:
+                terms.append((box_of(j, order, sizes, where, False), p > 0))
+                terms.append((box_of(j, order, sizes, where, True), p < sizes[d] - 1))
+        sure = [mine]
+        for box, there in terms[1:]:
+            ref = landed[a].at[box]
+            waiting = pltpu.make_async_copy(ref, ref, recvs[a].at[box])
+            if there is True:
+                waiting.wait()
+                sure.append(ref)
+            else:
+
+                def take(ref=ref, waiting=waiting, mine=mine):
+                    waiting.wait()
+                    add_up(mine, [mine, ref], mine.dtype)
+
+                loose.append((there, take))
+        if len(sure) > 1 and leaves >= 0:
+            add_up(mine, sure, mine.dtype)
+            sure = [mine]
+        for there, take in loose:
+            when(there, take)
+        if leaves < 0:
+            add_up(outs[a], sure, outs[a].dtype)
+            continue
+        d = order[leaves]
+        if sizes[d] == 2:
+            send(
+                a,
+                mine,
+                box_of(leaves, order, sizes, where, False),
+                dict(at, **{d: 1 - at[d]}),
+                True,
+            )
+        else:
+            p, q = at[d], where[d]
+            send(
+                a, mine, box_of(leaves, order, sizes, where, False), dict(at, **{d: p + 1}), q > p
+            )
+            send(
+                a,
+                mine,
+                jnp.where(
+                    q + 1 == p,
+                    box_of(leaves, order, sizes, where, True),
+                    box_of(leaves, order, sizes, where, False),
+                ),
+                dict(at, **{d: p - 1}),
+                q < p,
+            )
+    for there, copy in started:
+        when(there, copy.wait_send)
+
+
+def scatter_sends(order, sizes):
+    total = 0
+    for ks in visits(order, sizes):
+        leaves = max([j for j in range(len(order)) if ks[j]], default=-1)
+        if leaves >= 0:
+            total += 1 if sizes[order[leaves]] == 2 else 2
+    return total
+
+
+def scatter(arrays, orders, whole, identity, out_dtype=jnp.float32):
+    sizes = dims_of()
+    items = items_of(orders, [a.shape[1:] for a in arrays])
+    shapes = [arrays[a].shape[-2:] for a, _, _ in items]
+    types = [arrays[a].dtype for a, _, _ in items]
+    orders = [order for _, _, order in items]
+    stages = [math.prod(sizes[d] for d in order[:-1]) for order in orders]
+    landing = [boxes(order, sizes) for order in orders]
+    return pl.pallas_call(
+        functools.partial(scatter_kernel, items, whole, sizes),
+        out_shape=[jax.ShapeDtypeStruct(a.shape[1:], out_dtype) for a in arrays],
+        in_specs=[ANYWHERE] * len(arrays),
+        out_specs=[pl.BlockSpec(memory_space=pltpu.VMEM)] * len(arrays),
+        scratch_shapes=[pltpu.VMEM((n,) + s, t) for n, s, t in zip(stages, shapes, types)]
+        + [pltpu.VMEM((n,) + s, t) for n, s, t in zip(landing, shapes, types)]
+        + [pltpu.SemaphoreType.DMA((scatter_sends(order, sizes),)) for order in orders]
+        + [pltpu.SemaphoreType.DMA((n,)) for n in landing]
+        + [pltpu.SemaphoreType.DMA((n,)) for n in stages],
+        compiler_params=pltpu.CompilerParams(
+            collective_id=identity, has_side_effects=True, vmem_limit_bytes=60 << 20
+        ),
+    )(*arrays)
+
+
+PLANE = ("z", "y", "c")
+ZYX = ("z", "y", "x", "c")
+ZXY = ("z", "x", "y", "c")
+XYZ = ("x", "y", "z", "c")
+YZ = ("y", "z", "c")
+CHUNKS = 4
+CHUNK_ORDERS = [PLANE, PLANE, PLANE, YZ]
+ALL_ORDERS = [ZYX, XYZ, XYZ, ZXY, XYZ]
 
 
 def gather_plane(x):
@@ -127,38 +544,168 @@
     return lax.dynamic_slice_in_dim(x, index * half, half, axis) + arrived.astype(jnp.float32)
 
 
-def attention_forward(queries, keys, values, allowed, score_scale):
-    raw = jnp.einsum("mqhd,mkhd->mhqk", queries, keys, preferred_element_type=jnp.float32)
-    scores = jnp.where(allowed[:, None], raw * score_scale, NEGATIVE)
-    highest = jnp.max(scores, axis=-1, keepdims=True)
-    log_total = highest + jnp.log(jnp.sum(jnp.exp(scores - highest), axis=-1, keepdims=True))
-    weights = low(jnp.exp(scores - log_total))
-    mixture = jnp.einsum("mhqk,mkhd->mqhd", weights, values, preferred_element_type=jnp.float32)
-    return low(mixture), log_total
-
-
-def attention_backward(queries, keys, values, allowed, score_scale, log_total, grad_mixture):
-    raw = jnp.einsum("mqhd,mkhd->mhqk", queries, keys, preferred_element_type=jnp.float32)
-    scores = jnp.where(allowed[:, None], raw * score_scale, NEGATIVE)
-    probs = jnp.exp(scores - log_total)
-    grad_probs = jnp.einsum(
-        "mqhd,mkhd->mhqk", grad_mixture, values, preferred_element_type=jnp.float32
-    )
-    grad_scores = low(
-        probs * (grad_probs - jnp.sum(grad_probs * probs, axis=-1, keepdims=True))
-    )
-    grad_queries = (
-        jnp.einsum("mhqk,mkhd->mqhd", grad_scores, keys, preferred_element_type=jnp.float32)
-        * score_scale
-    )
-    grad_keys = (
-        jnp.einsum("mhqk,mqhd->mkhd", grad_scores, queries, preferred_element_type=jnp.float32)
-        * score_scale
-    )
-    grad_values = jnp.einsum(
-        "mhqk,mqhd->mkhd", low(probs), grad_mixture, preferred_element_type=jnp.float32
-    )
-    return grad_queries, grad_keys, grad_values
+def cross(a, b):
+    return lax.dot_general(a, b, (((1,), (1,)), ((), ())), preferred_element_type=jnp.float32)
+
+
+def heads_of(quads, rows, qn, qa, qb):
+    lanes = lax.broadcasted_iota(jnp.int32, (1, qa.shape[1]), 1) // (ROPE // 2)
+    ours = lanes == pl.program_id(0) % quads
+    nothing = jnp.zeros((), qa.dtype)
+    return (
+        ours,
+        qn[rows, :],
+        jnp.where(ours, qa[rows, :], nothing),
+        jnp.where(ours, qb[rows, :], nothing),
+    )
+
+
+def attend_kernel(tokens, scale, qn, qa, qb, latent, ka, kb, expand, bias, out):
+    quads = qa.shape[1] // (ROPE // 2)
+    for m in range(MICRO):
+        rows = pl.ds(m * tokens, tokens)
+        pair = low(dot(latent[m], expand[...]))
+        keys, values = pair[:, :NOPE], pair[:, NOPE:]
+        _, own, first, second = heads_of(quads, rows, qn, qa, qb)
+        scores = cross(own, keys) + cross(first, ka[m]) + cross(second, kb[m])
+        scores = scores * scale + bias[m]
+        raised = jnp.exp(scores - jnp.max(scores, axis=1, keepdims=True))
+        weights = low(raised / jnp.sum(raised, axis=1, keepdims=True))
+        out[rows, :] = low(dot(weights, values))
+
+
+def attend_back_kernel(
+    tokens, scale, qn, qa, qb, grad, latent, turned, ka, kb, expand, bias, gqn, gqa, gqb, glat, gka, gkb, gexp
+):
+    head = pl.program_id(0)
+    quads = qa.shape[1] // (ROPE // 2)
+
+    @pl.when(head == 0)
+    def _():
+        glat[...] = jnp.zeros_like(glat)
+        gka[...] = jnp.zeros_like(gka)
+        gkb[...] = jnp.zeros_like(gkb)
+
+    @pl.when(head % quads == 0)
+    def _():
+        gqa[...] = jnp.zeros_like(gqa)
+        gqb[...] = jnp.zeros_like(gqb)
+
+    expand_total = None
+    for m in range(MICRO):
+        rows = pl.ds(m * tokens, tokens)
+        pair = low(dot(latent[m], expand[...]))
+        keys, values = pair[:, :NOPE], pair[:, NOPE:]
+        ours, own, first, second = heads_of(quads, rows, qn, qa, qb)
+        grad_rows = grad[rows, :]
+        scores = cross(keys, own) + cross(ka[m], first) + cross(kb[m], second)
+        scores = scores * scale + bias[m]
+        raised = jnp.exp(scores - jnp.max(scores, axis=0, keepdims=True))
+        probs = raised / jnp.sum(raised, axis=0, keepdims=True)
+        grad_probs = cross(values, grad_rows)
+        shift = jnp.sum(grad_probs * probs, axis=0, keepdims=True)
+        back = low(probs * (grad_probs - shift))
+        across = back.T
+        gqn[rows, :] = low(dot(across, keys) * scale)
+        gqa[rows, :] += jnp.where(ours, dot(across, ka[m]) * scale, 0.0)
+        gqb[rows, :] += jnp.where(ours, dot(across, kb[m]) * scale, 0.0)
+        gka[m] += dot(back, first) * scale
+        gkb[m] += dot(back, second) * scale
+        both = jnp.concatenate(
+            [low(dot(back, own) * scale), low(dot(low(probs), grad_rows))], axis=1
+        )
+        glat[m] += cross(both, expand[...])
+        part = dot(turned[m], both)
+        expand_total = part if expand_total is None else expand_total + part
+    gexp[...] = low(expand_total)
+
+
+def whole_block(a):
+    return pl.BlockSpec(a.shape, lambda h: (0,) * len(a.shape))
+
+
+def attention_specs(rows, quads):
+    return [
+        pl.BlockSpec((rows, NOPE), lambda h: (0, h)),
+        pl.BlockSpec((rows, 128), lambda h: (0, h // quads)),
+        pl.BlockSpec((rows, 128), lambda h: (0, h // quads)),
+    ]
+
+
+def attention_forward(tokens, scale, qn, qa, qb, latent, ka, kb, expand, bias):
+    rows = qn.shape[0]
+    quads = 128 // (ROPE // 2)
+    return pl.pallas_call(
+        functools.partial(attend_kernel, tokens, scale),
+        grid=(H,),
+        out_shape=jax.ShapeDtypeStruct((rows, H * VDIM), jnp.bfloat16),
+        in_specs=attention_specs(rows, quads)
+        + [whole_block(latent), whole_block(ka), whole_block(kb)]
+        + [pl.BlockSpec((LAT, NOPE + VDIM), lambda h: (0, h)), whole_block(bias)],
+        out_specs=pl.BlockSpec((rows, VDIM), lambda h: (0, h)),
+        compiler_params=pltpu.CompilerParams(vmem_limit_bytes=56 << 20),
+        cost_estimate=pl.CostEstimate(
+            flops=25 * 10**9, bytes_accessed=20 * 10**6, transcendentals=0
+        ),
+    )(qn, qa, qb, latent, ka, kb, expand, bias)
+
+
+def attention_backward(tokens, scale, qn, qa, qb, grad, latent, ka, kb, expand, bias):
+    rows = qn.shape[0]
+    quads = 128 // (ROPE // 2)
+    turned = jnp.swapaxes(latent, 1, 2)
+    single = jax.ShapeDtypeStruct
+    return pl.pallas_call(
+        functools.partial(attend_back_kernel, tokens, scale),
+        grid=(H,),
+        out_shape=[
+            single(qn.shape, jnp.bfloat16),
+            single(qa.shape, jnp.float32),
+            single(qb.shape, jnp.float32),
+            single(latent.shape, jnp.float32),
+            single(ka.shape, jnp.float32),
+            single(kb.shape, jnp.float32),
+            single(expand.shape, jnp.bfloat16),
+        ],
+        in_specs=attention_specs(rows, quads)
+        + [pl.BlockSpec((rows, VDIM), lambda h: (0, h))]
+        + [whole_block(latent), whole_block(turned), whole_block(ka), whole_block(kb)]
+        + [pl.BlockSpec((LAT, NOPE + VDIM), lambda h: (0, h)), whole_block(bias)],
+        out_specs=attention_specs(rows, quads)
+        + [whole_block(latent), whole_block(ka), whole_block(kb)]
+        + [pl.BlockSpec((LAT, NOPE + VDIM), lambda h: (0, h))],
+        compiler_params=pltpu.CompilerParams(vmem_limit_bytes=56 << 20),
+        cost_estimate=pl.CostEstimate(
+            flops=50 * 10**9, bytes_accessed=30 * 10**6, transcendentals=0
+        ),
+    )(qn, qa, qb, grad, latent, turned, ka, kb, expand, bias)
+
+
+def combine_kernel(picked, rows, left, right, out):
+    out[...] = low(dot(picked[0], rows[0]) + dot(left[...], right[...]))
+
+
+def combine(picked, rows, left, right):
+    groups, group_rows, slots = picked.shape
+    total, inner = left.shape
+    return pl.pallas_call(
+        combine_kernel,
+        grid=(groups,),
+        out_shape=jax.ShapeDtypeStruct((total, D), jnp.bfloat16),
+        in_specs=[
+            pl.BlockSpec((1, group_rows, slots), lambda g: (g, 0, 0)),
+            pl.BlockSpec((1, slots, D), lambda g: (g, 0, 0)),
+            pl.BlockSpec((group_rows, inner), lambda g: (g, 0)),
+            pl.BlockSpec((inner, D), lambda g: (0, 0)),
+        ],
+        out_specs=pl.BlockSpec((group_rows, D), lambda g: (g, 0)),
+        compiler_params=pltpu.CompilerParams(vmem_limit_bytes=48 << 20),
+        cost_estimate=pl.CostEstimate(
+            flops=2 * total * (slots + inner) * D,
+            bytes_accessed=total * D * 4,
+            transcendentals=0,
+        ),
+    )(picked, rows.reshape(groups, slots, D), left, right)
 
 
 def body(
@@ -192,18 +739,7 @@
     head_width = NOPE + ROPE
     key_width = H * head_width
 
-    expert_gate = gather_dp(expert_gate[0], 0)
-    expert_up = gather_dp(expert_up[0], 0)
-    expert_down = gather_dp(expert_down[0], 1)
     shard = query_weight.shape[0]
-    units = shared_down.shape[0]
-    mine = n_dp * units
-    both = jnp.stack([shared_gate, shared_up], axis=1).reshape(shard, 2, n_dp, n_expert, units)
-    both = both.transpose(3, 0, 1, 2, 4).reshape(n_expert, shard, 2 * mine)
-    both = lax.all_to_all(both, "expert", split_axis=0, concat_axis=0, tiled=True)
-    shared_in = gather_dp(both.reshape(n_expert * shard, 2 * mine), 0)
-    shared_out_weight = gather_dp(shared_down, 0)
-
     small_latent = latent_gain.shape[0]
     small = jnp.concatenate(
         [
@@ -215,36 +751,79 @@
         axis=1,
     )
     small = jnp.pad(small, ((0, 0), (0, 128 - small.shape[1])))
-    all_query = gather_all(query_weight).reshape(D, key_width)
-    all_latent = gather_all(latent_weight).reshape(D, LAT + ROPE)
-    all_expand = gather_all(expand_weight).reshape(LAT, H * (NOPE + VDIM))
-    all_output = gather_all(output_weight.T).reshape(D, H * VDIM)
-    small = gather_all(small)
+    by_head = query_weight.reshape(shard, H, head_width)
+    split_query = jnp.concatenate(
+        [
+            by_head[..., :NOPE].reshape(shard, H * NOPE),
+            by_head[..., NOPE : NOPE + ROPE // 2].reshape(shard, H * ROPE // 2),
+            by_head[..., NOPE + ROPE // 2 :].reshape(shard, H * ROPE // 2),
+        ],
+        axis=1,
+    )
+    all_query, all_latent, all_expand, all_output, small = gather(
+        [split_query, latent_weight, expand_weight.reshape(16, -1), output_weight.T, small],
+        ALL_ORDERS,
+        True,
+        1,
+    )
+    all_query = all_query.reshape(D, key_width)
+    all_latent = all_latent.reshape(D, LAT + ROPE)
+    all_expand = all_expand.reshape(LAT, H * (NOPE + VDIM))
+    all_output = all_output.reshape(D, H * VDIM)
     gain_latent = small[:, :small_latent, experts_count + 2].reshape(LAT).astype(jnp.float32)
     small = small.reshape(D, 128)
     all_router = small[:, :experts_count]
     gain_first = small[:, experts_count].astype(jnp.float32)
     gain_second = small[:, experts_count + 1].astype(jnp.float32)
 
+    (later, all_query) = lax.optimization_barrier(
+        ((expert_gate, expert_up, expert_down, shared_gate, shared_up, shared_down, cotangent), all_query)
+    )
+    expert_gate, expert_up, expert_down, shared_gate, shared_up, shared_down, sent_cotangent = later
+    expert_gate = gather_dp(expert_gate[0], 0)
+    expert_up = gather_dp(expert_up[0], 0)
+    expert_down = gather_dp(expert_down[0], 1)
+    units = shared_down.shape[0]
+    mine = n_dp * units
+    both = jnp.stack([shared_gate, shared_up], axis=1).reshape(shard, 2, n_dp, n_expert, units)
+    both = both.transpose(3, 0, 1, 2, 4).reshape(n_expert, shard, 2 * mine)
+    both = lax.all_to_all(both, "expert", split_axis=0, concat_axis=0, tiled=True)
+    shared_in = gather_dp(both.reshape(n_expert * shard, 2 * mine), 0)
+    padded = -(-(mine + experts_count) // 128) * 128
+    rest = jnp.zeros((D, padded - mine - experts_count), jnp.bfloat16)
+    shared_in = jnp.concatenate(
+        [
+            shared_in[:, :mine],
+            all_router,
+            rest,
+            shared_in[:, mine:],
+            jnp.zeros((D, padded - mine), jnp.bfloat16),
+        ],
+        axis=1,
+    )
+    shared_out_weight = jnp.pad(gather_dp(shared_down, 0), ((0, padded - mine), (0, 0)))
+
+
     positions = lane * tokens + jnp.arange(tokens, dtype=jnp.int32)
     cosine_table, sine_table = angles(positions)
     cosine_rows = jnp.tile(cosine_table, (MICRO, 1))
     sine_rows = jnp.tile(sine_table, (MICRO, 1))
-    head_cosine = cosine_rows[:, None, :]
-    head_sine = sine_rows[:, None, :]
+    head_cosine = jnp.tile(cosine_rows, (1, H))
+    head_sine = jnp.tile(sine_rows, (1, H))
     inputs = layer_input[0].reshape(rows, D).astype(jnp.float32)
     hidden = low(root_normalize(inputs, gain_first))
     latent = dot(hidden, all_latent)
     compressed = low(root_normalize(latent[:, :LAT], gain_latent))
     key_rope = low(rotate(latent[:, LAT:], cosine_rows, sine_rows))
-    line = gather_plane(jnp.concatenate([compressed, key_rope], axis=1))
-    query_heads = dot(hidden, all_query).reshape(rows, H, head_width)
-    queries = low(
-        jnp.concatenate(
-            [query_heads[..., :NOPE], rotate(query_heads[..., NOPE:], head_cosine, head_sine)],
-            axis=-1,
-        )
-    ).reshape(MICRO, tokens, H, head_width)
+    (line,) = gather([jnp.concatenate([compressed, key_rope], axis=1)], [PLANE], False, 2)
+    query = dot(hidden, all_query)
+    plain = H * NOPE
+    half = H * ROPE // 2
+    query_plain = low(query[:, :plain])
+    turn_first = query[:, plain : plain + half]
+    turn_second = query[:, plain + half :]
+    query_first = low(turn_first * head_cosine - turn_second * head_sine)
+    query_second = low(turn_first * head_sine + turn_second * head_cosine)
     reach = (WINDOW + tokens - 2) // tokens
     span = reach + 1
     key_rows = span * tokens
@@ -254,16 +833,10 @@
     window = lax.dynamic_slice_in_dim(line, lane, span, 0)
     window = window.reshape(span, MICRO, tokens, LAT + ROPE).transpose(1, 0, 2, 3)
     window = window.reshape(MICRO, key_rows, LAT + ROPE)
-    window_latent = window[..., :LAT].reshape(MICRO * key_rows, LAT)
-    expanded = low(dot(window_latent, all_expand)).reshape(MICRO, key_rows, H, NOPE + VDIM)
-    keys = jnp.concatenate(
-        [
-            expanded[..., :NOPE],
-            jnp.broadcast_to(window[:, :, None, LAT:], (MICRO, key_rows, H, ROPE)),
-        ],
-        axis=-1,
-    )
-    values = expanded[..., NOPE:]
+    window_latent = window[..., :LAT]
+    quads = 128 // (ROPE // 2)
+    key_first = jnp.tile(window[..., LAT : LAT + ROPE // 2], (1, 1, quads))
+    key_second = jnp.tile(window[..., LAT + ROPE // 2 :], (1, 1, quads))
     key_positions = (lane - reach) * tokens + jnp.arange(key_rows, dtype=jnp.int32)
     apart = positions[:, None] - key_positions[None, :]
     reachable = (key_positions[None, :] >= 0) & (apart >= 0) & (apart < WINDOW)
@@ -277,13 +850,26 @@
             for m in range(MICRO)
         ]
     )
-    mixture, log_total = attention_forward(queries, keys, values, allowed, score_scale)
-    mixture = mixture.reshape(rows, H * VDIM)
+    bias = jnp.where(allowed, 0.0, NEGATIVE).astype(jnp.float32)
+    mixture = attention_forward(
+        tokens,
+        score_scale,
+        query_plain,
+        query_first,
+        query_second,
+        window_latent,
+        key_first,
+        key_second,
+        all_expand,
+        bias,
+    )
     residual = inputs + transposed_right(mixture, all_output)
     normed = low(root_normalize(residual, gain_second))
 
-    all_normed = gather_plane(normed).reshape(n_expert * rows, D)
-    all_cotangent = gather_plane(cotangent[0].reshape(rows, D)).reshape(n_expert * rows, D)
+    chunked = normed.reshape(CHUNKS, rows // CHUNKS, D)
+    (all_normed,) = gather([chunked], [CHUNK_ORDERS], False, 3)
+    all_normed = all_normed.reshape(n_expert * rows, D)
+    all_cotangent = gather_plane(sent_cotangent[0].reshape(rows, D)).reshape(n_expert * rows, D)
     all_routes = gather_plane(routes[0].reshape(rows, TOP))
     total_rows = n_expert * rows
     capacity = (9 * tokens * TOP + 8 * experts_count - 1) // (8 * experts_count)
@@ -299,7 +885,8 @@
     picked_bool = place == jnp.arange(slots, dtype=jnp.int32)[None, :, None]
     picked = picked_bool.astype(jnp.bfloat16)
     picked_float = picked_bool.astype(jnp.float32)
-    probabilities = jax.nn.softmax(dot(all_normed, all_router), axis=-1)
+    shared_pre = dot(all_normed, shared_in)
+    probabilities = jax.nn.softmax(shared_pre[:, mine : mine + experts_count], axis=-1)
     own_column = jnp.arange(experts_count, dtype=jnp.int32) == lane
     gate_rows = jnp.sum(jnp.where(own_column[None, :], probabilities, 0.0), axis=1)
     gate_slots = jnp.sum(
@@ -316,25 +903,17 @@
             )
         ).reshape(groups * slots, D)
 
-    def from_slots(x):
-        return jnp.einsum(
-            "gst,gsd->gtd",
-            picked,
-            x.reshape(groups, slots, D),
-            preferred_element_type=jnp.float32,
-        ).reshape(total_rows, D)
-
     arrived = to_slots(all_normed)
     gate_pre = dot(arrived, expert_gate)
     up_pre = dot(arrived, expert_up)
     expert_act = low(silu_product(gate_pre, up_pre))
     expert_out = low(dot(expert_act, expert_down))
-    shared_pre = dot(all_normed, shared_in)
-    shared_act = low(silu_product(shared_pre[:, :mine], shared_pre[:, mine:]))
-    partial_out = from_slots(low(gate_slots * expert_out.astype(jnp.float32))) + dot(
-        shared_act, shared_out_weight
-    )
-    expert_sum = scatter_plane(low(partial_out).reshape(n_expert, rows, D))
+    shared_act = low(silu_product(shared_pre[:, :padded], shared_pre[:, padded:]))
+    spread = jnp.swapaxes(picked, 1, 2)
+    partial_out = combine(
+        spread, low(gate_slots * expert_out.astype(jnp.float32)), shared_act, shared_out_weight
+    )
+    expert_sum = scatter_plane(partial_out.reshape(n_expert, rows, D))
     layer_output = low(residual + expert_sum.astype(jnp.float32))
 
     arrived_grad = to_slots(all_cotangent)
@@ -357,18 +936,29 @@
     )
     shared_back = jnp.concatenate(
         silu_back(
-            shared_pre[:, :mine],
-            shared_pre[:, mine:],
+            shared_pre[:, :padded],
+            shared_pre[:, padded:],
             transposed_right(all_cotangent, shared_out_weight),
         ),
         axis=1,
     ).astype(jnp.bfloat16)
-    partial_normed = from_slots(rows_grad) + transposed_right(shared_back, shared_in)
-    grad_normed = scatter_plane(low(partial_normed).reshape(n_expert, rows, D)).astype(
-        jnp.float32
-    )
-    shared_down_grad = scatter_dp(transposed_left(shared_act, all_cotangent), 0)
+    no_router = jnp.concatenate(
+        [
+            shared_in[:, :mine],
+            jnp.zeros((D, padded - mine), jnp.bfloat16),
+            shared_in[:, padded:],
+        ],
+        axis=1,
+    )
+    partial_normed = combine(spread, rows_grad, shared_back, no_router.T)
+    partial_normed = partial_normed.reshape(n_expert, CHUNKS, rows // CHUNKS, D)
+    (grad_normed,) = scatter([partial_normed], [CHUNK_ORDERS], False, 4)
+    grad_normed = grad_normed.reshape(rows, D)
+    shared_down_grad = scatter_dp(transposed_left(shared_act, all_cotangent)[:mine], 0)
     shared_in_grad = scatter_dp(transposed_left(all_normed, shared_back), 0)
+    shared_in_grad = jnp.concatenate(
+        [shared_in_grad[:, :mine], shared_in_grad[:, padded : padded + mine]], axis=1
+    )
     shared_in_grad = lax.all_to_all(
         low(shared_in_grad).reshape(n_expert, shard, 2 * mine),
         "expert",
@@ -398,42 +988,48 @@
 
     grad_attn = low(grad_residual)
     output_grad = transposed_left(grad_attn, mixture)
-    grad_mixture = low(dot(grad_attn, all_output)).reshape(MICRO, tokens, H, VDIM)
-    grad_queries, grad_keys, grad_values = attention_backward(
-        queries, keys, values, allowed, score_scale, log_total, grad_mixture
-    )
-    grad_queries = grad_queries.reshape(rows, H, head_width)
-    grad_expanded = low(
-        jnp.concatenate([grad_keys[..., :NOPE], grad_values], axis=-1)
-    ).reshape(MICRO * key_rows, H * (NOPE + VDIM))
-    expand_grad = transposed_left(window_latent, grad_expanded)
+    grad_mixture = low(dot(grad_attn, all_output))
+    grad_plain, grad_first, grad_second, grad_latents, grad_kfirst, grad_ksecond, expand_grad = (
+        attention_backward(
+            tokens,
+            score_scale,
+            query_plain,
+            query_first,
+            query_second,
+            grad_mixture,
+            window_latent,
+            key_first,
+            key_second,
+            all_expand,
+            jnp.swapaxes(bias, 1, 2),
+        )
+    )
+
+    def folded(x):
+        return jnp.sum(x.reshape(MICRO, key_rows, quads, ROPE // 2), axis=2)
+
     grad_window = jnp.concatenate(
-        [
-            transposed_right(grad_expanded, all_expand).reshape(MICRO, key_rows, LAT),
-            jnp.sum(grad_keys[..., NOPE:], axis=2),
-        ],
-        axis=-1,
+        [grad_latents, folded(grad_kfirst), folded(grad_ksecond)], axis=-1
     )
     grad_window = low(grad_window).reshape(MICRO, span, tokens, LAT + ROPE)
     grad_window = grad_window.transpose(1, 0, 2, 3).reshape(span, rows, LAT + ROPE)
     grad_line = lax.dynamic_update_slice_in_dim(
         jnp.zeros((n_expert + reach, rows, LAT + ROPE), jnp.bfloat16), grad_window, lane, 0
     )[reach:]
-    grad_line = scatter_plane(grad_line).astype(jnp.float32)
+    (grad_line,) = scatter([grad_line], [PLANE], False, 5)
     latent_part, latent_gain_grad = normalize_back(
         latent[:, :LAT], gain_latent, grad_line[:, :LAT]
     )
     grad_key_rope = rotate(grad_line[:, LAT:], cosine_rows, -sine_rows)
     grad_latent = low(jnp.concatenate([latent_part, grad_key_rope], axis=1))
     latent_grad = transposed_left(hidden, grad_latent)
-    grad_query = low(
-        jnp.concatenate(
-            [
-                grad_queries[..., :NOPE],
-                rotate(grad_queries[..., NOPE:], head_cosine, -head_sine),
-            ],
-            axis=-1,
-        ).reshape(rows, key_width)
+    grad_query = jnp.concatenate(
+        [
+            grad_plain,
+            low(grad_first * head_cosine + grad_second * head_sine),
+            low(grad_second * head_cosine - grad_first * head_sine),
+        ],
+        axis=1,
     )
     query_grad = transposed_left(hidden, grad_query)
     grad_hidden = transposed_right(grad_latent, all_latent) + transposed_right(
@@ -455,22 +1051,35 @@
     )[:, :, None]
     small_grad = jnp.concatenate([small_grad, latent_column], axis=2)
     small_grad = jnp.pad(small_grad, ((0, 0), (0, 0), (0, 128 - small_grad.shape[2])))
-    small_grad = scatter_all(small_grad)
-    query_grad = scatter_all(low(query_grad).reshape(devices, shard, key_width))
-    latent_grad = scatter_all(low(latent_grad).reshape(devices, shard, LAT + ROPE))
-    expand_grad = scatter_all(
-        low(expand_grad).reshape(devices, expand_weight.shape[0], expand_weight.shape[1])
-    )
-    output_grad = scatter_all(low(output_grad).reshape(devices, shard, H * VDIM))
+    query_grad, latent_grad, expand_grad, output_grad, small_grad = scatter(
+        [
+            low(query_grad).reshape(devices, shard, key_width),
+            low(latent_grad).reshape(devices, shard, LAT + ROPE),
+            expand_grad.reshape(devices, 16, -1),
+            low(output_grad).reshape(devices, shard, H * VDIM),
+            low(small_grad),
+        ],
+        ALL_ORDERS,
+        True,
+        6,
+    )
+    query_grad = jnp.concatenate(
+        [
+            query_grad[:, :plain].reshape(shard, H, NOPE),
+            query_grad[:, plain : plain + half].reshape(shard, H, ROPE // 2),
+            query_grad[:, plain + half :].reshape(shard, H, ROPE // 2),
+        ],
+        axis=2,
+    ).reshape(shard, key_width)
     return (
         layer_output.reshape(1, MICRO, tokens, D),
         input_grad.reshape(1, MICRO, tokens, D),
         small_grad[:, experts_count],
-        query_grad.astype(jnp.float32),
-        latent_grad.astype(jnp.float32),
+        query_grad,
+        latent_grad,
         small_grad[:small_latent, experts_count + 2],
-        expand_grad.astype(jnp.float32),
-        output_grad.astype(jnp.float32).T,
+        expand_grad.reshape(expand_weight.shape),
+        output_grad.T,
         small_grad[:, experts_count + 1],
         small_grad[:, :experts_count],
         shared_in_grad[0],

time: 2200 us -> 1480 us (0.67)
  waiting for transfers between devices: 1220 us -> 82 us
  Pallas kernels: 0 us -> 774 us
  matrix products: 486 us -> 275 us
  local copies, waits for them, and re-layouts: 241 us -> 146 us
  blocking collectives: 84.3 us -> 39.4 us
  other arithmetic: 116 us -> 93.7 us
    pallas_call x0 -> x10, Pallas kernels: none -> 774 us  [the longest x3 311 us: gather(): pl.pallas_call(functools.partial(gather_kernel, items, whole, sizes), out...]
    reduce_scatter x5 -> x0, waiting for transfers between devices: 413 us -> none  [scatter_all(): return lax.psum_scatter(x, BOTH, scatter_dimension=0, tiled=False)]
    reduce_scatter x3 -> x1, waiting for transfers between devices: 334 us -> 0.01 us  [scatter_plane(): return lax.psum_scatter(x, 'expert', scatter_dimension=0, tiled=False)]
    ppermute x5, waiting for transfers between devices: 154 us -> 15.6 us  [gather_dp(): other = lax.ppermute(x, 'dp', [(0, 1), (1, 0)])]
    dot_general x8 -> x0, matrix products: 114 us -> none  [the longest x2 39.7 us: from_slots(): jnp.einsum('gst,gsd->gtd', picked, x.reshape(groups, slots, D), preferred...]
    all_gather x4 -> x0, waiting for transfers between devices: 104 us -> none  [gather_all(): return lax.all_gather(x, BOTH, axis=0, tiled=False)]
    all_gather x3 -> x1, waiting for transfers between devices: 76 us -> 0.01 us  [gather_plane(): return lax.all_gather(x, 'expert', axis=0, tiled=False)]
    ppermute x5, waiting for transfers between devices: 129 us -> 56.3 us  [scatter_dp(): arrived = lax.ppermute(away, 'dp', [(0, 1), (1, 0)])]
  transfers between devices with their start and end apart: 28 -> 15, of which waited for: 16 -> 4; matrix products, arithmetic and copies ran while one was open for 21% -> 24% of each run, Pallas kernels for 0% -> 24%
where the time goes in v2:
time: 1480 us; the launch traced here: 1460 us
  Pallas kernels  774 us (52%)
  matrix products  275 us (19%)
  local copies, waits for them, and re-layouts  146 us (10%)
  other arithmetic  93.7 us (6%)
  waiting for transfers between devices  82 us (6%)
  blocking collectives  39.4 us (3%)
  starting transfers between devices  36.8 us (2%)
  between operations  15.7 us (1%)
    pallas_call x3, Pallas kernels, gather(): pl.pallas_call(functools.partial(gather_kernel, items, whole, sizes), out...  311 us
    pallas_call x3, Pallas kernels, scatter(): pl.pallas_call(functools.partial(scatter_kernel, items, whole, sizes), ou...  262 us
    pallas_call x1, Pallas kernels, attention_backward(): pl.pallas_call(functools.partial(attend_back_kernel, tokens, scale), grid...  110 us
    dot_general x8, matrix products, transposed_right(): lax.dot_general(left, right, (((1,), (1,)), ((), ())), preferred_element_...  89 us
    dot_general x9, matrix products, transposed_left(): lax.dot_general(left, right, (((0,), (0,)), ((), ())), preferred_element_...  85.4 us
    dot_general x7, matrix products, dot(): return jnp.dot(a, b, preferred_element_type=jnp.float32)  81.9 us
    ppermute x5, waiting for transfers between devices, scatter_dp(): arrived = lax.ppermute(away, 'dp', [(0, 1), (1, 0)])  56.3 us
    pallas_call x1, Pallas kernels, attention_forward(): pl.pallas_call(functools.partial(attend_kernel, tokens, scale), grid=(H,)...  51.4 us
  transfers between devices with their start and end apart: 15, of which 4 were waited for; matrix products, arithmetic and copies ran while one was open for 24% of the time, Pallas kernels for 24%

profile of v2, /device:TPU:0, one launch (start us, length us, event | category | flops | bytes accessed | tf_op | source)
XLA Modules:
  0.0 1462.6 jit_solution(13577519997656739869)
XLA Ops:
  12.8 117.5 %shard_map.297 = (bf16[32,64,3072]{2,1,0:T(8,128)(2,1)}, bf16[32,64,576]{2,1,0:T(8,128)(2,1)}, bf16[32,16,4096]{2,1,0:T(8,128)(2,1)}, bf16[32,64,2048]{2,1,0:T(8,128)(2,1)}, bf16[32,64,128]{2,1,0:T(8,128)(2,1)}) custom-call(bf16[64,3072]{1,0:T(8,128)(2,1)} %pad_maximum_fusion.17.refs_0_, bf16[64,576]{1,0:T(8,128)(2,1)} %refs_1_.1, bf16[16,4096]{1,0:T(8,128)(2,1)} %refs_2_.1, ...), custom_call_target="tpu_custom_call" | custom-call | bytes 168296448 | tf_op jit(solution)/shard_map/pallas_call | solution.py:272
  137.0 4.3 all-to-all-start
  144.7 39.4 %all_gather.6 = s32[16,256,6]{1,2,0:T(8,128)S(1)} all-gather(s32[1,256,6]{1,2,0:T(8,128)S(1)} %copy.258), channel_id=1, replica_groups=mesh['dp'=2,'expert'=16] {'expert'}, dimensions={0}, use_global_device_ids=true | all-gather | bytes 104448 | tf_op jit(solution)/shard_map/all_gather | solution.py:508
  196.8 8.8 fusion.93
  208.5 91.5 %shard_map.298 = bf16[16,256,576]{2,1,0:T(8,128)(2,1)} custom-call(bf16[256,576]{1,0:T(8,128)(2,1)} %pad_maximum_fusion.18.refs_0_), custom_call_target="tpu_custom_call" | custom-call | bytes 28311552 | tf_op jit(solution)/shard_map/pallas_call | solution.py:272
  300.1 3.1 pad_dynamic-slice_fusion
  303.2 7.1 copy.293
  310.3 7.1 copy.250
  319.3 3.3 fusion.86
  337.8 51.4 %shard_map.299 = bf16[256,2048]{1,0:T(8,128)(2,1)} custom-call(bf16[256,2048]{1,0:T(8,128)(2,1)} %slice.247.qn, bf16[256,512]{1,0:T(8,128)(2,1)} %get-tuple-element.182.qa, bf16[256,512]{1,0:T(8,128)(2,1)} %get-tuple-element.181.qb, bf16[2,1152,512]{2,1,0:T(8,128)(2,1)} %copy-done.14, bf16[2,1152,128]{2,1,0:T(8,128)(2,1)} %copy.255.ka, ...), custom_call_target="tpu_custom_call" | custom-call | flops 24999999488 | bytes 20000000 | tf_op jit(solution)/shard_map/pallas_call | solution.py:638
  389.3 6.2 multiply_reduce_fusion.2
  398.0 101.6 %shard_map.300 = bf16[16,4,64,2048]{3,2,1,0:T(8,128)(2,1)} custom-call(bf16[4,64,2048]{2,1,0:T(8,128)(2,1)} %bitcast.250), custom_call_target="tpu_custom_call" | custom-call | bytes 100663296 | tf_op jit(solution)/shard_map/pallas_call | solution.py:272
  499.7 11.1 convolution_convert_fusion.4
  516.8 15.6 %collective-permute-done = bf16[1024,352]{0,1:T(8,128)(2,1)S(1)} collective-permute-done((bf16[1024,352]{0,1:T(8,128)(2,1)S(1)}, bf16[1024,352]{0,1:T(8,128)(2,1)S(1)}, u32[]{:S(2)}, u32[]{:S(2)}) %collective-permute-start) | collective-permute-done | bytes 720928 | tf_op jit(solution)/shard_map/ppermute | solution.py:527
  533.0 11.7 fusion.95
  544.8 3.2 copy-done.10
  548.8 7.9 fusion.85
  556.6 5.6 copy.299
  562.2 5.6 copy.300
  570.4 4.7 broadcast_select_fusion.1
  575.2 4.1 broadcast_select_fusion.3
  579.3 3.4 broadcast_select_fusion.5
  583.3 14.0 fusion.15
  597.3 19.8 %multiply_convert_fusion.1 = (bf16[1792,1408]{1,0:T(8,128)(2,1)}, f32[1792,1408]{1,0:T(8,128)}) fusion(f32[1792,1408]{1,0:T(8,128)} %fusion.15, bf16[1792,2048]{1,0:T(8,128)(2,1)} %bitcast.232, bf16[1024,1408]{1,0:T(8,128)(2,1)} %get-tuple-element.180, bf16[1024,1408]{1,0:T(8,128)(2,1)S(1)} %get-tuple-element.179), kind=kOutput, calls=%fused_computation.13 | convolution fusion | flops 10361438208 | bytes 38338560 | tf_op jit(solution)/shard_map/dot_general | solution.py:520
  617.1 8.1 convolution_convert_fusion.3
  625.2 19.9 %fusion.2 = (f32[1792]{0:T(1024)S(1)}, bf16[1792,2048]{1,0:T(8,128)(2,1)}) fusion(bf16[16,112,2048]{2,1,0:T(8,128)(2,1)S(1)} %convolution_convert_fusion.3, bf16[1792,1408]{1,0:T(8,128)(2,1)} %get-tuple-element.217, bf16[1408,1024]{1,0:T(8,128)(2,1)} %get-tuple-element.176, bf16[1408,1024]{1,0:T(8,128)(2,1)} %get-tuple-element.175), kind=kOutput, calls=%fused_computation.6 | convolution fusion | flops 10364647424 | bytes 25500672 | tf_op jit(solution)/shard_map/dot_general | solution.py:520
  646.2 13.8 fusion.1
  660.1 11.3 fusion.9
  671.3 18.3 %shard_map.301 = bf16[4096,2048]{1,0:T(8,128)(2,1)} custom-call(bf16[16,256,112]{2,1,0:T(8,128)(2,1)S(1)} %copy-done, bf16[16,112,2048]{2,1,0:T(8,128)(2,1)} %bitcast.229, bf16[4096,256]{1,0:T(8,128)(2,1)S(1)} %get-tuple-element.172.left, bf16[256,2048]{1,0:T(8,128)(2,1)S(1)} %fusion.34.right), custom_call_target="tpu_custom_call" | custom-call | flops 6174015488 | bytes 33554432 | tf_op jit(solution)/shard_map/pallas_call | solution.py:691
  689.7 9.3 fusion.20
  702.4 13.1 fusion.82
  719.9 3.7 all-to-all-start.1
  723.6 15.1 %fusion.98 = f32[1408,2048]{1,0:T(8,128)S(1)} fusion(bf16[1792,1408]{1,0:T(8,128)(2,1)} %get-tuple-element.217, bf16[1792,2048]{1,0:T(8,128)(2,1)} %get-tuple-element.209), kind=kOutput, calls=%fused_computation.240 | convolution fusion | flops 10334765056 | bytes 23920640 | tf_op jit(solution)/shard_map/dot_general | solution.py:72
  740.8 4.2 copy-done.17
  749.2 24.4 %fusion.5 = (bf16[1792,1408]{1,0:T(8,128)(2,1)}, bf16[1792,1408]{1,0:T(8,128)(2,1)}) fusion(f32[1792,1408]{1,0:T(8,128)} %fusion.15, f32[1792,1408]{1,0:T(8,128)} %get-tuple-element.218, bf16[1792,2048]{1,0:T(8,128)(2,1)} %get-tuple-element.209, bf16[1408,1024]{1,0:T(8,128)(2,1)} %get-tuple-element.176, bf16[1408,1024]{1,0:T(8,128)(2,1)S(1)} %copy-done.31), kind=kOutput, calls=%fused_computation.11 | convolution fusion | flops 10381623296 | bytes 43384832 | tf_op jit(solution)/shard_map/dot_general | solution.py:78
  773.7 16.3 %fusion.96 = f32[2048,1408]{1,0:T(8,128)} fusion(bf16[1792,2048]{1,0:T(8,128)(2,1)S(1)} %bitcast.238, bf16[1792,1408]{1,0:T(8,128)(2,1)} %get-tuple-element.168), kind=kOutput, calls=%fused_computation.238 | convolution fusion | flops 10334765056 | bytes 23920640 | tf_op jit(solution)/shard_map/dot_general | solution.py:72
  790.0 14.7 %fusion.97 = f32[2048,1408]{1,0:T(8,128)} fusion(bf16[1792,2048]{1,0:T(8,128)(2,1)S(1)} %bitcast.239, bf16[1792,1408]{1,0:T(8,128)(2,1)S(1)} %copy-done.86), kind=kOutput, calls=%fused_computation.239 | convolution fusion | flops 10334765056 | bytes 23920640 | tf_op jit(solution)/shard_map/dot_general | solution.py:72
  804.7 14.3 fusion.13
  819.0 19.7 %add_convert_fusion = bf16[1792,2048]{1,0:T(8,128)(2,1)} fusion(f32[1792,2048]{1,0:T(8,128)} %fusion.13, bf16[1792,1408]{1,0:T(8,128)(2,1)} %get-tuple-element.168, bf16[1024,1408]{1,0:T(8,128)(2,1)} %copy-done.33, bf16[1024,1408]{1,0:T(8,128)(2,1)} %copy-done.32), kind=kOutput, calls=%fused_computation.7 | convolution fusion | flops 10353639424 | bytes 32833536 | tf_op jit(solution)/shard_map/dot_general | solution.py:78
  838.7 21.7 %shard_map.302 = bf16[4096,2048]{1,0:T(8,128)(2,1)} custom-call(bf16[16,256,112]{2,1,0:T(8,128)(2,1)S(1)} %copy-done.1, bf16[16,112,2048]{2,1,0:T(8,128)(2,1)} %bitcast.300, bf16[4096,512]{1,0:T(8,128)(2,1)} %pad_maximum_fusion.3.left, bf16[512,2048]{1,0:T(8,128)(2,1)S(1)} %copy-done.2), custom_call_target="tpu_custom_call" | custom-call | flops 10468982784 | bytes 33554432 | tf_op jit(solution)/shard_map/pallas_call | solution.py:691
  860.4 4.5 dynamic-slice_convert_fusion.2
  864.9 90.6 %shard_map.303 = f32[4,64,2048]{2,1,0:T(8,128)} custom-call(bf16[16,4,64,2048]{3,2,1,0:T(8,128)(2,1)} %bitcast.231), custom_call_target="tpu_custom_call" | custom-call | tf_op jit(solution)/shard_map/pallas_call | solution.py:481
  956.9 4.5 dynamic-slice_convert_fusion.1
  969.5 16.5 %all-to-all-start.2 = ((bf16[16,64,352]{2,1,0:T(8,128)(2,1)}), bf16[16,64,352]{2,1,0:T(8,128)(2,1)S(1)}, u32[]{:S(2)}, u32[]{:S(2)}) async-start(bf16[16,64,352]{2,1,0:T(8,128)(2,1)} %pad_maximum_fusion.13), calls=%async_computation.3 | async-start | bytes 1572864 | tf_op jit(solution)/shard_map/all_to_all | solution.py:962
  986.8 3.8 multiply_reduce_fusion
  994.6 10.1 all-to-all-done.2
  1012.0 7.7 add_bitcast_fusion
  1021.2 6.6 add_bitcast_fusion.2
  1027.8 54.7 %collective-permute-done.8 = bf16[1024,1408]{1,0:T(8,128)(2,1)} collective-permute-done((bf16[1024,1408]{1,0:T(8,128)(2,1)}, bf16[1024,1408]{1,0:T(8,128)(2,1)}, u32[]{:S(2)}, u32[]{:S(2)}) %collective-permute-start.8) | collective-permute-done | bytes 2883616 | tf_op jit(solution)/shard_map/ppermute | solution.py:543
  1082.5 4.8 add_bitcast_fusion.1
  1087.3 4.1 fusion.16
  1091.5 6.8 convolution_convert_fusion.6.grad
  1098.2 109.7 %shard_map.304 = (bf16[256,2048]{1,0:T(8,128)(2,1)}, f32[256,512]{1,0:T(8,128)}, f32[256,512]{1,0:T(8,128)}, f32[2,1152,512]{2,1,0:T(8,128)}, f32[2,1152,128]{2,...) custom-call(bf16[256,2048]{1,0:T(8,128)(2,1)} %slice.247.qn, bf16[256,512]{1,0:T(8,128)(2,1)} %get-tuple-element.182.qa, ...), custom_call_target="tpu_custom_call" | custom-call | flops 49999998976 | bytes 30000000 | tf_op jit(solution)/shard_map/pallas_call | solution.py:658
  1207.9 4.0 convert.80
  1217.0 2.8 pad_maximum_fusion.10
  1221.3 2.8 slice.195.refs_0_
  1224.2 51.4 %shard_map.305 = f32[256,576]{1,0:T(8,128)} custom-call(bf16[16,256,576]{2,1,0:T(8,128)(2,1)} %slice.195.refs_0_), custom_call_target="tpu_custom_call" | custom-call | tf_op jit(solution)/shard_map/pallas_call | solution.py:481
  1278.0 7.0 convolution_convert_fusion.1
  1285.3 6.6 fusion.38
  1291.9 6.7 convolution_convert_fusion
  1301.4 2.7 fusion.28
  1307.4 4.3 copy.280
  1311.7 120.0 %shard_map.306 = (f32[64,3072]{1,0:T(8,128)}, f32[64,576]{1,0:T(8,128)}, f32[16,4096]{1,0:T(8,128)}, f32[64,2048]{1,0:T(8,128)}, f32[64,128]{1,0:T(8,128)}) custom-call(bf16[32,64,3072]{2,1,0:T(8,128)(2,1)} %bitcast.227, bf16[32,64,576]{2,1,0:T(8,128)(2,1)} %bitcast.245, bf16[32,16,4096]{2,1,0:T(8,128)(2,1)} %bitcast.257, bf16[32,64,2048]{2,1,0:T(8,128)(2,1)} %bitcast.228, ...), custom_call_target="tpu_custom_call" | custom-call | tf_op jit(solution)/shard_map/pallas_call | solution.py:481
  1449.9 3.5 fusion.17
  (370 shorter events, 134.8 us)
Async XLA Ops:
  7.2 609.9 %all-gather.2.cloned.1.call-start = ((), (), s32[]{:S(2)}) async-start(), calls=%async_computation.5 | async-start | bytes 17825792 | tf_op jit(solution)/shard_map/all_gather | solution.py:508
  8.8 122.7 %copy-start.53 = (bf16[64,2816]{1,0:T(8,128)(2,1)S(1)}, bf16[64,2816]{1,0:T(8,128)(2,1)}, u32[]{:S(2)}) copy-start(bf16[64,2816]{1,0:T(8,128)(2,1)} %param.30) | copy-start | bytes 1081348
  8.9 124.0 %copy-start.54 = (bf16[64,2816]{1,0:T(8,128)(2,1)S(1)}, bf16[64,2816]{1,0:T(8,128)(2,1)}, u32[]{:S(2)}) copy-start(bf16[64,2816]{1,0:T(8,128)(2,1)} %param.31) | copy-start | bytes 1081348
  130.4 385.2 %collective-permute-start.4 = (bf16[88,2048]{1,0:T(8,128)(2,1)}, bf16[88,2048]{1,0:T(8,128)(2,1)}, u32[]{:S(2)}, u32[]{:S(2)}) collective-permute-start(bf16[88,2048]{1,0:T(8,128)(2,1)} %param.32), channel_id=1, source_target_pairs={{0,16},{16,0},{1,17},{17,1},{2,18},{18,2},{3,19},{19,3},{4,20},{20... | collective-permute-start | bytes 1081352 | tf_op jit(solution)/shard_map/ppermute | solution.py:527
  134.4 9.9 copy-start.85
  134.4 10.3 copy-start.82
  137.0 375.5 %all-to-all-start = ((bf16[16,64,352]{2,1,0:T(8,128)(2,1)}), bf16[16,64,352]{2,1,0:T(8,128)(2,1)}, u32[]{:S(2)}, u32[]{:S(2)}) async-start(bf16[16,64,352]{2,1,0:T(8,128)(2,1)} %reshape.737), calls=%async_computation | async-start | bytes 1572864 | tf_op jit(solution)/shard_map/all_to_all | solution.py:790
  141.3 946.0 %reduce-scatter.2.cloned.1.call-start = ((), (), s32[]{:S(2)}) async-start(), calls=%async_computation.4 | async-start | bytes 17825792 | tf_op jit(solution)/shard_map/reduce_scatter | solution.py:512
  141.4 428.1 %collective-permute-start.3 = (bf16[1408,1024]{1,0:T(8,128)(2,1)}, bf16[1408,1024]{1,0:T(8,128)(2,1)}, u32[]{:S(2)}, u32[]{:S(2)}) collective-permute-start(bf16[1408,1024]{1,0:T(8,128)(2,1)} %bitcast.259), channel_id=1, source_target_pairs={{0,16},{16,0},{1,17},{17,1},{2,18},{18,2},{3,19},{19,3},{4,20},{20... | collective-permute-start | bytes 8650760 | tf_op jit(solution)/shard_map/ppermute | solution.py:527
  142.3 432.9 %collective-permute-start.2 = (bf16[1024,1408]{1,0:T(8,128)(2,1)}, bf16[1024,1408]{1,0:T(8,128)(2,1)}, u32[]{:S(2)}, u32[]{:S(2)}) collective-permute-start(bf16[1024,1408]{1,0:T(8,128)(2,1)} %bitcast.260), channel_id=1, source_target_pairs={{0,16},{16,0},{1,17},{17,1},{2,18},{18,2},{3,19},{19,3},{4,20},{20... | collective-permute-start | bytes 8650760 | tf_op jit(solution)/shard_map/ppermute | solution.py:527
  143.5 435.8 %collective-permute-start.1 = (bf16[1024,1408]{1,0:T(8,128)(2,1)}, bf16[1024,1408]{1,0:T(8,128)(2,1)}, u32[]{:S(2)}, u32[]{:S(2)}) collective-permute-start(bf16[1024,1408]{1,0:T(8,128)(2,1)} %bitcast.261), channel_id=1, source_target_pairs={{0,16},{16,0},{1,17},{17,1},{2,18},{18,2},{3,19},{19,3},{4,20},{20... | collective-permute-start | bytes 8650760 | tf_op jit(solution)/shard_map/ppermute | solution.py:527
  186.0 10.3 copy-start.46
  186.0 10.3 copy-start.48
  192.7 14.4 copy-start.67
  196.3 10.8 copy-start.15
  196.5 9.2 copy-start.70
  207.1 93.0 %copy-start.80 = (f32[256]{0:T(256)}, f32[256]{0:T(256)S(1)}, u32[]{:S(2)}) copy-start(f32[256]{0:T(256)S(1)} %multiply_reduce_fusion.5) | copy-start | bytes 3076
  207.1 92.9 %copy-start.73 = (f32[256]{0:T(256)}, f32[256]{0:T(256)S(1)}, u32[]{:S(2)}) copy-start(f32[256]{0:T(256)S(1)} %fusion.65) | copy-start | bytes 3076
  319.3 13.4 copy-start.14
  398.0 101.7 %copy-start.64 = (s32[16,256]{1,0:T(8,128)S(1)}, s32[16,256]{1,0:T(8,128)}, u32[]{:S(2)}) copy-start(s32[16,256]{1,0:T(8,128)} %reduce_window_sum.25) | copy-start | bytes 49156
  398.0 101.7 %copy-start.66 = (pred[16,256]{1,0:T(8,128)(4,1)S(1)}, pred[16,256]{1,0:T(8,128)(4,1)}, u32[]{:S(2)}) copy-start(pred[16,256]{1,0:T(8,128)(4,1)} %copy-done.65) | copy-start | bytes 12292
  513.9 18.6 %collective-permute-start = (bf16[1024,352]{0,1:T(8,128)(2,1)S(1)}, bf16[1024,352]{0,1:T(8,128)(2,1)S(1)}, u32[]{:S(2)}, u32[]{:S(2)}) collective-permute-start(bf16[1024,352]{0,1:T(8,128)(2,1)S(1)} %copy.261), channel_id=1, source_target_pairs={{0,16},{16,0},{1,17},{17,1},{2,18},{18,2},{3,19},{19,3},{4,20},{20... | collective-permute-start | bytes 2162696 | tf_op jit(solution)/shard_map/ppermute | solution.py:527
  516.7 16.0 %copy-start.42 = (bf16[88,2048]{1,0:T(8,128)(2,1)}, bf16[88,2048]{1,0:T(8,128)(2,1)S(1)}, u32[]{:S(2)}) copy-start(bf16[88,2048]{1,0:T(8,128)(2,1)S(1)} %get-tuple-element.202) | copy-start | bytes 1081348
  516.8 15.9 %copy-start.55 = (bf16[2048,16]{0,1:T(8,128)(2,1)S(1)}, bf16[2048,16]{0,1:T(8,128)(2,1)}, u32[]{:S(2)}) copy-start(bf16[2048,16]{0,1:T(8,128)(2,1)} %copy.298) | copy-start | bytes 196612
  579.3 18.0 %copy-start.28 = (bf16[1024,1408]{1,0:T(8,128)(2,1)}, bf16[1024,1408]{1,0:T(8,128)(2,1)S(1)}, u32[]{:S(2)}) copy-start(bf16[1024,1408]{1,0:T(8,128)(2,1)S(1)} %get-tuple-element.179) | copy-start | bytes 8650756
  582.7 14.6 copy-start.32
  582.7 14.5 copy-start.33
  625.2 19.9 %copy-start.3 = (bf16[16,112,2048]{2,1,0:T(8,128)(2,1)}, bf16[16,112,2048]{2,1,0:T(8,128)(2,1)S(1)}, u32[]{:S(2)}) copy-start(bf16[16,112,2048]{2,1,0:T(8,128)(2,1)S(1)} %convolution_convert_fusion.3) | copy-start | bytes 22020100
  646.2 13.9 copy-start.23
  646.2 13.9 copy-start.24
  646.2 13.9 copy-start.43
  660.0 11.3 copy-start
  689.7 12.7 copy-start.38
  689.7 12.7 copy-start.40
  700.9 291.5 %collective-permute-start.6 = (bf16[88,2048]{1,0:T(8,128)(2,1)}, bf16[88,2048]{1,0:T(8,128)(2,1)}, u32[]{:S(2)}, u32[]{:S(2)}) collective-permute-start(bf16[88,2048]{1,0:T(8,128)(2,1)} %dynamic-slice_convert_fusion.4), channel_id=1, source_target_pairs={{0,16},{16,0},{1,17},{17,1},{2,18},{18,2},{3,19},{19,3},{4,20},{20... | collective-permute-start | bytes 1081352 | tf_op jit(solution)/shard_map/ppermute | solution.py:543
  718.7 243.8 %collective-permute-start.5 = (bf16[1024,512]{0,1:T(8,128)(2,1)}, bf16[1024,512]{0,1:T(8,128)(2,1)}, u32[]{:S(2)}, u32[]{:S(2)}) collective-permute-start(bf16[1024,512]{0,1:T(8,128)(2,1)} %dynamic-slice_convert_fusion.3), channel_id=1, source_target_pairs={{0,16},{16,0},{1,17},{17,1},{2,18},{18,2},{3,19},{19,3},{4,20},{20... | collective-permute-start | bytes 3145736 | tf_op jit(solution)/shard_map/ppermute | solution.py:543
  719.9 249.6 %all-to-all-start.1 = ((f32[16,1,256]{2,1,0:T(1,128)}), f32[16,1,256]{2,1,0:T(1,128)S(1)}, u32[]{:S(2)}, u32[]{:S(2)}) async-start(f32[16,1,256]{2,1,0:T(1,128)} %all_to_all.15), calls=%async_computation.2 | async-start | bytes 32768 | tf_op jit(solution)/shard_map/all_to_all | solution.py:924
  745.0 267.0 %collective-permute-start.9 = (bf16[1408,1024]{1,0:T(8,128)(2,1)}, bf16[1408,1024]{1,0:T(8,128)(2,1)}, u32[]{:S(2)}, u32[]{:S(2)}) collective-permute-start(bf16[1408,1024]{1,0:T(8,128)(2,1)} %dynamic-slice_convert_fusion), channel_id=1, source_target_pairs={{0,16},{16,0},{1,17},{17,1},{2,18},{18,2},{3,19},{19,3},{4,20},{20... | collective-permute-start | bytes 8650760 | tf_op jit(solution)/shard_map/ppermute | solution.py:543
  746.7 26.9 %slice-start.2 = ((s8[7340032]{0:T(1024)(128)(4,1)}), s8[4194304]{0:T(1024)(128)(4,1)S(1)}, s32[]{:S(2)}) async-start(s8[7340032]{0:T(1024)(128)(4,1)} %bitcast.236), calls=%async_computation.8 | async-start | bytes 8388608
  749.2 24.4 %slice-start.3 = ((s8[7340032]{0:T(1024)(128)(4,1)}), s8[3145728]{0:T(1024)(128)(4,1)S(1)}, s32[]{:S(2)}) async-start(s8[7340032]{0:T(1024)(128)(4,1)} %bitcast.236), calls=%async_computation.9 | async-start | bytes 6291456
  773.7 16.3 %copy-start.86 = (bf16[1792,1408]{1,0:T(8,128)(2,1)S(1)}, bf16[1792,1408]{1,0:T(8,128)(2,1)}, u32[]{:S(2)}) copy-start(bf16[1792,1408]{1,0:T(8,128)(2,1)} %get-tuple-element.169) | copy-start | bytes 15138820
  790.0 14.7 %copy-start.29 = (bf16[1024,1408]{1,0:T(8,128)(2,1)S(1)}, bf16[1024,1408]{1,0:T(8,128)(2,1)}, u32[]{:S(2)}) copy-start(bf16[1024,1408]{1,0:T(8,128)(2,1)} %copy-done.28) | copy-start | bytes 8650756
  790.0 14.7 %copy-start.30 = (bf16[1024,1408]{1,0:T(8,128)(2,1)S(1)}, bf16[1024,1408]{1,0:T(8,128)(2,1)}, u32[]{:S(2)}) copy-start(bf16[1024,1408]{1,0:T(8,128)(2,1)} %get-tuple-element.180) | copy-start | bytes 8650756
  819.0 19.7 %copy-start.1 = (bf16[16,256,112]{2,1,0:T(8,128)(2,1)S(1)}, bf16[16,256,112]{2,1,0:T(8,128)(2,1)}, u32[]{:S(2)}) copy-start(bf16[16,256,112]{2,1,0:T(8,128)(2,1)} %fusion.33.picked) | copy-start | bytes 2752516
  819.0 19.7 %copy-start.2 = (bf16[512,2048]{1,0:T(8,128)(2,1)S(1)}, bf16[512,2048]{1,0:T(8,128)(2,1)}, u32[]{:S(2)}) copy-start(bf16[512,2048]{1,0:T(8,128)(2,1)} %fusion.19.right) | copy-start | bytes 6291460
  955.5 65.7 %collective-permute-start.7 = (bf16[1024,1408]{1,0:T(8,128)(2,1)}, bf16[1024,1408]{1,0:T(8,128)(2,1)}, u32[]{:S(2)}, u32[]{:S(2)}) collective-permute-start(bf16[1024,1408]{1,0:T(8,128)(2,1)} %dynamic-slice_convert_fusion.2), channel_id=1, source_target_pairs={{0,16},{16,0},{1,17},{17,1},{2,18},{18,2},{3,19},{19,3},{4,20},{20... | collective-permute-start | bytes 8650760 | tf_op jit(solution)/shard_map/ppermute | solution.py:543
  961.4 121.0 %collective-permute-start.8 = (bf16[1024,1408]{1,0:T(8,128)(2,1)}, bf16[1024,1408]{1,0:T(8,128)(2,1)}, u32[]{:S(2)}, u32[]{:S(2)}) collective-permute-start(bf16[1024,1408]{1,0:T(8,128)(2,1)} %dynamic-slice_convert_fusion.1), channel_id=1, source_target_pairs={{0,16},{16,0},{1,17},{17,1},{2,18},{18,2},{3,19},{19,3},{4,20},{20... | collective-permute-start | bytes 8650760 | tf_op jit(solution)/shard_map/ppermute | solution.py:543
  964.1 22.6 %copy-start.7 = (f32[256,2048]{1,0:T(8,128)S(1)}, f32[256,2048]{1,0:T(8,128)}, u32[]{:S(2)}) copy-start(f32[256,2048]{1,0:T(8,128)} %copy-done.6) | copy-start | bytes 6291460
  964.2 22.6 %copy-start.12 = (bf16[32,64,128]{2,1,0:T(8,128)(2,1)S(1)}, bf16[32,64,128]{2,1,0:T(8,128)(2,1)}, u32[]{:S(2)}) copy-start(bf16[32,64,128]{2,1,0:T(8,128)(2,1)} %get-tuple-element.41) | copy-start | bytes 1572868
  964.2 22.6 %copy-start.62 = (f32[2048]{0:T(1024)S(1)}, f32[2048]{0:T(1024)}, u32[]{:S(2)}) copy-start(f32[2048]{0:T(1024)} %get-tuple-element.152) | copy-start | bytes 24580
  964.2 22.6 %copy-start.76 = (f32[256]{0:T(256)S(1)}, f32[256]{0:T(256)}, u32[]{:S(2)}) copy-start(f32[256]{0:T(256)} %copy-done.75) | copy-start | bytes 3076
  969.5 35.2 %all-to-all-start.2 = ((bf16[16,64,352]{2,1,0:T(8,128)(2,1)}), bf16[16,64,352]{2,1,0:T(8,128)(2,1)S(1)}, u32[]{:S(2)}, u32[]{:S(2)}) async-start(bf16[16,64,352]{2,1,0:T(8,128)(2,1)} %pad_maximum_fusion.13), calls=%async_computation.3 | async-start | bytes 1572864 | tf_op jit(solution)/shard_map/all_to_all | solution.py:962
  1011.9 70.5 %slice-start.4 = ((s8[11534336]{0:T(1024)(128)(4,1)}), s8[4194304]{0:T(1024)(128)(4,1)S(1)}, s32[]{:S(2)}) async-start(s8[11534336]{0:T(1024)(128)(4,1)} %bitcast.253), calls=%async_computation.10 | async-start | bytes 8388608
  1012.0 70.5 %slice-start.5 = ((s8[11534336]{0:T(1024)(128)(4,1)}), s8[4194304]{0:T(1024)(128)(4,1)S(1)}, s32[]{:S(2)}) async-start(s8[11534336]{0:T(1024)(128)(4,1)} %bitcast.253), calls=%async_computation.11 | async-start | bytes 8388608
  1019.6 62.8 %slice-start.6 = ((s8[11534336]{0:T(1024)(128)(4,1)}), s8[3145728]{0:T(1024)(128)(4,1)S(1)}, s32[]{:S(2)}) async-start(s8[11534336]{0:T(1024)(128)(4,1)} %bitcast.253), calls=%async_computation.12 | async-start | bytes 6291456
  1027.8 59.5 %copy-start.22 = (bf16[1,2,128,2048]{3,2,1,0:T(8,128)(2,1)S(1)}, bf16[1,2,128,2048]{3,2,1,0:T(8,128)(2,1)}, u32[]{:S(2)}) copy-start(bf16[1,2,128,2048]{3,2,1,0:T(8,128)(2,1)} %param.19) | copy-start | bytes 3145732
  1027.8 59.5 %copy-start.63 = (f32[2048]{0:T(1024)S(1)}, f32[2048]{0:T(1024)}, u32[]{:S(2)}) copy-start(f32[2048]{0:T(1024)} %get-tuple-element.152) | copy-start | bytes 24580
  1027.8 59.5 %copy-start.77 = (f32[256]{0:T(256)S(1)}, f32[256]{0:T(256)}, u32[]{:S(2)}) copy-start(f32[256]{0:T(256)} %copy-done.75) | copy-start | bytes 3076
  1224.2 51.5 %copy-start.47 = (f32[128,32]{1,0:T(8,128)S(1)}, f32[128,32]{1,0:T(8,128)}, u32[]{:S(2)}) copy-start(f32[128,32]{1,0:T(8,128)} %copy-done.46) | copy-start | bytes 49156
  1224.2 51.5 %copy-start.49 = (f32[128,32]{1,0:T(8,128)S(1)}, f32[128,32]{1,0:T(8,128)}, u32[]{:S(2)}) copy-start(f32[128,32]{1,0:T(8,128)} %copy-done.48) | copy-start | bytes 49156
  1224.2 52.6 %copy-start.16 = (f32[256,576]{1,0:T(8,128)S(1)}, f32[256,576]{1,0:T(8,128)}, u32[]{:S(2)}) copy-start(f32[256,576]{1,0:T(8,128)} %copy-done.15) | copy-start | bytes 1769476
  1224.2 52.6 %copy-start.68 = (f32[512]{0:T(512)S(1)}, f32[512]{0:T(512)}, u32[]{:S(2)}) copy-start(f32[512]{0:T(512)} %copy-done.67) | copy-start | bytes 6148
  1224.2 52.6 %copy-start.74 = (f32[256]{0:T(256)S(1)}, f32[256]{0:T(256)}, u32[]{:S(2)}) copy-start(f32[256]{0:T(256)} %copy-done.73) | copy-start | bytes 3076
  1311.7 126.5 %copy-start.79 = (f32[2,128]{1,0:T(2,128)S(1)}, f32[2,128]{1,0:T(2,128)}, u32[]{:S(2)}) copy-start(f32[2,128]{1,0:T(2,128)} %copy-done.78) | copy-start | bytes 3076
  (45 other events, 209.5 us)
Sparse Core Ops, SparseCore 0:
  130.5 160.8 all-gather.1
  689.8 176.2 reduce-scatter.1

commit v3 on v2

--- a/solution.py
+++ b/solution.py
@@ -109,9 +109,9 @@
     return (at["x"], expert_of(sizes, at))
 
 
-def slot_of(sizes, at, whole):
+def slot_of(sizes, at, order):
     e = expert_of(sizes, at)
-    if whole:
+    if "x" in order:
         return at["x"] * (sizes["z"] * sizes["y"] * sizes["c"]) + e
     return e
 
@@ -188,7 +188,7 @@
     return total
 
 
-def gather_kernel(items, whole, sizes, *refs):
+def gather_kernel(items, sizes, *refs):
     arrays = items[-1][0] + 1
     count = len(items)
     orders = [order for _, _, order in items]
@@ -200,9 +200,9 @@
     at = place_of(sizes)
     names = sorted({d for order in orders for d in order})
     greet(names, sizes, at)
-    me = slot_of(sizes, at, whole)
     keep = []
     for a in range(count):
+        me = slot_of(sizes, at, orders[a])
         own = pltpu.make_async_copy(ins[a], outs[a](me), own_sem.at[a])
         own.start()
         keep.append(own)
@@ -219,7 +219,7 @@
         where = dict(at)
         for d, k in zip(order, ks):
             where[d] = nearest(at[d], k, sizes[d])
-        slot = slot_of(sizes, where, whole)
+        slot = slot_of(sizes, where, order)
         here = outs[a](slot)
         if any(ks):
             pltpu.make_async_copy(here, here, recvs[a].at[slot]).wait()
@@ -264,19 +264,23 @@
     return items
 
 
-def gather(arrays, orders, whole, identity):
+def members(sizes, order):
+    return math.prod(sizes[d] for d in order)
+
+
+def gather(arrays, orders, identity):
     sizes = dims_of()
-    total = (sizes["x"] if whole else 1) * lax.axis_size("expert")
     items = items_of(orders, [a.shape for a in arrays])
-    sent = total * sum(a.size * a.dtype.itemsize for a in arrays)
+    totals = {a: members(sizes, order) for a, _, order in items}
+    sent = sum(totals[i] * a.size * a.dtype.itemsize for i, a in enumerate(arrays))
     return pl.pallas_call(
-        functools.partial(gather_kernel, items, whole, sizes),
-        out_shape=[jax.ShapeDtypeStruct((total,) + a.shape, a.dtype) for a in arrays],
+        functools.partial(gather_kernel, items, sizes),
+        out_shape=[jax.ShapeDtypeStruct((totals[i],) + a.shape, a.dtype) for i, a in enumerate(arrays)],
         in_specs=[ANYWHERE] * len(arrays),
         out_specs=[ANYWHERE] * len(arrays),
         scratch_shapes=[pltpu.SemaphoreType.DMA((len(items),))]
         + [pltpu.SemaphoreType.DMA((count_sends(order, sizes),)) for _, _, order in items]
-        + [pltpu.SemaphoreType.DMA((total,)) for _ in items],
+        + [pltpu.SemaphoreType.DMA((totals[a],)) for a, _, _ in items],
         compiler_params=pltpu.CompilerParams(collective_id=identity, has_side_effects=True),
         cost_estimate=pl.CostEstimate(flops=0, bytes_accessed=sent * 6, transcendentals=0),
     )(*arrays)
@@ -327,7 +331,7 @@
     lax.fori_loop(0, rows // step, one, 0)
 
 
-def scatter_kernel(items, whole, sizes, *refs):
+def scatter_kernel(items, sizes, *refs):
     arrays = items[-1][0] + 1
     count = len(items)
     orders = [order for _, _, order in items]
@@ -351,7 +355,7 @@
         where = dict(at)
         for d, k in zip(order, ks):
             where[d] = nearest(at[d], k, sizes[d])
-        slots[a, ks] = (where, slot_of(sizes, where, whole))
+        slots[a, ks] = (where, slot_of(sizes, where, order))
     for _, _, a, ks in plan:
         if ks[-1] == 0:
             where, slot = slots[a, ks]
@@ -470,7 +474,7 @@
     return total
 
 
-def scatter(arrays, orders, whole, identity, out_dtype=jnp.float32):
+def scatter(arrays, orders, identity, out_dtype=jnp.float32):
     sizes = dims_of()
     items = items_of(orders, [a.shape[1:] for a in arrays])
     shapes = [arrays[a].shape[-2:] for a, _, _ in items]
@@ -479,7 +483,7 @@
     stages = [math.prod(sizes[d] for d in order[:-1]) for order in orders]
     landing = [boxes(order, sizes) for order in orders]
     return pl.pallas_call(
-        functools.partial(scatter_kernel, items, whole, sizes),
+        functools.partial(scatter_kernel, items, sizes),
         out_shape=[jax.ShapeDtypeStruct(a.shape[1:], out_dtype) for a in arrays],
         in_specs=[ANYWHERE] * len(arrays),
         out_specs=[pl.BlockSpec(memory_space=pltpu.VMEM)] * len(arrays),
@@ -501,7 +505,8 @@
 YZ = ("y", "z", "c")
 CHUNKS = 4
 CHUNK_ORDERS = [PLANE, PLANE, PLANE, YZ]
-ALL_ORDERS = [ZYX, XYZ, XYZ, ZXY, XYZ]
+YZX = ("y", "z", "x", "c")
+ALL_ORDERS = [[ZYX, ZXY], YZX, XYZ, XYZ]
 
 
 def gather_plane(x):
@@ -516,77 +521,134 @@
     return x.astype(jnp.bfloat16)
 
 
+def wide(x):
+    return x.astype(jnp.float32)
+
+
 def dot(a, b):
     return jnp.dot(a, b, preferred_element_type=jnp.float32)
 
 
-def gather_dp(x, axis):
-    size = lax.axis_size("dp")
-    if size != 2:
-        return lax.all_gather(x, "dp", axis=axis, tiled=True)
-    other = lax.ppermute(x, "dp", [(0, 1), (1, 0)])
+def fetch_dp(x, axis):
+    if lax.axis_size("dp") != 2:
+        return x, lax.all_gather(x, "dp", axis=axis, tiled=True)
+    return x, lax.ppermute(x, "dp", [(0, 1), (1, 0)])
+
+
+def joined(pair, axis):
+    own, other = pair
+    if lax.axis_size("dp") != 2:
+        return other
     first = lax.axis_index("dp") == 0
     return jnp.concatenate(
-        [jnp.where(first, x, other), jnp.where(first, other, x)], axis=axis
-    )
-
-
-def scatter_dp(x, axis):
-    size = lax.axis_size("dp")
-    if size != 2:
-        return lax.psum_scatter(low(x), "dp", scatter_dimension=axis, tiled=True).astype(
-            jnp.float32
-        )
+        [jnp.where(first, own, other), jnp.where(first, other, own)], axis=axis
+    )
+
+
+def send_dp(x, axis):
+    if lax.axis_size("dp") != 2:
+        total = lax.psum_scatter(x, "dp", scatter_dimension=axis, tiled=True)
+        return total, jnp.zeros_like(total)
     half = x.shape[axis] // 2
     index = lax.axis_index("dp")
-    away = low(lax.dynamic_slice_in_dim(x, (1 - index) * half, half, axis))
+    away = lax.dynamic_slice_in_dim(x, (1 - index) * half, half, axis)
     arrived = lax.ppermute(away, "dp", [(0, 1), (1, 0)])
-    return lax.dynamic_slice_in_dim(x, index * half, half, axis) + arrived.astype(jnp.float32)
+    return lax.dynamic_slice_in_dim(x, index * half, half, axis), arrived
+
+
+def added(pair):
+    return pair[0].astype(jnp.float32) + pair[1].astype(jnp.float32)
 
 
 def cross(a, b):
     return lax.dot_general(a, b, (((1,), (1,)), ((), ())), preferred_element_type=jnp.float32)
 
 
-def heads_of(quads, rows, qn, qa, qb):
+HEADS = 2
+
+
+def spread_matrix(quads, dtype):
+    half = ROPE // 2
+    source = lax.broadcasted_iota(jnp.int32, (128, 256), 0)
+    target = lax.broadcasted_iota(jnp.int32, (128, 256), 1)
+    wanted = target % half + half * (target // (half * quads))
+    return (source == wanted).astype(jnp.float32).astype(dtype)
+
+
+def head_query(u, rows, qn, qa, qb):
+    quads = qa.shape[1] // (ROPE // 2)
     lanes = lax.broadcasted_iota(jnp.int32, (1, qa.shape[1]), 1) // (ROPE // 2)
-    ours = lanes == pl.program_id(0) % quads
+    ours = lanes == (pl.program_id(0) * HEADS + u) % quads
     nothing = jnp.zeros((), qa.dtype)
-    return (
-        ours,
-        qn[rows, :],
-        jnp.where(ours, qa[rows, :], nothing),
-        jnp.where(ours, qb[rows, :], nothing),
-    )
-
-
-def attend_kernel(tokens, scale, qn, qa, qb, latent, ka, kb, expand, bias, out):
-    quads = qa.shape[1] // (ROPE // 2)
+    parts = jnp.concatenate(
+        [jnp.where(ours, qa[rows, :], nothing), jnp.where(ours, qb[rows, :], nothing)], axis=1
+    )
+    turned = low(cross(parts, spread_matrix(quads, jnp.bfloat16)))
+    return ours, jnp.concatenate([qn[rows, u * NOPE : (u + 1) * NOPE], turned], axis=1)
+
+
+def load_window(tokens, span, line, window, sems):
+    lane = lax.axis_index("expert")
+    copies = []
+    for j in range(span):
+        source = lane - (span - 1) + j
+        rows = pl.ds(j * tokens, tokens)
+        for m in range(MICRO):
+            copy = pltpu.make_async_copy(
+                line.at[jnp.maximum(source, 0), pl.ds(m * tokens, tokens)],
+                window.at[m, rows],
+                sems.at[m, j],
+            )
+            pl.when(source >= 0)(copy.start)
+            copies.append((source >= 0, copy))
+
+            @pl.when(source < 0)
+            def _(m=m, rows=rows):
+                window[m, rows] = jnp.zeros((tokens, window.shape[2]), window.dtype)
+
+    left = window.shape[1] - span * tokens
+    if left:
+        for m in range(MICRO):
+            window[m, pl.ds(span * tokens, left)] = jnp.zeros((left, window.shape[2]), window.dtype)
+    for there, copy in copies:
+        pl.when(there)(copy.wait)
+
+
+def attend_kernel(tokens, span, scale, qn, qa, qb, line, expand, bias, out, window, sems):
+    @pl.when(pl.program_id(0) == 0)
+    def _():
+        load_window(tokens, span, line, window, sems)
+
     for m in range(MICRO):
         rows = pl.ds(m * tokens, tokens)
-        pair = low(dot(latent[m], expand[...]))
-        keys, values = pair[:, :NOPE], pair[:, NOPE:]
-        _, own, first, second = heads_of(quads, rows, qn, qa, qb)
-        scores = cross(own, keys) + cross(first, ka[m]) + cross(second, kb[m])
-        scores = scores * scale + bias[m]
-        raised = jnp.exp(scores - jnp.max(scores, axis=1, keepdims=True))
-        weights = low(raised / jnp.sum(raised, axis=1, keepdims=True))
-        out[rows, :] = low(dot(weights, values))
+        pairs = low(dot(window[m, :, :LAT], expand[...]))
+        turns = window[m, :, LAT:]
+        for u in range(HEADS):
+            pair = pairs[:, u * (NOPE + VDIM) : (u + 1) * (NOPE + VDIM)]
+            keys = jnp.concatenate([pair[:, :NOPE], turns], axis=1)
+            _, own = head_query(u, rows, qn, qa, qb)
+            scores = cross(own, keys) * scale + bias[m]
+            raised = jnp.exp(scores - jnp.max(scores, axis=1, keepdims=True))
+            weights = low(raised * (1.0 / jnp.sum(raised, axis=1, keepdims=True)))
+            out[rows, u * VDIM : (u + 1) * VDIM] = low(dot(weights, pair[:, NOPE:]))
 
 
 def attend_back_kernel(
-    tokens, scale, qn, qa, qb, grad, latent, turned, ka, kb, expand, bias, gqn, gqa, gqb, glat, gka, gkb, gexp
+    tokens, span, scale, qn, qa, qb, grad, line, expand, bias, gqn, gqa, gqb, gline, gexp, *scratch
 ):
+    window, upright, glat, gturns, gwindow, zeros, sems, out_sems = scratch
     head = pl.program_id(0)
     quads = qa.shape[1] // (ROPE // 2)
 
     @pl.when(head == 0)
     def _():
+        load_window(tokens, span, line, window, sems)
+        for m in range(MICRO):
+            upright[m] = window[m, :, :LAT].T
         glat[...] = jnp.zeros_like(glat)
-        gka[...] = jnp.zeros_like(gka)
-        gkb[...] = jnp.zeros_like(gkb)
-
-    @pl.when(head % quads == 0)
+        gturns[...] = jnp.zeros_like(gturns)
+
+    @pl.when((head * HEADS) % quads == 0)
     def _():
         gqa[...] = jnp.zeros_like(gqa)
         gqb[...] = jnp.zeros_like(gqb)
@@ -594,31 +656,67 @@
     expand_total = None
     for m in range(MICRO):
         rows = pl.ds(m * tokens, tokens)
-        pair = low(dot(latent[m], expand[...]))
-        keys, values = pair[:, :NOPE], pair[:, NOPE:]
-        ours, own, first, second = heads_of(quads, rows, qn, qa, qb)
-        grad_rows = grad[rows, :]
-        scores = cross(keys, own) + cross(ka[m], first) + cross(kb[m], second)
-        scores = scores * scale + bias[m]
-        raised = jnp.exp(scores - jnp.max(scores, axis=0, keepdims=True))
-        probs = raised / jnp.sum(raised, axis=0, keepdims=True)
-        grad_probs = cross(values, grad_rows)
-        shift = jnp.sum(grad_probs * probs, axis=0, keepdims=True)
-        back = low(probs * (grad_probs - shift))
-        across = back.T
-        gqn[rows, :] = low(dot(across, keys) * scale)
-        gqa[rows, :] += jnp.where(ours, dot(across, ka[m]) * scale, 0.0)
-        gqb[rows, :] += jnp.where(ours, dot(across, kb[m]) * scale, 0.0)
-        gka[m] += dot(back, first) * scale
-        gkb[m] += dot(back, second) * scale
-        both = jnp.concatenate(
-            [low(dot(back, own) * scale), low(dot(low(probs), grad_rows))], axis=1
-        )
+        pairs = low(dot(window[m, :, :LAT], expand[...]))
+        turns = window[m, :, LAT:]
+        grad_pairs = []
+        turns_total = None
+        for u in range(HEADS):
+            pair = pairs[:, u * (NOPE + VDIM) : (u + 1) * (NOPE + VDIM)]
+            keys = jnp.concatenate([pair[:, :NOPE], turns], axis=1)
+            ours, own = head_query(u, rows, qn, qa, qb)
+            grad_rows = grad[rows, u * VDIM : (u + 1) * VDIM]
+            scores = cross(keys, own) * scale + bias[m]
+            raised = jnp.exp(scores - jnp.max(scores, axis=0, keepdims=True))
+            probs = raised * (1.0 / jnp.sum(raised, axis=0, keepdims=True))
+            grad_probs = cross(pair[:, NOPE:], grad_rows)
+            shift = jnp.sum(grad_probs * probs, axis=0, keepdims=True)
+            back = low(probs * (grad_probs - shift))
+            grad_own = dot(back.T, keys) * scale
+            gqn[rows, u * NOPE : (u + 1) * NOPE] = low(grad_own[:, :NOPE])
+            spread = lax.dot_general(
+                grad_own[:, NOPE:],
+                spread_matrix(quads, jnp.float32),
+                (((1,), (0,)), ((), ())),
+                precision=HIGHEST_PRECISION,
+                preferred_element_type=jnp.float32,
+            )
+            gqa[rows, :] += jnp.where(ours, spread[:, :128], 0.0)
+            gqb[rows, :] += jnp.where(ours, spread[:, 128:], 0.0)
+            grad_keys = dot(back, own) * scale
+            turned = grad_keys[:, NOPE:]
+            turns_total = turned if turns_total is None else turns_total + turned
+            grad_pairs.append(low(grad_keys[:, :NOPE]))
+            grad_pairs.append(low(dot(low(probs), grad_rows)))
+        gturns[m] += turns_total
+        both = jnp.concatenate(grad_pairs, axis=1)
         glat[m] += cross(both, expand[...])
-        part = dot(turned[m], both)
+        part = dot(upright[m], both)
         expand_total = part if expand_total is None else expand_total + part
     gexp[...] = low(expand_total)
 
+    @pl.when(head == pl.num_programs(0) - 1)
+    def _():
+        lane = lax.axis_index("expert")
+        zeros[...] = jnp.zeros_like(zeros)
+        for m in range(MICRO):
+            gwindow[m, :, :LAT] = low(glat[m])
+            gwindow[m, :, LAT:] = low(gturns[m])
+        copies = []
+        for slot in range(gline.shape[0]):
+            j = slot - lane + span - 1
+            inside = (j >= 0) & (j < span)
+            start = pl.multiple_of(jnp.clip(j, 0, span - 1) * tokens, tokens)
+            for m in range(MICRO):
+                target = gline.at[slot, pl.ds(m * tokens, tokens)]
+                sem = out_sems.at[slot, m]
+                full = pltpu.make_async_copy(gwindow.at[m, pl.ds(start, tokens)], target, sem)
+                empty = pltpu.make_async_copy(zeros, target, sem)
+                pl.when(inside)(full.start)
+                pl.when(jnp.logical_not(inside))(empty.start)
+                copies.append(full)
+        for copy in copies:
+            copy.wait()
+
 
 def whole_block(a):
     return pl.BlockSpec(a.shape, lambda h: (0,) * len(a.shape))
@@ -626,63 +724,81 @@
 
 def attention_specs(rows, quads):
     return [
-        pl.BlockSpec((rows, NOPE), lambda h: (0, h)),
-        pl.BlockSpec((rows, 128), lambda h: (0, h // quads)),
-        pl.BlockSpec((rows, 128), lambda h: (0, h // quads)),
+        pl.BlockSpec((rows, HEADS * NOPE), lambda h: (0, h)),
+        pl.BlockSpec((rows, 128), lambda h: (0, h * HEADS // quads)),
+        pl.BlockSpec((rows, 128), lambda h: (0, h * HEADS // quads)),
     ]
 
 
-def attention_forward(tokens, scale, qn, qa, qb, latent, ka, kb, expand, bias):
+def attention_forward(tokens, span, scale, qn, qa, qb, line, expand, bias):
     rows = qn.shape[0]
     quads = 128 // (ROPE // 2)
+    key_rows = bias.shape[2]
     return pl.pallas_call(
-        functools.partial(attend_kernel, tokens, scale),
-        grid=(H,),
+        functools.partial(attend_kernel, tokens, span, scale),
+        grid=(H // HEADS,),
         out_shape=jax.ShapeDtypeStruct((rows, H * VDIM), jnp.bfloat16),
         in_specs=attention_specs(rows, quads)
-        + [whole_block(latent), whole_block(ka), whole_block(kb)]
-        + [pl.BlockSpec((LAT, NOPE + VDIM), lambda h: (0, h)), whole_block(bias)],
-        out_specs=pl.BlockSpec((rows, VDIM), lambda h: (0, h)),
+        + [ANYWHERE, pl.BlockSpec((LAT, HEADS * (NOPE + VDIM)), lambda h: (0, h)), whole_block(bias)],
+        out_specs=pl.BlockSpec((rows, HEADS * VDIM), lambda h: (0, h)),
+        scratch_shapes=[
+            pltpu.VMEM((MICRO, key_rows, line.shape[2]), jnp.bfloat16),
+            pltpu.SemaphoreType.DMA((MICRO, span)),
+        ],
         compiler_params=pltpu.CompilerParams(vmem_limit_bytes=56 << 20),
         cost_estimate=pl.CostEstimate(
             flops=25 * 10**9, bytes_accessed=20 * 10**6, transcendentals=0
         ),
-    )(qn, qa, qb, latent, ka, kb, expand, bias)
-
-
-def attention_backward(tokens, scale, qn, qa, qb, grad, latent, ka, kb, expand, bias):
+    )(qn, qa, qb, line, expand, bias)
+
+
+def attention_backward(tokens, span, scale, qn, qa, qb, grad, line, expand, bias):
     rows = qn.shape[0]
     quads = 128 // (ROPE // 2)
-    turned = jnp.swapaxes(latent, 1, 2)
+    key_rows = bias.shape[1]
+    width = line.shape[2]
     single = jax.ShapeDtypeStruct
     return pl.pallas_call(
-        functools.partial(attend_back_kernel, tokens, scale),
-        grid=(H,),
+        functools.partial(attend_back_kernel, tokens, span, scale),
+        grid=(H // HEADS,),
         out_shape=[
             single(qn.shape, jnp.bfloat16),
             single(qa.shape, jnp.float32),
             single(qb.shape, jnp.float32),
-            single(latent.shape, jnp.float32),
-            single(ka.shape, jnp.float32),
-            single(kb.shape, jnp.float32),
+            single(line.shape, jnp.bfloat16),
             single(expand.shape, jnp.bfloat16),
         ],
         in_specs=attention_specs(rows, quads)
-        + [pl.BlockSpec((rows, VDIM), lambda h: (0, h))]
-        + [whole_block(latent), whole_block(turned), whole_block(ka), whole_block(kb)]
-        + [pl.BlockSpec((LAT, NOPE + VDIM), lambda h: (0, h)), whole_block(bias)],
+        + [pl.BlockSpec((rows, HEADS * VDIM), lambda h: (0, h)), ANYWHERE]
+        + [pl.BlockSpec((LAT, HEADS * (NOPE + VDIM)), lambda h: (0, h)), whole_block(bias)],
         out_specs=attention_specs(rows, quads)
-        + [whole_block(latent), whole_block(ka), whole_block(kb)]
-        + [pl.BlockSpec((LAT, NOPE + VDIM), lambda h: (0, h))],
+        + [ANYWHERE, pl.BlockSpec((LAT, HEADS * (NOPE + VDIM)), lambda h: (0, h))],
+        scratch_shapes=[
+            pltpu.VMEM((MICRO, key_rows, width), jnp.bfloat16),
+            pltpu.VMEM((MICRO, LAT, key_rows), jnp.bfloat16),
+            pltpu.VMEM((MICRO, key_rows, LAT), jnp.float32),
+            pltpu.VMEM((MICRO, key_rows, 128), jnp.float32),
+            pltpu.VMEM((MICRO, key_rows, width), jnp.bfloat16),
+            pltpu.VMEM((tokens, width), jnp.bfloat16),
+            pltpu.SemaphoreType.DMA((MICRO, span)),
+            pltpu.SemaphoreType.DMA((line.shape[0], MICRO)),
+        ],
         compiler_params=pltpu.CompilerParams(vmem_limit_bytes=56 << 20),
         cost_estimate=pl.CostEstimate(
-            flops=50 * 10**9, bytes_accessed=30 * 10**6, transcendentals=0
+            flops=60 * 10**9, bytes_accessed=30 * 10**6, transcendentals=0
         ),
-    )(qn, qa, qb, grad, latent, turned, ka, kb, expand, bias)
-
-
-def combine_kernel(picked, rows, left, right, out):
-    out[...] = low(dot(picked[0], rows[0]) + dot(left[...], right[...]))
+    )(qn, qa, qb, grad, line, expand, bias)
+
+
+def combine_kernel(picked, rows, left, right, out, below):
+    inner = right.shape[0]
+
+    @pl.when(pl.program_id(0) == 0)
+    def _():
+        below[pl.ds(0, inner), :] = right[...]
+
+    below[pl.ds(inner, rows.shape[1]), :] = rows[0]
+    out[...] = low(dot(jnp.concatenate([left[...], picked[0]], axis=1), below[...]))
 
 
 def combine(picked, rows, left, right):
@@ -699,6 +815,7 @@
             pl.BlockSpec((inner, D), lambda g: (0, 0)),
         ],
         out_specs=pl.BlockSpec((group_rows, D), lambda g: (g, 0)),
+        scratch_shapes=[pltpu.VMEM((inner + slots, D), jnp.bfloat16)],
         compiler_params=pltpu.CompilerParams(vmem_limit_bytes=48 << 20),
         cost_estimate=pl.CostEstimate(
             flops=2 * total * (slots + inner) * D,
@@ -706,6 +823,11 @@
             transcendentals=0,
         ),
     )(picked, rows.reshape(groups, slots, D), left, right)
+
+
+def halves_of(x):
+    parts = 2 if x.shape[0] % 32 == 0 else 1
+    return x.reshape(parts, x.shape[0] // parts, x.shape[1])
 
 
 def body(
@@ -760,16 +882,14 @@
         ],
         axis=1,
     )
-    all_query, all_latent, all_expand, all_output, small = gather(
-        [split_query, latent_weight, expand_weight.reshape(16, -1), output_weight.T, small],
+    all_query, all_latent, all_expand, small = gather(
+        [halves_of(split_query), latent_weight, expand_weight.reshape(16, -1), small],
         ALL_ORDERS,
-        True,
         1,
     )
     all_query = all_query.reshape(D, key_width)
     all_latent = all_latent.reshape(D, LAT + ROPE)
     all_expand = all_expand.reshape(LAT, H * (NOPE + VDIM))
-    all_output = all_output.reshape(D, H * VDIM)
     gain_latent = small[:, :small_latent, experts_count + 2].reshape(LAT).astype(jnp.float32)
     small = small.reshape(D, 128)
     all_router = small[:, :experts_count]
@@ -777,32 +897,23 @@
     gain_second = small[:, experts_count + 1].astype(jnp.float32)
 
     (later, all_query) = lax.optimization_barrier(
-        ((expert_gate, expert_up, expert_down, shared_gate, shared_up, shared_down, cotangent), all_query)
-    )
-    expert_gate, expert_up, expert_down, shared_gate, shared_up, shared_down, sent_cotangent = later
-    expert_gate = gather_dp(expert_gate[0], 0)
-    expert_up = gather_dp(expert_up[0], 0)
-    expert_down = gather_dp(expert_down[0], 1)
+        (
+            (expert_gate, expert_up, expert_down, shared_gate, shared_up, shared_down, output_weight),
+            all_query,
+        )
+    )
+    expert_gate, expert_up, expert_down, shared_gate, shared_up, shared_down, output_weight = later
+    all_output = lax.all_gather(output_weight.T, ("dp", "expert"), axis=0, tiled=True)
+    parts_gate = fetch_dp(expert_gate[0], 0)
+    parts_up = fetch_dp(expert_up[0], 0)
+    parts_down = fetch_dp(expert_down[0], 1)
     units = shared_down.shape[0]
     mine = n_dp * units
     both = jnp.stack([shared_gate, shared_up], axis=1).reshape(shard, 2, n_dp, n_expert, units)
     both = both.transpose(3, 0, 1, 2, 4).reshape(n_expert, shard, 2 * mine)
     both = lax.all_to_all(both, "expert", split_axis=0, concat_axis=0, tiled=True)
-    shared_in = gather_dp(both.reshape(n_expert * shard, 2 * mine), 0)
-    padded = -(-(mine + experts_count) // 128) * 128
-    rest = jnp.zeros((D, padded - mine - experts_count), jnp.bfloat16)
-    shared_in = jnp.concatenate(
-        [
-            shared_in[:, :mine],
-            all_router,
-            rest,
-            shared_in[:, mine:],
-            jnp.zeros((D, padded - mine), jnp.bfloat16),
-        ],
-        axis=1,
-    )
-    shared_out_weight = jnp.pad(gather_dp(shared_down, 0), ((0, padded - mine), (0, 0)))
-
+    parts_in = fetch_dp(both.reshape(n_expert * shard, 2 * mine), 0)
+    parts_out = fetch_dp(shared_down, 0)
 
     positions = lane * tokens + jnp.arange(tokens, dtype=jnp.int32)
     cosine_table, sine_table = angles(positions)
@@ -815,7 +926,12 @@
     latent = dot(hidden, all_latent)
     compressed = low(root_normalize(latent[:, :LAT], gain_latent))
     key_rope = low(rotate(latent[:, LAT:], cosine_rows, sine_rows))
-    (line,) = gather([jnp.concatenate([compressed, key_rope], axis=1)], [PLANE], False, 2)
+    payload = jnp.concatenate(
+        [compressed, key_rope, jnp.zeros((rows, 128 - ROPE), jnp.bfloat16)], axis=1
+    )
+    columns = jnp.pad(routes[0].reshape(rows, TOP).T, ((0, 8 - TOP), (0, 0)))
+    line, all_routes = gather([payload, columns], [PLANE, PLANE], 2)
+    sent_cotangent, line = lax.optimization_barrier((cotangent, line))
     query = dot(hidden, all_query)
     plain = H * NOPE
     half = H * ROPE // 2
@@ -826,17 +942,7 @@
     query_second = low(turn_first * head_sine + turn_second * head_cosine)
     reach = (WINDOW + tokens - 2) // tokens
     span = reach + 1
-    key_rows = span * tokens
-    line = jnp.concatenate(
-        [jnp.zeros((reach,) + line.shape[1:], line.dtype), line], axis=0
-    )
-    window = lax.dynamic_slice_in_dim(line, lane, span, 0)
-    window = window.reshape(span, MICRO, tokens, LAT + ROPE).transpose(1, 0, 2, 3)
-    window = window.reshape(MICRO, key_rows, LAT + ROPE)
-    window_latent = window[..., :LAT]
-    quads = 128 // (ROPE // 2)
-    key_first = jnp.tile(window[..., LAT : LAT + ROPE // 2], (1, 1, quads))
-    key_second = jnp.tile(window[..., LAT + ROPE // 2 :], (1, 1, quads))
+    key_rows = -(-span * tokens // 128) * 128
     key_positions = (lane - reach) * tokens + jnp.arange(key_rows, dtype=jnp.int32)
     apart = positions[:, None] - key_positions[None, :]
     reachable = (key_positions[None, :] >= 0) & (apart >= 0) & (apart < WINDOW)
@@ -853,13 +959,12 @@
     bias = jnp.where(allowed, 0.0, NEGATIVE).astype(jnp.float32)
     mixture = attention_forward(
         tokens,
+        span,
         score_scale,
         query_plain,
         query_first,
         query_second,
-        window_latent,
-        key_first,
-        key_second,
+        line,
         all_expand,
         bias,
     )
@@ -867,17 +972,26 @@
     normed = low(root_normalize(residual, gain_second))
 
     chunked = normed.reshape(CHUNKS, rows // CHUNKS, D)
-    (all_normed,) = gather([chunked], [CHUNK_ORDERS], False, 3)
+    own_probs = jax.nn.softmax(dot(normed, all_router), axis=-1)
+    all_normed, all_probs = gather([chunked, own_probs.T], [CHUNK_ORDERS, PLANE], 3)
     all_normed = all_normed.reshape(n_expert * rows, D)
+    fetched = (parts_gate, parts_up, parts_down, parts_in, parts_out)
+    all_normed, fetched = lax.optimization_barrier((all_normed, fetched))
+    expert_gate, expert_up = joined(fetched[0], 0), joined(fetched[1], 0)
+    expert_down = joined(fetched[2], 1)
+    padded = -(-mine // 128) * 128
+    shared_in = jnp.pad(
+        joined(fetched[3], 0).reshape(D, 2, mine), ((0, 0), (0, 0), (0, padded - mine))
+    ).reshape(D, 2 * padded)
+    shared_out_weight = jnp.pad(joined(fetched[4], 0), ((0, padded - mine), (0, 0)))
     all_cotangent = gather_plane(sent_cotangent[0].reshape(rows, D)).reshape(n_expert * rows, D)
-    all_routes = gather_plane(routes[0].reshape(rows, TOP))
     total_rows = n_expert * rows
     capacity = (9 * tokens * TOP + 8 * experts_count - 1) // (8 * experts_count)
     per_group = max(1, 256 // tokens)
     group_rows = per_group * tokens
     groups = total_rows // group_rows
     slots = -(-per_group * capacity // 16) * 16
-    named = jnp.any(all_routes == lane, axis=-1).reshape(-1, tokens).astype(jnp.int32)
+    named = jnp.any(all_routes[:, :TOP] == lane, axis=1).reshape(-1, tokens).astype(jnp.int32)
     rank = jnp.cumsum(named, axis=1) - named
     kept = (named > 0) & (rank < capacity)
     offset = (jnp.arange(named.shape[0], dtype=jnp.int32) % per_group) * capacity
@@ -885,10 +999,8 @@
     picked_bool = place == jnp.arange(slots, dtype=jnp.int32)[None, :, None]
     picked = picked_bool.astype(jnp.bfloat16)
     picked_float = picked_bool.astype(jnp.float32)
-    shared_pre = dot(all_normed, shared_in)
-    probabilities = jax.nn.softmax(shared_pre[:, mine : mine + experts_count], axis=-1)
-    own_column = jnp.arange(experts_count, dtype=jnp.int32) == lane
-    gate_rows = jnp.sum(jnp.where(own_column[None, :], probabilities, 0.0), axis=1)
+    shared_pre = low(dot(all_normed, shared_in))
+    gate_rows = lax.dynamic_index_in_dim(all_probs, lane, 1, keepdims=False)
     gate_slots = jnp.sum(
         picked_float * gate_rows.reshape(groups, 1, group_rows), axis=2
     ).reshape(groups * slots, 1)
@@ -904,11 +1016,11 @@
         ).reshape(groups * slots, D)
 
     arrived = to_slots(all_normed)
-    gate_pre = dot(arrived, expert_gate)
-    up_pre = dot(arrived, expert_up)
-    expert_act = low(silu_product(gate_pre, up_pre))
+    gate_pre = low(dot(arrived, expert_gate))
+    up_pre = low(dot(arrived, expert_up))
+    expert_act = low(silu_product(wide(gate_pre), wide(up_pre)))
     expert_out = low(dot(expert_act, expert_down))
-    shared_act = low(silu_product(shared_pre[:, :padded], shared_pre[:, padded:]))
+    shared_act = low(silu_product(wide(shared_pre[:, :padded]), wide(shared_pre[:, padded:])))
     spread = jnp.swapaxes(picked, 1, 2)
     partial_out = combine(
         spread, low(gate_slots * expert_out.astype(jnp.float32)), shared_act, shared_out_weight
@@ -925,42 +1037,85 @@
         gate_grad_rows, "expert", split_axis=0, concat_axis=0, tiled=True
     ).T
     slot_grad = low(gate_slots * arrived_grad.astype(jnp.float32))
-    expert_down_grad = transposed_left(expert_act, slot_grad)
-    gate_back, up_back = silu_back(gate_pre, up_pre, transposed_right(slot_grad, expert_down))
+    expert_down_grad = low(transposed_left(expert_act, slot_grad))
+    gate_back, up_back = silu_back(
+        wide(gate_pre), wide(up_pre), transposed_right(slot_grad, expert_down)
+    )
     gate_back = low(gate_back)
     up_back = low(up_back)
-    expert_gate_grad = transposed_left(arrived, gate_back)
-    expert_up_grad = transposed_left(arrived, up_back)
+    expert_gate_grad = low(transposed_left(arrived, gate_back))
+    expert_up_grad = low(transposed_left(arrived, up_back))
     rows_grad = low(
         transposed_right(gate_back, expert_gate) + transposed_right(up_back, expert_up)
     )
     shared_back = jnp.concatenate(
         silu_back(
-            shared_pre[:, :padded],
-            shared_pre[:, padded:],
+            wide(shared_pre[:, :padded]),
+            wide(shared_pre[:, padded:]),
             transposed_right(all_cotangent, shared_out_weight),
         ),
         axis=1,
     ).astype(jnp.bfloat16)
-    no_router = jnp.concatenate(
+    partial_normed = combine(spread, rows_grad, shared_back, shared_in.T)
+    partial_normed = partial_normed.reshape(n_expert, CHUNKS, rows // CHUNKS, D)
+    (grad_normed,) = scatter([partial_normed], [CHUNK_ORDERS], 4)
+    grad_normed = grad_normed.reshape(rows, D)
+    sums = [
+        send_dp(expert_gate_grad, 0),
+        send_dp(expert_up_grad, 0),
+        send_dp(expert_down_grad, 1),
+        send_dp(low(transposed_left(shared_act, all_cotangent)[:mine]), 0),
+        send_dp(low(transposed_left(all_normed, shared_back)), 0),
+    ]
+
+    logit_grad = low(
+        own_probs * (gate_grads - jnp.sum(gate_grads * own_probs, axis=-1, keepdims=True))
+    )
+    router_weight_grad = transposed_left(normed, logit_grad)
+    grad_normed = grad_normed + transposed_right(logit_grad, all_router)
+    residual_extra, feed_gain_grad = normalize_back(residual, gain_second, grad_normed)
+    grad_residual = cotangent[0].reshape(rows, D).astype(jnp.float32) + residual_extra
+
+    grad_attn = low(grad_residual)
+    output_grad = low(transposed_left(grad_attn, mixture))
+    output_grad = lax.psum_scatter(output_grad, ("dp", "expert"), scatter_dimension=0, tiled=True)
+    grad_mixture = low(dot(grad_attn, all_output))
+    grad_plain, grad_first, grad_second, grad_line, expand_grad = attention_backward(
+        tokens,
+        span,
+        score_scale,
+        query_plain,
+        query_first,
+        query_second,
+        grad_mixture,
+        line,
+        all_expand,
+        jnp.swapaxes(bias, 1, 2),
+    )
+    grad_query = jnp.concatenate(
         [
-            shared_in[:, :mine],
-            jnp.zeros((D, padded - mine), jnp.bfloat16),
-            shared_in[:, padded:],
+            grad_plain,
+            low(grad_first * head_cosine + grad_second * head_sine),
+            low(grad_second * head_cosine - grad_first * head_sine),
         ],
         axis=1,
     )
-    partial_normed = combine(spread, rows_grad, shared_back, no_router.T)
-    partial_normed = partial_normed.reshape(n_expert, CHUNKS, rows // CHUNKS, D)
-    (grad_normed,) = scatter([partial_normed], [CHUNK_ORDERS], False, 4)
-    grad_normed = grad_normed.reshape(rows, D)
-    shared_down_grad = scatter_dp(transposed_left(shared_act, all_cotangent)[:mine], 0)
-    shared_in_grad = scatter_dp(transposed_left(all_normed, shared_back), 0)
-    shared_in_grad = jnp.concatenate(
-        [shared_in_grad[:, :mine], shared_in_grad[:, padded : padded + mine]], axis=1
-    )
+    query_grad = low(transposed_left(hidden, grad_query))
+    grad_line, query_grad, expand_grad = scatter(
+        [
+            grad_line,
+            query_grad.reshape(devices, shard, key_width),
+            expand_grad.reshape(devices, 16, -1),
+        ],
+        [PLANE, ZYX, XYZ],
+        5,
+    )
+    sums, grad_line = lax.optimization_barrier((sums, grad_line))
+    expert_grads = [added(pair)[None] for pair in sums[:3]]
+    shared_down_grad = added(sums[3])
+    shared_in_grad = low(added(sums[4])).reshape(n_expert, shard, 2, padded)[..., :mine]
     shared_in_grad = lax.all_to_all(
-        low(shared_in_grad).reshape(n_expert, shard, 2 * mine),
+        shared_in_grad.reshape(n_expert, shard, 2 * mine),
         "expert",
         split_axis=0,
         concat_axis=0,
@@ -971,67 +1126,12 @@
         .transpose(2, 1, 3, 0, 4)
         .reshape(2, shard, n_dp * n_expert * units)
     )
-    expert_grads = (
-        scatter_dp(expert_gate_grad, 0)[None],
-        scatter_dp(expert_up_grad, 0)[None],
-        scatter_dp(expert_down_grad, 1)[None],
-    )
-
-    own_probs = lax.dynamic_slice_in_dim(probabilities, lane * rows, rows, 0)
-    logit_grad = low(
-        own_probs * (gate_grads - jnp.sum(gate_grads * own_probs, axis=-1, keepdims=True))
-    )
-    router_weight_grad = transposed_left(normed, logit_grad)
-    grad_normed = grad_normed + transposed_right(logit_grad, all_router)
-    residual_extra, feed_gain_grad = normalize_back(residual, gain_second, grad_normed)
-    grad_residual = cotangent[0].reshape(rows, D).astype(jnp.float32) + residual_extra
-
-    grad_attn = low(grad_residual)
-    output_grad = transposed_left(grad_attn, mixture)
-    grad_mixture = low(dot(grad_attn, all_output))
-    grad_plain, grad_first, grad_second, grad_latents, grad_kfirst, grad_ksecond, expand_grad = (
-        attention_backward(
-            tokens,
-            score_scale,
-            query_plain,
-            query_first,
-            query_second,
-            grad_mixture,
-            window_latent,
-            key_first,
-            key_second,
-            all_expand,
-            jnp.swapaxes(bias, 1, 2),
-        )
-    )
-
-    def folded(x):
-        return jnp.sum(x.reshape(MICRO, key_rows, quads, ROPE // 2), axis=2)
-
-    grad_window = jnp.concatenate(
-        [grad_latents, folded(grad_kfirst), folded(grad_ksecond)], axis=-1
-    )
-    grad_window = low(grad_window).reshape(MICRO, span, tokens, LAT + ROPE)
-    grad_window = grad_window.transpose(1, 0, 2, 3).reshape(span, rows, LAT + ROPE)
-    grad_line = lax.dynamic_update_slice_in_dim(
-        jnp.zeros((n_expert + reach, rows, LAT + ROPE), jnp.bfloat16), grad_window, lane, 0
-    )[reach:]
-    (grad_line,) = scatter([grad_line], [PLANE], False, 5)
     latent_part, latent_gain_grad = normalize_back(
         latent[:, :LAT], gain_latent, grad_line[:, :LAT]
     )
-    grad_key_rope = rotate(grad_line[:, LAT:], cosine_rows, -sine_rows)
+    grad_key_rope = rotate(grad_line[:, LAT : LAT + ROPE], cosine_rows, -sine_rows)
     grad_latent = low(jnp.concatenate([latent_part, grad_key_rope], axis=1))
     latent_grad = transposed_left(hidden, grad_latent)
-    grad_query = jnp.concatenate(
-        [
-            grad_plain,
-            low(grad_first * head_cosine + grad_second * head_sine),
-            low(grad_second * head_cosine - grad_first * head_sine),
-        ],
-        axis=1,
-    )
-    query_grad = transposed_left(hidden, grad_query)
     grad_hidden = transposed_right(grad_latent, all_latent) + transposed_right(
         grad_query, all_query
     )
@@ -1051,17 +1151,8 @@
     )[:, :, None]
     small_grad = jnp.concatenate([small_grad, latent_column], axis=2)
     small_grad = jnp.pad(small_grad, ((0, 0), (0, 0), (0, 128 - small_grad.shape[2])))
-    query_grad, latent_grad, expand_grad, output_grad, small_grad = scatter(
-        [
-            low(query_grad).reshape(devices, shard, key_width),
-            low(latent_grad).reshape(devices, shard, LAT + ROPE),
-            expand_grad.reshape(devices, 16, -1),
-            low(output_grad).reshape(devices, shard, H * VDIM),
-            low(small_grad),
-        ],
-        ALL_ORDERS,
-        True,
-        6,
+    latent_grad, small_grad = scatter(
+        [low(latent_grad).reshape(devices, shard, LAT + ROPE), low(small_grad)], [ZYX, ZXY], 6
     )
     query_grad = jnp.concatenate(
         [
@@ -1079,7 +1170,7 @@
         latent_grad,
         small_grad[:small_latent, experts_count + 2],
         expand_grad.reshape(expand_weight.shape),
-        output_grad.T,
+        wide(output_grad).T,
         small_grad[:, experts_count + 1],
         small_grad[:, :experts_count],
         shared_in_grad[0],

time: 1480 us -> 1260 us (0.85)
  waiting for transfers between devices: 82 us -> 0.12 us
  local copies, waits for them, and re-layouts: 146 us -> 82.7 us
  blocking collectives: 39.4 us -> 0 us
  Pallas kernels: 774 us -> 740 us
  matrix products: 275 us -> 293 us
    ppermute x10, waiting for transfers between devices: 71.9 us -> 0.03 us  [the longest x5 0.01 us: fetch_dp(): return (x, lax.ppermute(x, 'dp', [(0, 1), (1, 0)]))]
    all_gather x1 -> x0, blocking collectives: 39.4 us -> none  [gather_plane(): return lax.all_gather(x, 'expert', axis=0, tiled=False)]
    pallas_call x8, Pallas kernels: 734 us -> 700 us  [the longest x3 310 us: gather(): pl.pallas_call(functools.partial(gather_kernel, items, sizes), out_shape=...]
    unnamed x203 -> x193, local copies, waits for them, and re-layouts: 37.6 us -> 8.39 us
    slice x9 -> x1, local copies, waits for them, and re-layouts: 22.1 us -> 0.06 us  [body(): transposed_left(shared_act, all_cotangent)[:mine]]
    dynamic_slice x1 -> x6, local copies, waits for them, and re-layouts: 3.12 us -> 18 us  [the longest x5 17.1 us: send_dp(): away = lax.dynamic_slice_in_dim(x, (1 - index) * half, half, axis)]
    dot_general x7 -> x8, matrix products: 81.9 us -> 79.4 us  [dot(): return jnp.dot(a, b, preferred_element_type=jnp.float32)]
  transfers between devices with their start and end apart: 15 -> 17, of which waited for: 4 -> 0; matrix products, arithmetic and copies ran while one was open for 24% -> 32% of each run, Pallas kernels for 24% -> 51%
where the time goes in v3:
time: 1260 us; the launch traced here: 1250 us
  Pallas kernels  740 us (59%)
  matrix products  293 us (23%)
  other arithmetic  86.3 us (7%)
  local copies, waits for them, and re-layouts  82.7 us (7%)
  starting transfers between devices  29.6 us (2%)
  between operations  15.7 us (1%)
    pallas_call x3, Pallas kernels, gather(): pl.pallas_call(functools.partial(gather_kernel, items, sizes), out_shape=...  310 us
    pallas_call x3, Pallas kernels, scatter(): pl.pallas_call(functools.partial(scatter_kernel, items, sizes), out_shape...  264 us
    dot_general x9, matrix products, transposed_left(): lax.dot_general(left, right, (((0,), (0,)), ((), ())), preferred_element_...  99.1 us
    dot_general x8, matrix products, transposed_right(): lax.dot_general(left, right, (((1,), (1,)), ((), ())), preferred_element_...  94.7 us
    pallas_call x1, Pallas kernels, attention_backward(): pl.pallas_call(functools.partial(attend_back_kernel, tokens, span, scale)...  88.6 us
    dot_general x8, matrix products, dot(): return jnp.dot(a, b, preferred_element_type=jnp.float32)  79.4 us
    pallas_call x2, Pallas kernels, combine(): pl.pallas_call(combine_kernel, grid=(groups,), out_shape=jax.ShapeDtypeSt...  40.3 us
    pallas_call x1, Pallas kernels, attention_forward(): pl.pallas_call(functools.partial(attend_kernel, tokens, span, scale), gri...  37.2 us
  transfers between devices with their start and end apart: 17, of which 0 were waited for; matrix products, arithmetic and copies ran while one was open for 32% of the time, Pallas kernels for 51%

profile of v3, /device:TPU:0, one launch (start us, length us, event | category | flops | bytes accessed | tf_op | source)
XLA Modules:
  0.0 1247.1 jit_solution(7358072413873931482)
XLA Ops:
  12.6 88.8 %shard_map.297 = (bf16[32,2,32,3072]{3,2,1,0:T(8,128)(2,1)}, bf16[32,64,576]{2,1,0:T(8,128)(2,1)}, bf16[32,16,4096]{2,1,0:T(8,128)(2,1)}, bf16[32,64,128]{2,1,0:T(8,128)(2,1)}) custom-call(bf16[2,32,3072]{2,1,0:T(8,128)(2,1)} %pad_maximum_fusion.15.refs_0_, bf16[64,576]{1,0:T(8,128)(2,1)} %refs_1_.1, bf16[16,4096]{1,0:T(8,128)(2,1)} %refs_2_.1, ...), custom_call_target="tpu_custom_call" | custom-call | bytes 117964800 | tf_op jit(solution)/shard_map/pallas_call | solution.py:276
  102.7 2.7 slice_convert_fusion.2
  107.4 2.9 fusion.93
  112.1 70.3 %shard_map.298 = (bf16[16,256,640]{2,1,0:T(8,128)(2,1)}, s32[16,8,256]{2,1,0:T(8,128)}) custom-call(bf16[256,640]{1,0:T(8,128)(2,1)} %maximum_maximum_fusion.refs_0_, s32[8,256]{1,0:T(8,128)} %pad.32.refs_1_), custom_call_target="tpu_custom_call" | custom-call | bytes 32243712 | tf_op jit(solution)/shard_map/pallas_call | solution.py:276
  182.5 4.4 collective-permute-start.4
  193.8 3.6 all-to-all-start
  197.7 2.0 collective-permute-start.1
  204.0 2.7 copy.168.bias
  207.0 6.8 fusion.92
  216.1 37.2 %shard_map.299 = bf16[256,2048]{1,0:T(8,128)(2,1)} custom-call(bf16[256,2048]{1,0:T(8,128)(2,1)} %slice.207.qn, bf16[256,512]{1,0:T(8,128)(2,1)} %get-tuple-element.226.qa, bf16[256,512]{1,0:T(8,128)(2,1)} %get-tuple-element.225.qb, bf16[16,256,640]{2,1,0:T(8,128)(2,1)} %get-tuple-element.71.line, bf16[512,4096]{1,0:T(8,128)(2,1)} %bitcast.274, ...), custom_call_target="tpu_custom_call" | custom-call | flops 24999999488 | bytes 20000000 | tf_op jit(solution)/shard_map/pallas_call | solution.py:737
  258.0 6.3 multiply_reduce_fusion.2
  266.9 151.2 %shard_map.300 = (bf16[16,4,64,2048]{3,2,1,0:T(8,128)(2,1)}, f32[16,16,256]{2,1,0:T(8,128)}) custom-call(bf16[4,64,2048]{2,1,0:T(8,128)(2,1)} %bitcast.218, f32[16,256]{1,0:T(8,128)} %fusion.81.refs_1_), custom_call_target="tpu_custom_call" | custom-call | bytes 102236160 | tf_op jit(solution)/shard_map/pallas_call | solution.py:276
  421.0 2.0 broadcast_select_fusion.9
  423.9 5.1 broadcast_select_fusion.5
  429.0 5.0 broadcast_select_fusion.3
  434.1 5.0 broadcast_select_fusion.1
  439.0 8.1 convolution_convert_fusion.10
  447.2 16.6 %convolution_convert_fusion.8 = bf16[4096,512]{1,0:T(8,128)(2,1)} fusion(bf16[4096,2048]{1,0:T(8,128)(2,1)} %bitcast.213, bf16[2048,512]{0,1:T(8,128)(2,1)S(1)} %bitcast.206), kind=kOutput, calls=%fused_computation.33 | convolution fusion | flops 8592031744 | bytes 23068672 | tf_op jit(solution)/shard_map/dot_general | solution.py:529
  463.8 13.2 %convolution_convert_fusion.6 = bf16[1792,1408]{1,0:T(8,128)(2,1)} fusion(bf16[1792,2048]{1,0:T(8,128)(2,1)S(1)} %bitcast.219, bf16[1024,1408]{1,0:T(8,128)(2,1)S(1)} %copy-done.34, bf16[1024,1408]{1,0:T(8,128)(2,1)S(1)} %copy-done.32), kind=kOutput, calls=%fused_computation.27 | convolution fusion | flops 10348822528 | bytes 18153472 | tf_op jit(solution)/shard_map/dot_general | solution.py:529
  477.1 13.7 %convolution_convert_fusion.5 = bf16[1792,1408]{1,0:T(8,128)(2,1)} fusion(bf16[1792,2048]{1,0:T(8,128)(2,1)S(1)} %bitcast.220, bf16[1024,1408]{1,0:T(8,128)(2,1)S(1)} %copy-done.31, bf16[1024,1408]{1,0:T(8,128)(2,1)S(1)} %copy-done.29), kind=kOutput, calls=%fused_computation.26 | convolution fusion | flops 10348822528 | bytes 18153472 | tf_op jit(solution)/shard_map/dot_general | solution.py:529
  490.8 11.3 convolution_convert_fusion.9
  502.0 18.9 %fusion.2 = (f32[1792]{0:T(1024)S(1)}, bf16[1792,2048]{1,0:T(8,128)(2,1)}) fusion(bf16[16,112,2048]{2,1,0:T(8,128)(2,1)} %convolution_convert_fusion.9, bf16[1408,1024]{1,0:T(8,128)(2,1)} %get-tuple-element.223, bf16[1408,1024]{1,0:T(8,128)(2,1)S(1)} %copy-done.36, bf16[1792,1408]{1,0:T(8,128)(2,1)} %convolution_convert_fusion.5, ...), kind=kOutput, calls=%fused_computation.9 | convolution fusion | flops 10384832512 | bytes 30546944 | tf_op jit(solution)/shard_map/dot_general | solution.py:529
  522.0 12.4 fusion.16
  534.5 10.9 fusion.1
  545.4 18.4 %shard_map.301 = bf16[4096,2048]{1,0:T(8,128)(2,1)} custom-call(bf16[16,256,112]{2,1,0:T(8,128)(2,1)S(1)} %copy-done, bf16[16,112,2048]{2,1,0:T(8,128)(2,1)} %bitcast.215, bf16[4096,256]{1,0:T(8,128)(2,1)S(1)} %get-tuple-element.224.left, bf16[256,2048]{1,0:T(8,128)(2,1)S(1)} %fusion.33.right), custom_call_target="tpu_custom_call" | custom-call | flops 6174015488 | bytes 33554432 | tf_op jit(solution)/shard_map/pallas_call | solution.py:807
  563.9 9.2 fusion.94
  575.4 14.0 %convolution_convert_fusion.12 = bf16[2048,512]{1,0:T(8,128)(2,1)S(1)} fusion(bf16[4096,2048]{1,0:T(8,128)(2,1)} %bitcast.214, bf16[4096,256]{1,0:T(8,128)(2,1)S(1)} %copy-done.44, bf16[4096,256]{1,0:T(8,128)(2,1)S(1)} %copy-done.42), kind=kOutput, calls=%fused_computation.58 | convolution fusion | flops 8599371776 | bytes 23068672 | tf_op jit(solution)/shard_map/dot_general | solution.py:72
  592.2 4.1 all-to-all-start.1
  596.4 19.5 %convolution_convert_fusion.7 = bf16[1408,2048]{1,0:T(8,128)(2,1)S(1)} fusion(bf16[1792,2048]{1,0:T(8,128)(2,1)} %get-tuple-element.255, bf16[1792,1408]{1,0:T(8,128)(2,1)} %convolution_convert_fusion.5, bf16[1792,1408]{1,0:T(8,128)(2,1)} %convolution_convert_fusion.6), kind=kOutput, calls=%fused_computation.28 | convolution fusion | flops 10357833728 | bytes 23199744 | tf_op jit(solution)/shard_map/dot_general | solution.py:72
  615.9 3.3 constant_dynamic-slice_fusion.4
  620.6 2.4 pad_maximum_fusion.3.left
  623.0 22.3 %fusion.9 = (bf16[1792,1408]{1,0:T(8,128)(2,1)}, f32[1792,1408]{1,0:T(8,128)}) fusion(bf16[1792,1408]{1,0:T(8,128)(2,1)} %convolution_convert_fusion.6, bf16[1792,1408]{1,0:T(8,128)(2,1)} %convolution_convert_fusion.5, bf16[1792,2048]{1,0:T(8,128)(2,1)} %get-tuple-element.255, bf16[1408,1024]{1,0:T(8,128)(2,1)} %get-tuple-element.223, ...), kind=kOutput, calls=%fused_computation.20 | convolution fusion | flops 10379100160 | bytes 38338560 | tf_op jit(solution)/shard_map/dot_general | solution.py:78
  645.3 17.2 %convolution_convert_fusion.3 = bf16[2048,1408]{1,0:T(8,128)(2,1)} fusion(bf16[1792,2048]{1,0:T(8,128)(2,1)} %bitcast.221, bf16[1792,1408]{1,0:T(8,128)(2,1)} %get-tuple-element.267), kind=kOutput, calls=%fused_computation.24 | convolution fusion | flops 10337648640 | bytes 18153472 | tf_op jit(solution)/shard_map/dot_general | solution.py:72
  662.6 14.5 %fusion.18 = f32[1792,2048]{1,0:T(8,128)} fusion(bf16[1792,1408]{1,0:T(8,128)(2,1)S(1)} %copy-done.91, bf16[1024,1408]{1,0:T(8,128)(2,1)S(1)} %copy-done.35, bf16[1024,1408]{1,0:T(8,128)(2,1)S(1)} %copy-done.33), kind=kOutput, calls=%fused_computation.54 | convolution fusion | flops 10346299392 | bytes 25493504 | tf_op jit(solution)/shard_map/dot_general | solution.py:78
  677.1 25.2 %add_convert_fusion = bf16[1792,2048]{1,0:T(8,128)(2,1)} fusion(f32[1792,2048]{1,0:T(8,128)} %fusion.18, bf16[1024,1408]{1,0:T(8,128)(2,1)} %get-tuple-element.221, bf16[1024,1408]{1,0:T(8,128)(2,1)S(1)} %copy-done.30, f32[1792,1408]{1,0:T(8,128)} %get-tuple-element.268, bf16[1792,1408]{1,0:T(8,128)(2,1)} %convolution_convert_fusion.6), kind=kOutput, calls=%fused_computation.10 | convolution fusion | flops 10371301376 | bytes 42926080 | tf_op jit(solution)/shard_map/dot_general | solution.py:78
  702.3 21.2 %convolution_convert_fusion.2 = bf16[2048,1408]{1,0:T(8,128)(2,1)} fusion(bf16[1792,2048]{1,0:T(8,128)(2,1)} %bitcast.222, f32[1792,1408]{1,0:T(8,128)} %get-tuple-element.268, bf16[1792,1408]{1,0:T(8,128)(2,1)} %convolution_convert_fusion.6), kind=kOutput, calls=%fused_computation.23 | convolution fusion | flops 10355310592 | bytes 28246016 | tf_op jit(solution)/shard_map/dot_general | solution.py:72
  723.5 21.9 %shard_map.302 = bf16[4096,2048]{1,0:T(8,128)(2,1)} custom-call(bf16[16,256,112]{2,1,0:T(8,128)(2,1)S(1)} %copy-done.1, bf16[16,112,2048]{2,1,0:T(8,128)(2,1)} %bitcast.276, bf16[4096,512]{1,0:T(8,128)(2,1)} %pad_maximum_fusion.3.left, bf16[512,2048]{1,0:T(8,128)(2,1)S(1)} %bitcast.207), custom_call_target="tpu_custom_call" | custom-call | flops 10468982784 | bytes 33554432 | tf_op jit(solution)/shard_map/pallas_call | solution.py:807
  745.4 91.2 %shard_map.303 = f32[4,64,2048]{2,1,0:T(8,128)} custom-call(bf16[16,4,64,2048]{3,2,1,0:T(8,128)(2,1)} %bitcast.217), custom_call_target="tpu_custom_call" | custom-call | tf_op jit(solution)/shard_map/pallas_call | solution.py:485
  837.5 3.7 multiply_reduce_fusion
  841.2 4.5 fusion.19
  845.8 5.6 convolution_convert_fusion.1
  851.4 5.5 constant_dynamic-slice_fusion.6
  857.4 5.8 constant_dynamic-slice_fusion.8
  866.7 6.9 convolution_convert_fusion.13.grad
  873.6 88.6 %shard_map.304 = (bf16[256,2048]{1,0:T(8,128)(2,1)}, f32[256,512]{1,0:T(8,128)}, f32[256,512]{1,0:T(8,128)}, bf16[16,256,640]{2,1,0:T(8,128)(2,1)}, bf16[512,4096]{1,0:T(8,128)(2,1)}) custom-call(bf16[256,2048]{1,0:T(8,128)(2,1)} %slice.207.qn, bf16[256,512]{1,0:T(8,128)(2,1)} %get-tuple-element.226.qa, bf16[256,512]{1,0:T(8,128)(2,1)} %get-tuple-element.225.qb, ...), custom_call_target="tpu_custom_call" | custom-call | flops 60000002048 | bytes 30000000 | tf_op jit(solution)/shard_map/pallas_call | solution.py:761
  963.7 8.0 convolution_convert_fusion
  971.7 142.8 %shard_map.305 = (f32[256,640]{1,0:T(8,128)}, f32[64,3072]{1,0:T(8,128)}, f32[16,4096]{1,0:T(8,128)}) custom-call(bf16[16,256,640]{2,1,0:T(8,128)(2,1)} %get-tuple-element.95.refs_0_, bf16[32,64,3072]{2,1,0:T(8,128)(2,1)} %bitcast.211, bf16[32,16,4096]{2,1,0:T(8,128)(2,1)} %bitcast.234), custom_call_target="tpu_custom_call" | custom-call | tf_op jit(solution)/shard_map/pallas_call | solution.py:485
  1114.7 2.9 add_convert_fusion.1
  1117.6 2.1 reshape.723
  1119.7 3.7 reshape.724
  1124.6 7.1 fusion.36
  1131.8 3.3 fusion.27
  1136.4 7.6 all-to-all-start.2
  1148.4 2.0 copy.187
  1154.2 2.6 pad_maximum_fusion.12
  1156.8 2.5 reshape.722
  1165.6 3.5 convolution_convert_fusion.11
  1169.0 4.3 copy.183
  1173.4 29.4 %shard_map.306 = (f32[64,576]{1,0:T(8,128)}, f32[64,128]{1,0:T(8,128)}) custom-call(bf16[32,64,576]{2,1,0:T(8,128)(2,1)} %bitcast.223, bf16[32,64,128]{2,1,0:T(8,128)(2,1)} %pad.36.refs_1_), custom_call_target="tpu_custom_call" | custom-call | tf_op jit(solution)/shard_map/pallas_call | solution.py:485
  1207.4 3.4 fusion.20
  1210.8 5.1 add_bitcast_fusion.2
  1215.9 5.1 add_bitcast_fusion.1
  1222.9 5.6 add_bitcast_fusion
  1228.5 3.6 reshape.734
  (339 shorter events, 80.5 us)
Async XLA Ops:
  7.2 94.3 %copy-start.86 = (s32[1,2,128,6]{2,1,3,0:T(2,128)S(1)}, s32[1,2,128,6]{2,1,3,0:T(2,128)}, u32[]{:S(2)}) copy-start(s32[1,2,128,6]{2,1,3,0:T(2,128)} %param.21) | copy-start | bytes 18436
  7.2 250.8 %all-gather.3.cloned.1.call-start = ((), (), s32[]{:S(2)}) async-start(), calls=%async_computation.5 | async-start | bytes 8650752 | tf_op jit(solution)/shard_map/all_gather | solution.py:906
  8.9 97.5 %copy-start.5 = (bf16[1,2,128,2048]{3,2,1,0:T(8,128)(2,1)S(1)}, bf16[1,2,128,2048]{3,2,1,0:T(8,128)(2,1)}, u32[]{:S(2)}) copy-start(bf16[1,2,128,2048]{3,2,1,0:T(8,128)(2,1)} %param.18) | copy-start | bytes 3145732
  101.4 389.3 %all-gather.5.cloned.1.call-start = ((), (), s32[]{:S(2)}) async-start(), calls=%async_computation.7 | async-start | bytes 17825792 | tf_op jit(solution)/shard_map/all_gather | solution.py:513
  105.7 100.9 %copy-start.64 = (f32[2048,1]{0,1:T(1,128)}, f32[2048,1]{0,1:T(1,128)S(1)}, u32[]{:S(2)}) copy-start(f32[2048,1]{0,1:T(1,128)S(1)} %copy.202) | copy-start | bytes 24580
  106.7 99.9 %copy-start.83 = (f32[2,128]{1,0:T(2,128)}, f32[2,128]{1,0:T(2,128)S(1)}, u32[]{:S(2)}) copy-start(f32[2,128]{1,0:T(2,128)S(1)} %fusion.28) | copy-start | bytes 3076
  107.1 93.1 %copy-start.50 = (f32[128,32]{1,0:T(8,128)}, f32[128,32]{1,0:T(8,128)S(1)}, u32[]{:S(2)}) copy-start(f32[128,32]{1,0:T(8,128)S(1)} %get-tuple-element.259) | copy-start | bytes 49156
  107.1 93.2 %copy-start.52 = (f32[128,32]{1,0:T(8,128)}, f32[128,32]{1,0:T(8,128)S(1)}, u32[]{:S(2)}) copy-start(f32[128,32]{1,0:T(8,128)S(1)} %get-tuple-element.260) | copy-start | bytes 49156
  107.4 79.4 %copy-start.61 = (bf16[64,2816]{1,0:T(8,128)(2,1)S(1)}, bf16[64,2816]{1,0:T(8,128)(2,1)}, u32[]{:S(2)}) copy-start(bf16[64,2816]{1,0:T(8,128)(2,1)} %param.30) | copy-start | bytes 1081348
  107.4 81.2 %copy-start.62 = (bf16[64,2816]{1,0:T(8,128)(2,1)S(1)}, bf16[64,2816]{1,0:T(8,128)(2,1)}, u32[]{:S(2)}) copy-start(bf16[64,2816]{1,0:T(8,128)(2,1)} %param.31) | copy-start | bytes 1081348
  110.6 81.6 %copy-start.85 = (f32[256]{0:T(256)}, f32[256]{0:T(256)S(1)}, u32[]{:S(2)}) copy-start(f32[256]{0:T(256)S(1)} %multiply_reduce_fusion.5) | copy-start | bytes 3076
  111.2 81.1 %copy-start.76 = (f32[256]{0:T(256)}, f32[256]{0:T(256)S(1)}, u32[]{:S(2)}) copy-start(f32[256]{0:T(256)S(1)} %fusion.67) | copy-start | bytes 3076
  182.5 236.6 %collective-permute-start.4 = (bf16[88,2048]{1,0:T(8,128)(2,1)}, bf16[88,2048]{1,0:T(8,128)(2,1)}, u32[]{:S(2)}, u32[]{:S(2)}) collective-permute-start(bf16[88,2048]{1,0:T(8,128)(2,1)} %param.32), channel_id=1, source_target_pairs={{0,16},{16,0},{1,17},{17,1},{2,18},{18,2},{3,19},{19,3},{4,20},{20... | collective-permute-start | bytes 1081352 | tf_op jit(solution)/shard_map/ppermute | solution.py:535
  188.1 11.7 copy-start.90
  193.8 61.9 %all-to-all-start = ((bf16[16,64,352]{2,1,0:T(8,128)(2,1)}), bf16[16,64,352]{2,1,0:T(8,128)(2,1)S(1)}, u32[]{:S(2)}, u32[]{:S(2)}) async-start(bf16[16,64,352]{2,1,0:T(8,128)(2,1)} %reshape.701), calls=%async_computation | async-start | bytes 1572864 | tf_op jit(solution)/shard_map/all_to_all | solution.py:914
  197.4 643.8 %reduce-scatter.3.cloned.1.call-start = ((), (), s32[]{:S(2)}) async-start(), calls=%async_computation.6 | async-start | bytes 17825792 | tf_op jit(solution)/shard_map/reduce_scatter | solution.py:517
  197.6 221.4 %collective-permute-start = (bf16[1024,1408]{1,0:T(8,128)(2,1)}, bf16[1024,1408]{1,0:T(8,128)(2,1)}, u32[]{:S(2)}, u32[]{:S(2)}) collective-permute-start(bf16[1024,1408]{1,0:T(8,128)(2,1)} %bitcast.235), channel_id=1, source_target_pairs={{0,16},{16,0},{1,17},{17,1},{2,18},{18,2},{3,19},{19,3},{4,20},{20... | collective-permute-start | bytes 8650760 | tf_op jit(solution)/shard_map/ppermute | solution.py:535
  197.7 221.4 %collective-permute-start.1 = (bf16[1024,1408]{1,0:T(8,128)(2,1)}, bf16[1024,1408]{1,0:T(8,128)(2,1)}, u32[]{:S(2)}, u32[]{:S(2)}) collective-permute-start(bf16[1024,1408]{1,0:T(8,128)(2,1)} %bitcast.237), channel_id=1, source_target_pairs={{0,16},{16,0},{1,17},{17,1},{2,18},{18,2},{3,19},{19,3},{4,20},{20... | collective-permute-start | bytes 8650760 | tf_op jit(solution)/shard_map/ppermute | solution.py:535
  199.8 219.3 %collective-permute-start.2 = (bf16[1408,1024]{1,0:T(8,128)(2,1)}, bf16[1408,1024]{1,0:T(8,128)(2,1)}, u32[]{:S(2)}, u32[]{:S(2)}) collective-permute-start(bf16[1408,1024]{1,0:T(8,128)(2,1)} %bitcast.239), channel_id=1, source_target_pairs={{0,16},{16,0},{1,17},{17,1},{2,18},{18,2},{3,19},{19,3},{4,20},{20... | collective-permute-start | bytes 8650760 | tf_op jit(solution)/shard_map/ppermute | solution.py:535
  200.6 14.4 %copy-start.21 = (f32[256,512]{1,0:T(8,128)}, f32[256,512]{1,0:T(8,128)S(1)}, u32[]{:S(2)}) copy-start(f32[256,512]{1,0:T(8,128)S(1)} %copy.162) | copy-start | bytes 1572868
  200.9 14.1 %copy-start.23 = (f32[256,512]{1,0:T(8,128)}, f32[256,512]{1,0:T(8,128)S(1)}, u32[]{:S(2)}) copy-start(f32[256,512]{1,0:T(8,128)S(1)} %copy.160) | copy-start | bytes 1572868
  216.1 37.2 %copy-start.67 = (s32[16,8,256]{2,1,0:T(8,128)S(1)}, s32[16,8,256]{2,1,0:T(8,128)}, u32[]{:S(2)}) copy-start(s32[16,8,256]{2,1,0:T(8,128)} %get-tuple-element.74) | copy-start | bytes 393220
  216.1 37.3 %copy-start.25 = (f32[2048,1]{1,0:T(8,128)S(1)}, f32[2048,1]{1,0:T(8,128)}, u32[]{:S(2)}) copy-start(f32[2048,1]{1,0:T(8,128)} %get-tuple-element.247) | copy-start | bytes 24580
  255.9 163.1 %collective-permute-start.3 = (bf16[1024,352]{0,1:T(8,128)(2,1)S(1)}, bf16[1024,352]{0,1:T(8,128)(2,1)S(1)}, u32[]{:S(2)}, u32[]{:S(2)}) collective-permute-start(bf16[1024,352]{0,1:T(8,128)(2,1)S(1)} %copy.172), channel_id=1, source_target_pairs={{0,16},{16,0},{1,17},{17,1},{2,18},{18,2},{3,19},{19,3},{4,20},{20... | collective-permute-start | bytes 2162696 | tf_op jit(solution)/shard_map/ppermute | solution.py:535
  266.2 151.9 %copy-start.70 = (f32[256]{0:T(256)}, f32[256]{0:T(256)S(1)}, u32[]{:S(2)}) copy-start(f32[256]{0:T(256)S(1)} %get-tuple-element.263) | copy-start | bytes 3076
  266.2 153.6 %copy-start.59 = (f32[256,16]{0,1:T(8,128)}, f32[256,16]{0,1:T(8,128)S(1)}, u32[]{:S(2)}) copy-start(f32[256,16]{0,1:T(8,128)S(1)} %get-tuple-element.264) | copy-start | bytes 49156
  266.3 151.8 %copy-start.74 = (f32[256]{0:T(256)}, f32[256]{0:T(256)S(1)}, u32[]{:S(2)}) copy-start(f32[256]{0:T(256)S(1)} %fusion.62) | copy-start | bytes 3076
  421.0 26.1 %copy-start.2 = (bf16[2048,2,256]{0,2,1:T(8,128)(2,1)}, bf16[2048,2,256]{0,2,1:T(8,128)(2,1)S(1)}, u32[]{:S(2)}) copy-start(bf16[2048,2,256]{0,2,1:T(8,128)(2,1)S(1)} %pad.33) | copy-start | bytes 6291460
  447.1 29.9 %copy-start.11 = (bf16[16,112,2048]{2,1,0:T(8,128)(2,1)}, bf16[16,112,2048]{2,1,0:T(8,128)(2,1)S(1)}, u32[]{:S(2)}) copy-start(bf16[16,112,2048]{2,1,0:T(8,128)(2,1)S(1)} %convolution_convert_fusion.10) | copy-start | bytes 22020100
  447.2 16.6 %copy-start.32 = (bf16[1024,1408]{1,0:T(8,128)(2,1)S(1)}, bf16[1024,1408]{1,0:T(8,128)(2,1)}, u32[]{:S(2)}) copy-start(bf16[1024,1408]{1,0:T(8,128)(2,1)} %get-tuple-element.218) | copy-start | bytes 8650756
  447.2 16.6 %copy-start.34 = (bf16[1024,1408]{1,0:T(8,128)(2,1)S(1)}, bf16[1024,1408]{1,0:T(8,128)(2,1)}, u32[]{:S(2)}) copy-start(bf16[1024,1408]{1,0:T(8,128)(2,1)} %get-tuple-element.219) | copy-start | bytes 8650756
  463.8 13.3 %copy-start.29 = (bf16[1024,1408]{1,0:T(8,128)(2,1)S(1)}, bf16[1024,1408]{1,0:T(8,128)(2,1)}, u32[]{:S(2)}) copy-start(bf16[1024,1408]{1,0:T(8,128)(2,1)} %get-tuple-element.220) | copy-start | bytes 8650756
  463.8 13.3 %copy-start.31 = (bf16[1024,1408]{1,0:T(8,128)(2,1)S(1)}, bf16[1024,1408]{1,0:T(8,128)(2,1)}, u32[]{:S(2)}) copy-start(bf16[1024,1408]{1,0:T(8,128)(2,1)} %get-tuple-element.221) | copy-start | bytes 8650756
  522.0 12.5 copy-start.4
  574.1 540.6 %collective-permute-start.8 = (bf16[88,2048]{1,0:T(8,128)(2,1)}, bf16[88,2048]{1,0:T(8,128)(2,1)}, u32[]{:S(2)}, u32[]{:S(2)}) collective-permute-start(bf16[88,2048]{1,0:T(8,128)(2,1)} %get-tuple-element.243), channel_id=1, source_target_pairs={{0,16},{16,0},{1,17},{17,1},{2,18},{18,2},{3,19},{19,3},{4,20},{20... | collective-permute-start | bytes 1081352 | tf_op jit(solution)/shard_map/ppermute | solution.py:555
  590.9 523.7 %collective-permute-start.9 = (bf16[1024,512]{1,0:T(8,128)(2,1)}, bf16[1024,512]{1,0:T(8,128)(2,1)}, u32[]{:S(2)}, u32[]{:S(2)}) collective-permute-start(bf16[1024,512]{1,0:T(8,128)(2,1)} %get-tuple-element.229), channel_id=1, source_target_pairs={{0,16},{16,0},{1,17},{17,1},{2,18},{18,2},{3,19},{19,3},{4,20},{20... | collective-permute-start | bytes 3145736 | tf_op jit(solution)/shard_map/ppermute | solution.py:555
  592.2 244.5 %all-to-all-start.1 = ((f32[16,1,256]{2,1,0:T(1,128)}), f32[16,1,256]{2,1,0:T(1,128)}, u32[]{:S(2)}, u32[]{:S(2)}) async-start(f32[16,1,256]{2,1,0:T(1,128)} %all_to_all.15), calls=%async_computation.2 | async-start | bytes 32768 | tf_op jit(solution)/shard_map/all_to_all | solution.py:1036
  596.3 640.7 %reduce-scatter.5.cloned.1.call-start = ((), (), s32[]{:S(2)}) async-start(), calls=%async_computation.8 | async-start | bytes 8650752 | tf_op jit(solution)/shard_map/reduce_scatter | solution.py:1081
  619.2 495.5 %collective-permute-start.7 = (bf16[1408,1024]{1,0:T(8,128)(2,1)}, bf16[1408,1024]{1,0:T(8,128)(2,1)}, u32[]{:S(2)}, u32[]{:S(2)}) collective-permute-start(bf16[1408,1024]{1,0:T(8,128)(2,1)} %get-tuple-element.212), channel_id=1, source_target_pairs={{0,16},{16,0},{1,17},{17,1},{2,18},{18,2},{3,19},{19,3},{4,20},{20... | collective-permute-start | bytes 8650760 | tf_op jit(solution)/shard_map/ppermute | solution.py:555
  645.3 17.3 %copy-start.33 = (bf16[1024,1408]{1,0:T(8,128)(2,1)S(1)}, bf16[1024,1408]{1,0:T(8,128)(2,1)}, u32[]{:S(2)}) copy-start(bf16[1024,1408]{1,0:T(8,128)(2,1)} %get-tuple-element.218) | copy-start | bytes 8650756
  645.3 17.3 %copy-start.35 = (bf16[1024,1408]{1,0:T(8,128)(2,1)S(1)}, bf16[1024,1408]{1,0:T(8,128)(2,1)}, u32[]{:S(2)}) copy-start(bf16[1024,1408]{1,0:T(8,128)(2,1)} %get-tuple-element.219) | copy-start | bytes 8650756
  645.3 17.3 %copy-start.91 = (bf16[1792,1408]{1,0:T(8,128)(2,1)S(1)}, bf16[1792,1408]{1,0:T(8,128)(2,1)}, u32[]{:S(2)}) copy-start(bf16[1792,1408]{1,0:T(8,128)(2,1)} %get-tuple-element.267) | copy-start | bytes 15138820
  662.6 14.5 %copy-start.30 = (bf16[1024,1408]{1,0:T(8,128)(2,1)S(1)}, bf16[1024,1408]{1,0:T(8,128)(2,1)}, u32[]{:S(2)}) copy-start(bf16[1024,1408]{1,0:T(8,128)(2,1)} %get-tuple-element.220) | copy-start | bytes 8650756
  702.3 21.2 %copy-start.1 = (bf16[16,256,112]{2,1,0:T(8,128)(2,1)S(1)}, bf16[16,256,112]{2,1,0:T(8,128)(2,1)}, u32[]{:S(2)}) copy-start(bf16[16,256,112]{2,1,0:T(8,128)(2,1)} %fusion.32.picked) | copy-start | bytes 2752516
  702.3 21.2 %copy-start.3 = (bf16[2048,2,256]{0,2,1:T(8,128)(2,1)S(1)}, bf16[2048,2,256]{0,2,1:T(8,128)(2,1)}, u32[]{:S(2)}) copy-start(bf16[2048,2,256]{0,2,1:T(8,128)(2,1)} %copy-done.2) | copy-start | bytes 6291460
  745.4 91.3 %copy-start.60 = (f32[256,16]{0,1:T(8,128)S(1)}, f32[256,16]{0,1:T(8,128)}, u32[]{:S(2)}) copy-start(f32[256,16]{0,1:T(8,128)} %copy-done.59) | copy-start | bytes 49156
  745.4 91.3 %copy-start.71 = (f32[256]{0:T(256)S(1)}, f32[256]{0:T(256)}, u32[]{:S(2)}) copy-start(f32[256]{0:T(256)} %copy-done.70) | copy-start | bytes 3076
  745.4 91.3 %copy-start.75 = (f32[256]{0:T(256)S(1)}, f32[256]{0:T(256)}, u32[]{:S(2)}) copy-start(f32[256]{0:T(256)} %copy-done.74) | copy-start | bytes 3076
  745.4 92.1 %copy-start.8 = (f32[256,2048]{1,0:T(8,128)S(1)}, f32[256,2048]{1,0:T(8,128)}, u32[]{:S(2)}) copy-start(f32[256,2048]{1,0:T(8,128)} %copy-done.7) | copy-start | bytes 6291460
  745.4 92.1 %copy-start.18 = (bf16[32,64,128]{2,1,0:T(8,128)(2,1)S(1)}, bf16[32,64,128]{2,1,0:T(8,128)(2,1)}, u32[]{:S(2)}) copy-start(bf16[32,64,128]{2,1,0:T(8,128)(2,1)} %get-tuple-element.66) | copy-start | bytes 1572868
  745.4 92.1 %copy-start.69 = (f32[2048,1]{0,1:T(1,128)S(1)}, f32[2048,1]{0,1:T(1,128)}, u32[]{:S(2)}) copy-start(f32[2048,1]{0,1:T(1,128)} %copy-done.68) | copy-start | bytes 24580
  745.4 92.1 %copy-start.82 = (f32[256]{0:T(256)S(1)}, f32[256]{0:T(256)}, u32[]{:S(2)}) copy-start(f32[256]{0:T(256)} %copy-done.81) | copy-start | bytes 3076
  856.9 257.8 %collective-permute-start.6 = (bf16[1024,1408]{1,0:T(8,128)(2,1)}, bf16[1024,1408]{1,0:T(8,128)(2,1)}, u32[]{:S(2)}, u32[]{:S(2)}) collective-permute-start(bf16[1024,1408]{1,0:T(8,128)(2,1)} %get-tuple-element.214), channel_id=1, source_target_pairs={{0,16},{16,0},{1,17},{17,1},{2,18},{18,2},{3,19},{19,3},{4,20},{20... | collective-permute-start | bytes 8650760 | tf_op jit(solution)/shard_map/ppermute | solution.py:555
  863.2 251.5 %collective-permute-start.5 = (bf16[1024,1408]{1,0:T(8,128)(2,1)}, bf16[1024,1408]{1,0:T(8,128)(2,1)}, u32[]{:S(2)}, u32[]{:S(2)}) collective-permute-start(bf16[1024,1408]{1,0:T(8,128)(2,1)} %get-tuple-element.216), channel_id=1, source_target_pairs={{0,16},{16,0},{1,17},{17,1},{2,18},{18,2},{3,19},{19,3},{4,20},{20... | collective-permute-start | bytes 8650760 | tf_op jit(solution)/shard_map/ppermute | solution.py:555
  873.6 88.7 %copy-start.22 = (f32[256,512]{1,0:T(8,128)S(1)}, f32[256,512]{1,0:T(8,128)}, u32[]{:S(2)}) copy-start(f32[256,512]{1,0:T(8,128)} %copy-done.21) | copy-start | bytes 1572868
  873.6 88.7 %copy-start.24 = (f32[256,512]{1,0:T(8,128)S(1)}, f32[256,512]{1,0:T(8,128)}, u32[]{:S(2)}) copy-start(f32[256,512]{1,0:T(8,128)} %copy-done.23) | copy-start | bytes 1572868
  873.6 90.2 %copy-start.13 = (bf16[256,2048]{1,0:T(8,128)(2,1)S(1)}, bf16[256,2048]{1,0:T(8,128)(2,1)}, u32[]{:S(2)}) copy-start(bf16[256,2048]{1,0:T(8,128)(2,1)} %copy-done.12) | copy-start | bytes 3145732
  1136.4 92.2 %all-to-all-start.2 = ((bf16[16,64,352]{2,1,0:T(8,128)(2,1)}), bf16[16,64,352]{2,1,0:T(8,128)(2,1)}, u32[]{:S(2)}, u32[]{:S(2)}) async-start(bf16[16,64,352]{2,1,0:T(8,128)(2,1)} %reshape.724), calls=%async_computation.4 | async-start | bytes 1572864 | tf_op jit(solution)/shard_map/all_to_all | solution.py:1117
  1148.4 17.1 %copy-start.41 = (bf16[256,512]{1,0:T(8,128)(2,1)S(1)}, bf16[256,512]{1,0:T(8,128)(2,1)}, u32[]{:S(2)}) copy-start(bf16[256,512]{1,0:T(8,128)(2,1)} %copy-done.40) | copy-start | bytes 786436
  1148.4 17.1 %copy-start.56 = (bf16[256,32]{1,0:T(8,128)(2,1)S(1)}, bf16[256,32]{1,0:T(8,128)(2,1)}, u32[]{:S(2)}) copy-start(bf16[256,32]{1,0:T(8,128)(2,1)} %copy-done.55) | copy-start | bytes 49156
  1148.4 17.1 %copy-start.58 = (bf16[256,32]{1,0:T(8,128)(2,1)S(1)}, bf16[256,32]{1,0:T(8,128)(2,1)}, u32[]{:S(2)}) copy-start(bf16[256,32]{1,0:T(8,128)(2,1)} %copy-done.57) | copy-start | bytes 49156
  1169.0 38.3 %copy-start.84 = (f32[2,128]{1,0:T(2,128)S(1)}, f32[2,128]{1,0:T(2,128)}, u32[]{:S(2)}) copy-start(f32[2,128]{1,0:T(2,128)} %copy-done.83) | copy-start | bytes 3076
  1169.0 38.3 %copy-start.87 = (f32[256]{0:T(256)S(1)}, f32[256]{0:T(256)}, u32[]{:S(2)}) copy-start(f32[256]{0:T(256)} %get-tuple-element.199) | copy-start | bytes 3076
  1169.0 38.3 %copy-start.80 = (f32[256]{0:T(256)S(1)}, f32[256]{0:T(256)}, u32[]{:S(2)}) copy-start(f32[256]{0:T(256)} %copy-done.78) | copy-start | bytes 3076
  (45 other events, 293.2 us)
Sparse Core Ops, SparseCore 0:
  101.5 85.9 all-gather.2
  189.7 174.6 all-gather.4
  564.0 177.0 reduce-scatter.2
  851.5 166.0 reduce-scatter.4

commit v4 on v3

--- a/solution.py
+++ b/solution.py
@@ -282,7 +282,7 @@
         + [pltpu.SemaphoreType.DMA((count_sends(order, sizes),)) for _, _, order in items]
         + [pltpu.SemaphoreType.DMA((totals[a],)) for a, _, _ in items],
         compiler_params=pltpu.CompilerParams(collective_id=identity, has_side_effects=True),
-        cost_estimate=pl.CostEstimate(flops=0, bytes_accessed=sent * 6, transcendentals=0),
+        cost_estimate=pl.CostEstimate(flops=0, bytes_accessed=sent // 16, transcendentals=0),
     )(*arrays)
 
 
@@ -506,7 +506,7 @@
 CHUNKS = 4
 CHUNK_ORDERS = [PLANE, PLANE, PLANE, YZ]
 YZX = ("y", "z", "x", "c")
-ALL_ORDERS = [[ZYX, ZXY], YZX, XYZ, XYZ]
+ALL_ORDERS = [[ZYX, ZXY], XYZ, XYZ, [ZXY, ZYX], XYZ]
 
 
 def gather_plane(x):
@@ -747,7 +747,7 @@
         ],
         compiler_params=pltpu.CompilerParams(vmem_limit_bytes=56 << 20),
         cost_estimate=pl.CostEstimate(
-            flops=25 * 10**9, bytes_accessed=20 * 10**6, transcendentals=0
+            flops=10**9, bytes_accessed=10**6, transcendentals=0
         ),
     )(qn, qa, qb, line, expand, bias)
 
@@ -790,32 +790,29 @@
     )(qn, qa, qb, grad, line, expand, bias)
 
 
-def combine_kernel(picked, rows, left, right, out, below):
-    inner = right.shape[0]
-
-    @pl.when(pl.program_id(0) == 0)
-    def _():
-        below[pl.ds(0, inner), :] = right[...]
-
-    below[pl.ds(inner, rows.shape[1]), :] = rows[0]
-    out[...] = low(dot(jnp.concatenate([left[...], picked[0]], axis=1), below[...]))
+def combine_kernel(picked, rows, left, right, out):
+    beside = dot(left[...], right[...])
+    height = picked.shape[1]
+    for i in range(picked.shape[0]):
+        part = slice(i * height, (i + 1) * height)
+        out[part, :] = low(beside[part, :] + dot(picked[i], rows[i]))
 
 
 def combine(picked, rows, left, right):
     groups, group_rows, slots = picked.shape
     total, inner = left.shape
+    step = 2 if groups % 2 == 0 else 1
     return pl.pallas_call(
         combine_kernel,
-        grid=(groups,),
+        grid=(groups // step,),
         out_shape=jax.ShapeDtypeStruct((total, D), jnp.bfloat16),
         in_specs=[
-            pl.BlockSpec((1, group_rows, slots), lambda g: (g, 0, 0)),
-            pl.BlockSpec((1, slots, D), lambda g: (g, 0, 0)),
-            pl.BlockSpec((group_rows, inner), lambda g: (g, 0)),
+            pl.BlockSpec((step, group_rows, slots), lambda g: (g, 0, 0)),
+            pl.BlockSpec((step, slots, D), lambda g: (g, 0, 0)),
+            pl.BlockSpec((step * group_rows, inner), lambda g: (g, 0)),
             pl.BlockSpec((inner, D), lambda g: (0, 0)),
         ],
-        out_specs=pl.BlockSpec((group_rows, D), lambda g: (g, 0)),
-        scratch_shapes=[pltpu.VMEM((inner + slots, D), jnp.bfloat16)],
+        out_specs=pl.BlockSpec((step * group_rows, D), lambda g: (g, 0)),
         compiler_params=pltpu.CompilerParams(vmem_limit_bytes=48 << 20),
         cost_estimate=pl.CostEstimate(
             flops=2 * total * (slots + inner) * D,
@@ -882,14 +879,21 @@
         ],
         axis=1,
     )
-    all_query, all_latent, all_expand, small = gather(
-        [halves_of(split_query), latent_weight, expand_weight.reshape(16, -1), small],
+    all_query, all_latent, all_expand, all_output, small = gather(
+        [
+            halves_of(split_query),
+            latent_weight,
+            expand_weight.reshape(16, -1),
+            halves_of(output_weight.T),
+            small,
+        ],
         ALL_ORDERS,
         1,
     )
     all_query = all_query.reshape(D, key_width)
     all_latent = all_latent.reshape(D, LAT + ROPE)
     all_expand = all_expand.reshape(LAT, H * (NOPE + VDIM))
+    all_output = all_output.reshape(D, H * VDIM)
     gain_latent = small[:, :small_latent, experts_count + 2].reshape(LAT).astype(jnp.float32)
     small = small.reshape(D, 128)
     all_router = small[:, :experts_count]
@@ -898,12 +902,11 @@
 
     (later, all_query) = lax.optimization_barrier(
         (
-            (expert_gate, expert_up, expert_down, shared_gate, shared_up, shared_down, output_weight),
+            (expert_gate, expert_up, expert_down, shared_gate, shared_up, shared_down),
             all_query,
         )
     )
-    expert_gate, expert_up, expert_down, shared_gate, shared_up, shared_down, output_weight = later
-    all_output = lax.all_gather(output_weight.T, ("dp", "expert"), axis=0, tiled=True)
+    expert_gate, expert_up, expert_down, shared_gate, shared_up, shared_down = later
     parts_gate = fetch_dp(expert_gate[0], 0)
     parts_up = fetch_dp(expert_up[0], 0)
     parts_down = fetch_dp(expert_down[0], 1)
@@ -931,7 +934,9 @@
     )
     columns = jnp.pad(routes[0].reshape(rows, TOP).T, ((0, 8 - TOP), (0, 0)))
     line, all_routes = gather([payload, columns], [PLANE, PLANE], 2)
-    sent_cotangent, line = lax.optimization_barrier((cotangent, line))
+    cotangent_rows = cotangent[0].reshape(rows, D)
+    first_half, line = lax.optimization_barrier((cotangent_rows[:, : D // 2], line))
+    first_half = gather_plane(first_half).reshape(n_expert * rows, D // 2)
     query = dot(hidden, all_query)
     plain = H * NOPE
     half = H * ROPE // 2
@@ -976,7 +981,10 @@
     all_normed, all_probs = gather([chunked, own_probs.T], [CHUNK_ORDERS, PLANE], 3)
     all_normed = all_normed.reshape(n_expert * rows, D)
     fetched = (parts_gate, parts_up, parts_down, parts_in, parts_out)
-    all_normed, fetched = lax.optimization_barrier((all_normed, fetched))
+    second_half, all_normed = lax.optimization_barrier((cotangent_rows[:, D // 2 :], all_normed))
+    fetched = [lax.optimization_barrier((pair, all_normed))[0] for pair in fetched]
+    second_half = gather_plane(second_half).reshape(n_expert * rows, D // 2)
+    cotangent_halves = (first_half, second_half)
     expert_gate, expert_up = joined(fetched[0], 0), joined(fetched[1], 0)
     expert_down = joined(fetched[2], 1)
     padded = -(-mine // 128) * 128
@@ -984,7 +992,6 @@
         joined(fetched[3], 0).reshape(D, 2, mine), ((0, 0), (0, 0), (0, padded - mine))
     ).reshape(D, 2 * padded)
     shared_out_weight = jnp.pad(joined(fetched[4], 0), ((0, padded - mine), (0, 0)))
-    all_cotangent = gather_plane(sent_cotangent[0].reshape(rows, D)).reshape(n_expert * rows, D)
     total_rows = n_expert * rows
     capacity = (9 * tokens * TOP + 8 * experts_count - 1) // (8 * experts_count)
     per_group = max(1, 256 // tokens)
@@ -1010,16 +1017,16 @@
             jnp.einsum(
                 "gst,gtd->gsd",
                 picked,
-                x.reshape(groups, group_rows, D),
+                x.reshape(groups, group_rows, x.shape[1]),
                 preferred_element_type=jnp.float32,
             )
-        ).reshape(groups * slots, D)
+        ).reshape(groups * slots, x.shape[1])
 
     arrived = to_slots(all_normed)
     gate_pre = low(dot(arrived, expert_gate))
     up_pre = low(dot(arrived, expert_up))
     expert_act = low(silu_product(wide(gate_pre), wide(up_pre)))
-    expert_out = low(dot(expert_act, expert_down))
+    expert_out = lax.optimization_barrier(low(dot(expert_act, expert_down)))
     shared_act = low(silu_product(wide(shared_pre[:, :padded]), wide(shared_pre[:, padded:])))
     spread = jnp.swapaxes(picked, 1, 2)
     partial_out = combine(
@@ -1028,7 +1035,7 @@
     expert_sum = scatter_plane(partial_out.reshape(n_expert, rows, D))
     layer_output = low(residual + expert_sum.astype(jnp.float32))
 
-    arrived_grad = to_slots(all_cotangent)
+    arrived_grad = jnp.concatenate([to_slots(x) for x in cotangent_halves], axis=1)
     gate_dots = jnp.sum(
         expert_out.astype(jnp.float32) * arrived_grad.astype(jnp.float32), axis=1
     ).reshape(groups, slots, 1)
@@ -1052,7 +1059,8 @@
         silu_back(
             wide(shared_pre[:, :padded]),
             wide(shared_pre[:, padded:]),
-            transposed_right(all_cotangent, shared_out_weight),
+            transposed_right(cotangent_halves[0], shared_out_weight[:, : D // 2])
+            + transposed_right(cotangent_halves[1], shared_out_weight[:, D // 2 :]),
         ),
         axis=1,
     ).astype(jnp.bfloat16)
@@ -1064,21 +1072,31 @@
         send_dp(expert_gate_grad, 0),
         send_dp(expert_up_grad, 0),
         send_dp(expert_down_grad, 1),
-        send_dp(low(transposed_left(shared_act, all_cotangent)[:mine]), 0),
+        send_dp(
+            jnp.concatenate(
+                [low(transposed_left(shared_act, x)[:mine]) for x in cotangent_halves], axis=1
+            ),
+            0,
+        ),
         send_dp(low(transposed_left(all_normed, shared_back)), 0),
     ]
 
     logit_grad = low(
         own_probs * (gate_grads - jnp.sum(gate_grads * own_probs, axis=-1, keepdims=True))
     )
-    router_weight_grad = transposed_left(normed, logit_grad)
+    wide_logits = jnp.pad(logit_grad, ((0, 0), (0, 128 - experts_count)))
+    router_weight_grad = transposed_left(normed, wide_logits)
     grad_normed = grad_normed + transposed_right(logit_grad, all_router)
     residual_extra, feed_gain_grad = normalize_back(residual, gain_second, grad_normed)
     grad_residual = cotangent[0].reshape(rows, D).astype(jnp.float32) + residual_extra
 
     grad_attn = low(grad_residual)
     output_grad = low(transposed_left(grad_attn, mixture))
-    output_grad = lax.psum_scatter(output_grad, ("dp", "expert"), scatter_dimension=0, tiled=True)
+    middle = output_grad.shape[1] // 2
+    later_grad = output_grad[:, middle:].reshape(devices, shard, middle)
+    output_grad = lax.psum_scatter(
+        output_grad[:, :middle], ("dp", "expert"), scatter_dimension=0, tiled=True
+    )
     grad_mixture = low(dot(grad_attn, all_output))
     grad_plain, grad_first, grad_second, grad_line, expand_grad = attention_backward(
         tokens,
@@ -1138,21 +1156,18 @@
     input_extra, attention_gain_grad = normalize_back(inputs, gain_first, grad_hidden)
     input_grad = grad_residual + input_extra
 
-    small_grad = jnp.concatenate(
-        [
-            router_weight_grad,
-            attention_gain_grad[:, None],
-            feed_gain_grad[:, None],
-        ],
-        axis=1,
-    ).reshape(devices, shard, experts_count + 2)
-    latent_column = jnp.pad(
+    column = jnp.arange(128, dtype=jnp.int32)[None, :]
+    latent_rows = jnp.pad(
         latent_gain_grad.reshape(devices, small_latent), ((0, 0), (0, shard - small_latent))
-    )[:, :, None]
-    small_grad = jnp.concatenate([small_grad, latent_column], axis=2)
-    small_grad = jnp.pad(small_grad, ((0, 0), (0, 0), (0, 128 - small_grad.shape[2])))
-    latent_grad, small_grad = scatter(
-        [low(latent_grad).reshape(devices, shard, LAT + ROPE), low(small_grad)], [ZYX, ZXY], 6
+    ).reshape(D)
+    small_grad = router_weight_grad
+    for place, vector in enumerate((attention_gain_grad, feed_gain_grad, latent_rows)):
+        small_grad = jnp.where(column == experts_count + place, vector[:, None], small_grad)
+    small_grad = small_grad.reshape(devices, shard, 128)
+    latent_grad, small_grad, later_grad = scatter(
+        [low(latent_grad).reshape(devices, shard, LAT + ROPE), low(small_grad), later_grad],
+        [ZYX, XYZ, ZXY],
+        6,
     )
     query_grad = jnp.concatenate(
         [
@@ -1170,7 +1185,7 @@
         latent_grad,
         small_grad[:small_latent, experts_count + 2],
         expand_grad.reshape(expand_weight.shape),
-        wide(output_grad).T,
+        jnp.concatenate([wide(output_grad), later_grad], axis=1).T,
         small_grad[:, experts_count + 1],
         small_grad[:, :experts_count],
         shared_in_grad[0],

time: 1260 us -> 1200 us (0.952)
  Pallas kernels: 740 us -> 672 us
  waiting for transfers between devices: 0.12 us -> 17.6 us
    pallas_call x3, Pallas kernels: 310 us -> 264 us  [gather(): pl.pallas_call(functools.partial(gather_kernel, items, sizes), out_shape=...]
    ppermute x5, waiting for transfers between devices: 0.01 us -> 17.4 us  [fetch_dp(): return (x, lax.ppermute(x, 'dp', [(0, 1), (1, 0)]))]
    pallas_call x3, Pallas kernels: 264 us -> 249 us  [scatter(): pl.pallas_call(functools.partial(scatter_kernel, items, sizes), out_shape...]
    dot_general x8 -> x9, matrix products: 94.7 us -> 90.1 us  [transposed_right(): lax.dot_general(left, right, (((1,), (1,)), ((), ())), preferred_element_...]
    dot_general x9 -> x10, matrix products: 99.1 us -> 95.1 us  [transposed_left(): lax.dot_general(left, right, (((0,), (0,)), ((), ())), preferred_element_...]
  transfers between devices with their start and end apart: 17 -> 17, of which waited for: 0 -> 1; matrix products, arithmetic and copies ran while one was open for 32% -> 33% of each run, Pallas kernels for 51% -> 41%
where the time goes in v4:
time: 1200 us; the launch traced here: 1190 us
  Pallas kernels  672 us (56%)
  matrix products  284 us (24%)
  other arithmetic  94.8 us (8%)
  local copies, waits for them, and re-layouts  78.8 us (7%)
  starting transfers between devices  31.4 us (3%)
  waiting for transfers between devices  17.6 us (1%)
  between operations  15.6 us (1%)
    pallas_call x3, Pallas kernels, gather(): pl.pallas_call(functools.partial(gather_kernel, items, sizes), out_shape=...  264 us
    pallas_call x3, Pallas kernels, scatter(): pl.pallas_call(functools.partial(scatter_kernel, items, sizes), out_shape...  249 us
    dot_general x10, matrix products, transposed_left(): lax.dot_general(left, right, (((0,), (0,)), ((), ())), preferred_element_...  95.1 us
    dot_general x9, matrix products, transposed_right(): lax.dot_general(left, right, (((1,), (1,)), ((), ())), preferred_element_...  90.1 us
    pallas_call x1, Pallas kernels, attention_backward(): pl.pallas_call(functools.partial(attend_back_kernel, tokens, span, scale)...  88.7 us
    dot_general x8, matrix products, dot(): return jnp.dot(a, b, preferred_element_type=jnp.float32)  74.6 us
    pallas_call x1, Pallas kernels, attention_forward(): pl.pallas_call(functools.partial(attend_kernel, tokens, span, scale), gri...  37.1 us
    pallas_call x2, Pallas kernels, combine(): pl.pallas_call(combine_kernel, grid=(groups // step,), out_shape=jax.Shap...  33.4 us
  transfers between devices with their start and end apart: 17, of which 1 were waited for; matrix products, arithmetic and copies ran while one was open for 33% of the time, Pallas kernels for 41%

profile of v4, /device:TPU:0, one launch (start us, length us, event | category | flops | bytes accessed | tf_op | source)
XLA Modules:
  0.0 1194.3 jit_solution(3674732583034663976)
XLA Ops:
  15.9 118.4 %shard_map.297 = (bf16[32,2,32,3072]{3,2,1,0:T(8,128)(2,1)}, bf16[32,64,576]{2,1,0:T(8,128)(2,1)}, bf16[32,16,4096]{2,1,0:T(8,128)(2,1)}, bf16[32,2,32,2048]{3,2,1,0:T(8,128)(2,1)}, bf16[32,64,128]{2,1,0:T(8,128)(2,1)}) custom-call(bf16[2,32,3072]{2,1,0:T(8,128)(2,1)} %pad_maximum_fusion.16.refs_0_, bf16[64,576]{1,0:T(8,128)(2,1)} %refs_1_.1, ...), custom_call_target="tpu_custom_call" | custom-call | bytes 1753088 | tf_op jit(solution)/shard_map/pallas_call | solution.py:276
  135.6 2.5 slice_convert_fusion.3
  138.8 2.8 fusion.105
  143.9 46.0 %shard_map.298 = (bf16[16,256,640]{2,1,0:T(8,128)(2,1)}, s32[16,8,256]{2,1,0:T(8,128)}) custom-call(bf16[256,640]{1,0:T(8,128)(2,1)} %maximum_maximum_fusion.refs_0_, s32[8,256]{1,0:T(8,128)} %pad.30.refs_1_), custom_call_target="tpu_custom_call" | custom-call | bytes 335872 | tf_op jit(solution)/shard_map/pallas_call | solution.py:276
  197.4 4.0 all-to-all-start
  209.1 2.7 copy.158.bias
  213.7 6.8 fusion.104
  222.7 37.1 %shard_map.299 = bf16[256,2048]{1,0:T(8,128)(2,1)} custom-call(bf16[256,2048]{1,0:T(8,128)(2,1)} %slice.248.qn, bf16[256,512]{1,0:T(8,128)(2,1)} %get-tuple-element.232.qa, bf16[256,512]{1,0:T(8,128)(2,1)} %get-tuple-element.231.qb, bf16[16,256,640]{2,1,0:T(8,128)(2,1)} %get-tuple-element.73.line, bf16[512,4096]{1,0:T(8,128)(2,1)} %bitcast.244, ...), custom_call_target="tpu_custom_call" | custom-call | flops 1000000000 | bytes 1000000 | tf_op jit(solution)/shard_map/pallas_call | solution.py:737
  259.8 6.6 multiply_reduce_fusion.2
  269.7 99.4 %shard_map.300 = (bf16[16,4,64,2048]{3,2,1,0:T(8,128)(2,1)}, f32[16,16,256]{2,1,0:T(8,128)}) custom-call(bf16[4,64,2048]{2,1,0:T(8,128)(2,1)} %bitcast.238, f32[16,256]{1,0:T(8,128)} %fusion.95.refs_1_), custom_call_target="tpu_custom_call" | custom-call | bytes 1064960 | tf_op jit(solution)/shard_map/pallas_call | solution.py:276
  371.3 11.4 convolution_convert_fusion.9
  388.3 17.4 %collective-permute-done.3 = bf16[1024,352]{0,1:T(8,128)(2,1)S(1)} collective-permute-done((bf16[1024,352]{0,1:T(8,128)(2,1)}, bf16[1024,352]{0,1:T(8,128)(2,1)S(1)}, u32[]{:S(2)}, u32[]{:S(2)}) %collective-permute-start.3) | collective-permute-done | bytes 720928 | tf_op jit(solution)/shard_map/ppermute | solution.py:535
  409.6 14.8 %convolution_convert_fusion.8 = bf16[4096,512]{1,0:T(8,128)(2,1)} fusion(bf16[4096,2048]{1,0:T(8,128)(2,1)} %bitcast.214, bf16[2048,512]{0,1:T(8,128)(2,1)S(1)} %bitcast.205), kind=kOutput, calls=%fused_computation.34 | convolution fusion | flops 8592031744 | bytes 23068672 | tf_op jit(solution)/shard_map/dot_general | solution.py:529
  424.5 2.5 broadcast_select_fusion.5
  427.2 7.1 broadcast_select_fusion.3
  434.2 5.2 broadcast_select_fusion.1
  439.5 13.3 %convolution_convert_fusion.6 = bf16[1792,1408]{1,0:T(8,128)(2,1)} fusion(bf16[1792,2048]{1,0:T(8,128)(2,1)S(1)} %bitcast.232, bf16[1024,1408]{1,0:T(8,128)(2,1)S(1)} %get-tuple-element.225, bf16[1024,1408]{1,0:T(8,128)(2,1)S(1)} %get-tuple-element.224), kind=kOutput, calls=%fused_computation.27 | convolution fusion | flops 10348822528 | bytes 18153472 | tf_op jit(solution)/shard_map/dot_general | solution.py:529
  452.8 13.6 %convolution_convert_fusion.5 = bf16[1792,1408]{1,0:T(8,128)(2,1)} fusion(bf16[1792,2048]{1,0:T(8,128)(2,1)S(1)} %bitcast.233, bf16[1024,1408]{1,0:T(8,128)(2,1)S(1)} %copy-done.32, bf16[1024,1408]{1,0:T(8,128)(2,1)S(1)} %copy-done.31), kind=kOutput, calls=%fused_computation.26 | convolution fusion | flops 10348822528 | bytes 18153472 | tf_op jit(solution)/shard_map/dot_general | solution.py:529
  466.4 16.0 %convolution_convert_fusion.4 = bf16[1792,2048]{1,0:T(8,128)(2,1)} fusion(bf16[1408,1024]{1,0:T(8,128)(2,1)S(1)} %copy-done.35, bf16[1408,1024]{1,0:T(8,128)(2,1)S(1)} %copy-done.33, bf16[1792,1408]{1,0:T(8,128)(2,1)} %convolution_convert_fusion.5, bf16[1792,1408]{1,0:T(8,128)(2,1)S(1)} %copy-done.85), kind=kOutput, calls=%fused_computation.25 | convolution fusion | flops 10370154496 | bytes 23199744 | tf_op jit(solution)/shard_map/dot_general | solution.py:529
  482.5 6.4 convolution_convert_fusion.14
  489.0 6.4 convolution_convert_fusion.13
  495.4 7.1 fusion.2
  503.7 7.5 fusion
  511.1 5.9 fusion.45
  517.1 5.8 fusion.16
  522.9 14.8 %shard_map.301 = bf16[4096,2048]{1,0:T(8,128)(2,1)} custom-call(bf16[16,256,112]{2,1,0:T(8,128)(2,1)S(1)} %copy-done, bf16[16,112,2048]{2,1,0:T(8,128)(2,1)} %bitcast.218, bf16[4096,256]{1,0:T(8,128)(2,1)S(1)} %get-tuple-element.230.left, bf16[256,2048]{1,0:T(8,128)(2,1)S(1)} %fusion.36.right), custom_call_target="tpu_custom_call" | custom-call | flops 6174015488 | bytes 33554432 | tf_op jit(solution)/shard_map/pallas_call | solution.py:805
  537.8 5.9 fusion.106
  543.7 6.6 fusion.107
  553.0 12.9 %convolution_convert_fusion.11 = bf16[2048,512]{1,0:T(8,128)(2,1)S(1)} fusion(bf16[4096,2048]{1,0:T(8,128)(2,1)S(1)} %bitcast.217, bf16[4096,256]{1,0:T(8,128)(2,1)} %get-tuple-element.217, bf16[4096,256]{1,0:T(8,128)(2,1)} %get-tuple-element.216), kind=kOutput, calls=%fused_computation.59 | convolution fusion | flops 8599371776 | bytes 23068672 | tf_op jit(solution)/shard_map/dot_general | solution.py:72
  568.7 6.2 all-to-all-start.1
  575.0 22.4 %convolution_convert_fusion.7 = bf16[1408,2048]{1,0:T(8,128)(2,1)S(1)} fusion(f32[1792]{0:T(1024)S(1)} %mul.443, bf16[1792,1024]{1,0:T(8,128)(2,1)} %bitcast.223, bf16[1792,1024]{1,0:T(8,128)(2,1)} %bitcast.220, bf16[1792,1408]{1,0:T(8,128)(2,1)} %convolution_convert_fusion.5, bf16[1792,1408]{1,0:T(8,128)(2,1)} %convolution_convert_fusion.6), kind=kOutput, calls=%fused_computation.28 | convolution fusion | flops 10379853824 | bytes 23206912 | tf_op jit(solution)/shard_map/dot_general | solution.py:72
  597.4 3.2 constant_dynamic-slice_fusion.2
  602.2 22.5 %fusion.9 = (bf16[1792,1408]{1,0:T(8,128)(2,1)}, f32[1792,1408]{1,0:T(8,128)}) fusion(bf16[1792,1408]{1,0:T(8,128)(2,1)} %convolution_convert_fusion.6, bf16[1792,1408]{1,0:T(8,128)(2,1)} %convolution_convert_fusion.5, bf16[1408,1024]{1,0:T(8,128)(2,1)} %get-tuple-element.229, bf16[1408,1024]{1,0:T(8,128)(2,1)S(1)} %copy-done.34, f32[1792]{0:T(1024)S(1)} %mul.443, ...), kind=kOutput, calls=%fused_computation.20 | convolution fusion | flops 10401120256 | bytes 38345728 | tf_op jit(solution)/shard_map/dot_general | solution.py:78
  624.7 18.3 %convolution_convert_fusion.2 = bf16[2048,1408]{1,0:T(8,128)(2,1)S(1)} fusion(bf16[1792,2048]{1,0:T(8,128)(2,1)} %bitcast.228, f32[1792,1408]{1,0:T(8,128)} %get-tuple-element.272, bf16[1792,1408]{1,0:T(8,128)(2,1)} %convolution_convert_fusion.6), kind=kOutput, calls=%fused_computation.23 | convolution fusion | flops 10355310592 | bytes 28246016 | tf_op jit(solution)/shard_map/dot_general | solution.py:72
  643.0 3.4 constant_dynamic-slice_fusion.4
  647.6 14.5 %convolution_convert_fusion.3 = bf16[2048,1408]{1,0:T(8,128)(2,1)S(1)} fusion(bf16[1792,2048]{1,0:T(8,128)(2,1)} %bitcast.229, bf16[1792,1408]{1,0:T(8,128)(2,1)S(1)} %copy-done.83), kind=kOutput, calls=%fused_computation.24 | convolution fusion | flops 10337648640 | bytes 18153472 | tf_op jit(solution)/shard_map/dot_general | solution.py:72
  662.1 3.3 constant_dynamic-slice_fusion.6
  666.4 2.3 pad_maximum_fusion.4.left
  669.1 14.3 %fusion.18 = f32[1792,2048]{1,0:T(8,128)} fusion(bf16[1792,1408]{1,0:T(8,128)(2,1)S(1)} %copy-done.83, bf16[1024,1408]{1,0:T(8,128)(2,1)S(1)} %copy-done.30, bf16[1024,1408]{1,0:T(8,128)(2,1)S(1)} %copy-done.28), kind=kOutput, calls=%fused_computation.55 | convolution fusion | flops 10346299392 | bytes 25493504 | tf_op jit(solution)/shard_map/dot_general | solution.py:78
  683.4 20.4 %add_convert_fusion = bf16[1792,2048]{1,0:T(8,128)(2,1)} fusion(f32[1792,2048]{1,0:T(8,128)} %fusion.18, bf16[1024,1408]{1,0:T(8,128)(2,1)} %get-tuple-element.227, bf16[1024,1408]{1,0:T(8,128)(2,1)} %get-tuple-element.226, f32[1792,1408]{1,0:T(8,128)} %get-tuple-element.272, bf16[1792,1408]{1,0:T(8,128)(2,1)} %convolution_convert_fusion.6), kind=kOutput, calls=%fused_computation.10 | convolution fusion | flops 10371301376 | bytes 42926080 | tf_op jit(solution)/shard_map/dot_general | solution.py:78
  703.8 18.6 %shard_map.302 = bf16[4096,2048]{1,0:T(8,128)(2,1)} custom-call(bf16[16,256,112]{2,1,0:T(8,128)(2,1)S(1)} %copy-done.1, bf16[16,112,2048]{2,1,0:T(8,128)(2,1)} %bitcast.291, bf16[4096,512]{1,0:T(8,128)(2,1)} %pad_maximum_fusion.4.left, bf16[512,2048]{1,0:T(8,128)(2,1)S(1)} %bitcast.206), custom_call_target="tpu_custom_call" | custom-call | flops 10468982784 | bytes 33554432 | tf_op jit(solution)/shard_map/pallas_call | solution.py:805
  722.5 91.6 %shard_map.303 = f32[4,64,2048]{2,1,0:T(8,128)} custom-call(bf16[16,4,64,2048]{3,2,1,0:T(8,128)(2,1)} %bitcast.226), custom_call_target="tpu_custom_call" | custom-call | tf_op jit(solution)/shard_map/pallas_call | solution.py:485
  815.6 4.2 multiply_reduce_fusion
  819.9 4.4 fusion.22
  824.3 6.8 convolution_convert_fusion.12.grad
  831.1 2.4 convolution_convert_fusion.1
  833.5 3.9 fusion.98
  837.5 88.7 %shard_map.304 = (bf16[256,2048]{1,0:T(8,128)(2,1)}, f32[256,512]{1,0:T(8,128)}, f32[256,512]{1,0:T(8,128)}, bf16[16,256,640]{2,1,0:T(8,128)(2,1)}, bf16[512,4096]{1,0:T(8,128)(2,1)}) custom-call(bf16[256,2048]{1,0:T(8,128)(2,1)} %slice.248.qn, bf16[256,512]{1,0:T(8,128)(2,1)} %get-tuple-element.232.qa, bf16[256,512]{1,0:T(8,128)(2,1)} %get-tuple-element.231.qb, ...), custom_call_target="tpu_custom_call" | custom-call | flops 60000002048 | bytes 30000000 | tf_op jit(solution)/shard_map/pallas_call | solution.py:761
  927.7 7.9 convolution_convert_fusion
  935.6 112.5 %shard_map.305 = (f32[256,640]{1,0:T(8,128)}, f32[64,3072]{1,0:T(8,128)}, f32[16,4096]{1,0:T(8,128)}) custom-call(bf16[16,256,640]{2,1,0:T(8,128)(2,1)} %get-tuple-element.98.refs_0_, bf16[32,64,3072]{2,1,0:T(8,128)(2,1)} %bitcast.212, bf16[32,16,4096]{2,1,0:T(8,128)(2,1)} %bitcast.248), custom_call_target="tpu_custom_call" | custom-call | tf_op jit(solution)/shard_map/pallas_call | solution.py:485
  1048.3 2.8 add_convert_fusion.1
  1053.2 3.7 reshape.753
  1060.7 10.5 all-to-all-start.2
  1079.0 2.6 pad_maximum_fusion.13
  1081.6 2.5 reshape.751
  1088.4 4.3 copy.173
  1092.7 7.1 fusion.40
  1099.9 3.2 fusion.30
  1105.2 45.1 %shard_map.306 = (f32[64,576]{1,0:T(8,128)}, f32[64,128]{1,0:T(8,128)}, f32[64,1024]{1,0:T(8,128)}) custom-call(bf16[32,64,576]{2,1,0:T(8,128)(2,1)} %bitcast.234, bf16[32,64,128]{2,1,0:T(8,128)(2,1)} %bitcast.265, bf16[32,64,1024]{2,1,0:T(8,128)(2,1)} %bitcast.227), custom_call_target="tpu_custom_call" | custom-call | tf_op jit(solution)/shard_map/pallas_call | solution.py:485
  1154.8 3.4 fusion.23
  1158.3 5.1 add_bitcast_fusion.2
  1163.3 5.1 add_bitcast_fusion.1
  1170.3 5.6 add_bitcast_fusion
  1176.0 3.6 reshape.761
  (352 shorter events, 95.1 us)
Async XLA Ops:
  7.2 475.3 %all-gather.5.cloned.1.call-start = ((), (), s32[]{:S(2)}) async-start(), calls=%async_computation.7 | async-start | bytes 8912896 | tf_op jit(solution)/shard_map/all_gather | solution.py:513
  11.3 202.0 %copy-start.67 = (f32[2,128]{1,0:T(2,128)}, f32[2,128]{1,0:T(2,128)S(1)}, u32[]{:S(2)}) copy-start(f32[2,128]{1,0:T(2,128)S(1)} %fusion.31) | copy-start | bytes 3076
  13.2 125.2 %copy-start.4 = (bf16[1,2,128,2048]{3,2,1,0:T(8,128)(2,1)S(1)}, bf16[1,2,128,2048]{3,2,1,0:T(8,128)(2,1)}, u32[]{:S(2)}) copy-start(bf16[1,2,128,2048]{3,2,1,0:T(8,128)(2,1)} %param.18) | copy-start | bytes 3145732
  138.4 74.9 %copy-start.52 = (f32[2048,1]{0,1:T(1,128)}, f32[2048,1]{0,1:T(1,128)S(1)}, u32[]{:S(2)}) copy-start(f32[2048,1]{0,1:T(1,128)S(1)} %copy.192) | copy-start | bytes 24580
  138.7 51.7 %copy-start.48 = (bf16[64,2816]{1,0:T(8,128)(2,1)S(1)}, bf16[64,2816]{1,0:T(8,128)(2,1)}, u32[]{:S(2)}) copy-start(bf16[64,2816]{1,0:T(8,128)(2,1)} %param.30) | copy-start | bytes 1081348
  138.8 53.5 %copy-start.49 = (bf16[64,2816]{1,0:T(8,128)(2,1)S(1)}, bf16[64,2816]{1,0:T(8,128)(2,1)}, u32[]{:S(2)}) copy-start(bf16[64,2816]{1,0:T(8,128)(2,1)} %param.31) | copy-start | bytes 1081348
  141.7 54.1 %copy-start.73 = (f32[256]{0:T(256)}, f32[256]{0:T(256)S(1)}, u32[]{:S(2)}) copy-start(f32[256]{0:T(256)S(1)} %multiply_reduce_fusion.5) | copy-start | bytes 3076
  141.7 54.1 %copy-start.62 = (f32[256]{0:T(256)}, f32[256]{0:T(256)S(1)}, u32[]{:S(2)}) copy-start(f32[256]{0:T(256)S(1)} %fusion.79) | copy-start | bytes 3076
  142.8 62.5 %copy-start.42 = (f32[128,32]{1,0:T(8,128)}, f32[128,32]{1,0:T(8,128)S(1)}, u32[]{:S(2)}) copy-start(f32[128,32]{1,0:T(8,128)S(1)} %get-tuple-element.265) | copy-start | bytes 49156
  142.8 62.6 %copy-start.44 = (f32[128,32]{1,0:T(8,128)}, f32[128,32]{1,0:T(8,128)S(1)}, u32[]{:S(2)}) copy-start(f32[128,32]{1,0:T(8,128)S(1)} %get-tuple-element.266) | copy-start | bytes 49156
  189.9 194.7 %collective-permute-start.4 = (bf16[88,2048]{1,0:T(8,128)(2,1)}, bf16[88,2048]{1,0:T(8,128)(2,1)}, u32[]{:S(2)}, u32[]{:S(2)}) collective-permute-start(bf16[88,2048]{1,0:T(8,128)(2,1)} %param.32), channel_id=1, source_target_pairs={{0,16},{16,0},{1,17},{17,1},{2,18},{18,2},{3,19},{19,3},{4,20},{20... | collective-permute-start | bytes 1081352 | tf_op jit(solution)/shard_map/ppermute | solution.py:535
  191.7 13.2 %copy-start.79 = (s32[1,2,6]{2,1,0:T(2,128)S(1)}, s32[1,2,6]{2,1,0:T(2,128)}, u32[]{:S(2)}) copy-start(s32[1,2,6]{2,1,0:T(2,128)} %param.20) | copy-start | bytes 148
  197.4 187.3 %all-to-all-start = ((bf16[16,64,352]{2,1,0:T(8,128)(2,1)}), bf16[16,64,352]{2,1,0:T(8,128)(2,1)S(1)}, u32[]{:S(2)}, u32[]{:S(2)}) async-start(bf16[16,64,352]{2,1,0:T(8,128)(2,1)} %reshape.729), calls=%async_computation | async-start | bytes 1572864 | tf_op jit(solution)/shard_map/all_to_all | solution.py:917
  201.3 287.6 %all-gather.7.cloned.1.call-start = ((), (), s32[]{:S(2)}) async-start(), calls=%async_computation.8 | async-start | bytes 8912896 | tf_op jit(solution)/shard_map/all_gather | solution.py:513
  201.6 222.9 %collective-permute-start.1 = (bf16[1024,1408]{1,0:T(8,128)(2,1)}, bf16[1024,1408]{1,0:T(8,128)(2,1)}, u32[]{:S(2)}, u32[]{:S(2)}) collective-permute-start(bf16[1024,1408]{1,0:T(8,128)(2,1)} %bitcast.251), channel_id=1, source_target_pairs={{0,16},{16,0},{1,17},{17,1},{2,18},{18,2},{3,19},{19,3},{4,20},{20... | collective-permute-start | bytes 8650760 | tf_op jit(solution)/shard_map/ppermute | solution.py:535
  202.9 221.6 %collective-permute-start = (bf16[1024,1408]{1,0:T(8,128)(2,1)}, bf16[1024,1408]{1,0:T(8,128)(2,1)}, u32[]{:S(2)}, u32[]{:S(2)}) collective-permute-start(bf16[1024,1408]{1,0:T(8,128)(2,1)} %bitcast.249), channel_id=1, source_target_pairs={{0,16},{16,0},{1,17},{17,1},{2,18},{18,2},{3,19},{19,3},{4,20},{20... | collective-permute-start | bytes 8650760 | tf_op jit(solution)/shard_map/ppermute | solution.py:535
  203.7 220.8 %collective-permute-start.2 = (bf16[1408,1024]{1,0:T(8,128)(2,1)}, bf16[1408,1024]{1,0:T(8,128)(2,1)}, u32[]{:S(2)}, u32[]{:S(2)}) collective-permute-start(bf16[1408,1024]{1,0:T(8,128)(2,1)} %bitcast.253), channel_id=1, source_target_pairs={{0,16},{16,0},{1,17},{17,1},{2,18},{18,2},{3,19},{19,3},{4,20},{20... | collective-permute-start | bytes 8650760 | tf_op jit(solution)/shard_map/ppermute | solution.py:535
  205.7 15.9 %copy-start.18 = (f32[256,512]{1,0:T(8,128)}, f32[256,512]{1,0:T(8,128)S(1)}, u32[]{:S(2)}) copy-start(f32[256,512]{1,0:T(8,128)S(1)} %copy.152) | copy-start | bytes 1572868
  206.0 15.6 %copy-start.20 = (f32[256,512]{1,0:T(8,128)}, f32[256,512]{1,0:T(8,128)S(1)}, u32[]{:S(2)}) copy-start(f32[256,512]{1,0:T(8,128)S(1)} %copy.150) | copy-start | bytes 1572868
  213.3 53.2 %copy-start.56 = (f32[2048,1]{0,1:T(1,128)}, f32[2048,1]{0,1:T(1,128)S(1)}, u32[]{:S(2)}) copy-start(f32[2048,1]{0,1:T(1,128)S(1)} %copy.193) | copy-start | bytes 24580
  266.4 116.2 %copy-start.76 = (f32[256]{0:T(256)}, f32[256]{0:T(256)S(1)}, u32[]{:S(2)}) copy-start(f32[256]{0:T(256)S(1)} %get-tuple-element.267) | copy-start | bytes 3076
  266.5 102.9 %copy-start.55 = (s32[16,8,256]{2,1,0:T(8,128)S(1)}, s32[16,8,256]{2,1,0:T(8,128)}, u32[]{:S(2)}) copy-start(s32[16,8,256]{2,1,0:T(8,128)} %get-tuple-element.76) | copy-start | bytes 393220
  266.5 102.9 %copy-start.71 = (f32[256]{0:T(256)}, f32[256]{0:T(256)S(1)}, u32[]{:S(2)}) copy-start(f32[256]{0:T(256)S(1)} %fusion.80) | copy-start | bytes 3076
  369.1 450.8 %reduce-scatter.3.cloned.1.call-start = ((), (), s32[]{:S(2)}) async-start(), calls=%async_computation.5 | async-start | bytes 17825792 | tf_op jit(solution)/shard_map/reduce_scatter | solution.py:517
  385.8 19.9 %collective-permute-start.3 = (bf16[1024,352]{0,1:T(8,128)(2,1)}, bf16[1024,352]{0,1:T(8,128)(2,1)S(1)}, u32[]{:S(2)}, u32[]{:S(2)}) collective-permute-start(bf16[1024,352]{0,1:T(8,128)(2,1)} %copy.162), channel_id=1, source_target_pairs={{0,16},{16,0},{1,17},{17,1},{2,18},{18,2},{3,19},{19,3},{4,20},{20... | collective-permute-start | bytes 2162696 | tf_op jit(solution)/shard_map/ppermute | solution.py:535
  409.6 14.9 %copy-start.2 = (bf16[2048,2,256]{0,2,1:T(8,128)(2,1)}, bf16[2048,2,256]{0,2,1:T(8,128)(2,1)S(1)}, u32[]{:S(2)}) copy-start(bf16[2048,2,256]{0,2,1:T(8,128)(2,1)S(1)} %pad.31) | copy-start | bytes 6291460
  409.6 14.9 %copy-start.24 = (bf16[1,1024,1408]{2,1,0:T(8,128)(2,1)S(1)}, bf16[1,1024,1408]{2,1,0:T(8,128)(2,1)}, u32[]{:S(2)}) copy-start(bf16[1,1024,1408]{2,1,0:T(8,128)(2,1)} %param.33) | copy-start | bytes 8650756
  427.2 12.3 %copy-start.27 = (bf16[1024,1408]{1,0:T(8,128)(2,1)}, bf16[1024,1408]{1,0:T(8,128)(2,1)S(1)}, u32[]{:S(2)}) copy-start(bf16[1024,1408]{1,0:T(8,128)(2,1)S(1)} %get-tuple-element.224) | copy-start | bytes 8650756
  427.2 12.3 %copy-start.29 = (bf16[1024,1408]{1,0:T(8,128)(2,1)}, bf16[1024,1408]{1,0:T(8,128)(2,1)S(1)}, u32[]{:S(2)}) copy-start(bf16[1024,1408]{1,0:T(8,128)(2,1)S(1)} %get-tuple-element.225) | copy-start | bytes 8650756
  427.2 12.3 %slice-start.6 = ((s8[7340032]{0:T(1024)(128)(4,1)}), s8[4194304]{0:T(1024)(128)(4,1)S(1)}, s32[]{:S(2)}) async-start(s8[7340032]{0:T(1024)(128)(4,1)} %bitcast.230), calls=%async_computation.15 | async-start | bytes 8388608
  439.5 13.3 %copy-start.31 = (bf16[1024,1408]{1,0:T(8,128)(2,1)S(1)}, bf16[1024,1408]{1,0:T(8,128)(2,1)}, u32[]{:S(2)}) copy-start(bf16[1024,1408]{1,0:T(8,128)(2,1)} %get-tuple-element.226) | copy-start | bytes 8650756
  439.5 13.3 %copy-start.32 = (bf16[1024,1408]{1,0:T(8,128)(2,1)S(1)}, bf16[1024,1408]{1,0:T(8,128)(2,1)}, u32[]{:S(2)}) copy-start(bf16[1024,1408]{1,0:T(8,128)(2,1)} %get-tuple-element.227) | copy-start | bytes 8650756
  452.8 13.6 %copy-start.33 = (bf16[1408,1024]{1,0:T(8,128)(2,1)S(1)}, bf16[1408,1024]{1,0:T(8,128)(2,1)}, u32[]{:S(2)}) copy-start(bf16[1408,1024]{1,0:T(8,128)(2,1)} %get-tuple-element.228) | copy-start | bytes 8650756
  452.8 13.6 %copy-start.35 = (bf16[1408,1024]{1,0:T(8,128)(2,1)S(1)}, bf16[1408,1024]{1,0:T(8,128)(2,1)}, u32[]{:S(2)}) copy-start(bf16[1408,1024]{1,0:T(8,128)(2,1)} %get-tuple-element.229) | copy-start | bytes 8650756
  452.8 13.6 %copy-start.85 = (bf16[1792,1408]{1,0:T(8,128)(2,1)S(1)}, bf16[1792,1408]{1,0:T(8,128)(2,1)}, u32[]{:S(2)}) copy-start(bf16[1792,1408]{1,0:T(8,128)(2,1)} %convolution_convert_fusion.6) | copy-start | bytes 15138820
  503.7 13.4 %slice-start = ((s8[8388608]{0:T(1024)(128)(4,1)}), s8[4194304]{0:T(1024)(128)(4,1)S(1)}, s32[]{:S(2)}) async-start(s8[8388608]{0:T(1024)(128)(4,1)} %bitcast.209), calls=%async_computation.9 | async-start | bytes 8388608
  537.8 15.2 %slice-start.2 = ((s8[16777216]{0:T(1024)(128)(4,1)}), s8[4194304]{0:T(1024)(128)(4,1)S(1)}, s32[]{:S(2)}) async-start(s8[16777216]{0:T(1024)(128)(4,1)} %bitcast.215), calls=%async_computation.11 | async-start | bytes 8388608
  537.8 15.2 %slice-start.3 = ((s8[16777216]{0:T(1024)(128)(4,1)}), s8[4194304]{0:T(1024)(128)(4,1)S(1)}, s32[]{:S(2)}) async-start(s8[16777216]{0:T(1024)(128)(4,1)} %bitcast.215), calls=%async_computation.12 | async-start | bytes 8388608
  543.7 9.3 slice-start.4
  551.3 496.9 %collective-permute-start.8 = (bf16[88,2048]{1,0:T(8,128)(2,1)}, bf16[88,2048]{1,0:T(8,128)(2,1)}, u32[]{:S(2)}, u32[]{:S(2)}) collective-permute-start(bf16[88,2048]{1,0:T(8,128)(2,1)} %get-tuple-element.251), channel_id=1, source_target_pairs={{0,16},{16,0},{1,17},{17,1},{2,18},{18,2},{3,19},{19,3},{4,20},{20... | collective-permute-start | bytes 1081352 | tf_op jit(solution)/shard_map/ppermute | solution.py:555
  567.4 480.8 %collective-permute-start.9 = (bf16[1024,512]{1,0:T(8,128)(2,1)}, bf16[1024,512]{1,0:T(8,128)(2,1)}, u32[]{:S(2)}, u32[]{:S(2)}) collective-permute-start(bf16[1024,512]{1,0:T(8,128)(2,1)} %get-tuple-element.235), channel_id=1, source_target_pairs={{0,16},{16,0},{1,17},{17,1},{2,18},{18,2},{3,19},{19,3},{4,20},{20... | collective-permute-start | bytes 3145736 | tf_op jit(solution)/shard_map/ppermute | solution.py:555
  568.7 245.4 %all-to-all-start.1 = ((f32[16,1,256]{2,1,0:T(1,128)}), f32[16,1,256]{2,1,0:T(1,128)}, u32[]{:S(2)}, u32[]{:S(2)}) async-start(f32[16,1,256]{2,1,0:T(1,128)} %all_to_all.15), calls=%async_computation.2 | async-start | bytes 32768 | tf_op jit(solution)/shard_map/all_to_all | solution.py:1043
  574.9 609.5 %reduce-scatter.5.cloned.1.call-start = ((), (), s32[]{:S(2)}) async-start(), calls=%async_computation.6 | async-start | bytes 4325376 | tf_op jit(solution)/shard_map/reduce_scatter | solution.py:1097
  600.6 447.7 %collective-permute-start.7 = (bf16[1408,1024]{1,0:T(8,128)(2,1)}, bf16[1408,1024]{1,0:T(8,128)(2,1)}, u32[]{:S(2)}, u32[]{:S(2)}) collective-permute-start(bf16[1408,1024]{1,0:T(8,128)(2,1)} %get-tuple-element.218), channel_id=1, source_target_pairs={{0,16},{16,0},{1,17},{17,1},{2,18},{18,2},{3,19},{19,3},{4,20},{20... | collective-permute-start | bytes 8650760 | tf_op jit(solution)/shard_map/ppermute | solution.py:555
  646.4 401.8 %collective-permute-start.6 = (bf16[1024,1408]{1,0:T(8,128)(2,1)}, bf16[1024,1408]{1,0:T(8,128)(2,1)}, u32[]{:S(2)}, u32[]{:S(2)}) collective-permute-start(bf16[1024,1408]{1,0:T(8,128)(2,1)} %get-tuple-element.220), channel_id=1, source_target_pairs={{0,16},{16,0},{1,17},{17,1},{2,18},{18,2},{3,19},{19,3},{4,20},{20... | collective-permute-start | bytes 8650760 | tf_op jit(solution)/shard_map/ppermute | solution.py:555
  665.4 382.9 %collective-permute-start.5 = (bf16[1024,1408]{1,0:T(8,128)(2,1)}, bf16[1024,1408]{1,0:T(8,128)(2,1)}, u32[]{:S(2)}, u32[]{:S(2)}) collective-permute-start(bf16[1024,1408]{1,0:T(8,128)(2,1)} %get-tuple-element.222), channel_id=1, source_target_pairs={{0,16},{16,0},{1,17},{17,1},{2,18},{18,2},{3,19},{19,3},{4,20},{20... | collective-permute-start | bytes 8650760 | tf_op jit(solution)/shard_map/ppermute | solution.py:555
  683.4 20.4 %copy-start.1 = (bf16[16,256,112]{2,1,0:T(8,128)(2,1)S(1)}, bf16[16,256,112]{2,1,0:T(8,128)(2,1)}, u32[]{:S(2)}) copy-start(bf16[16,256,112]{2,1,0:T(8,128)(2,1)} %fusion.35.picked) | copy-start | bytes 2752516
  683.4 20.4 %copy-start.3 = (bf16[2048,2,256]{0,2,1:T(8,128)(2,1)S(1)}, bf16[2048,2,256]{0,2,1:T(8,128)(2,1)}, u32[]{:S(2)}) copy-start(bf16[2048,2,256]{0,2,1:T(8,128)(2,1)} %copy-done.2) | copy-start | bytes 6291460
  722.4 91.7 %copy-start.47 = (f32[256,16]{0,1:T(8,128)S(1)}, f32[256,16]{0,1:T(8,128)}, u32[]{:S(2)}) copy-start(f32[256,16]{0,1:T(8,128)} %copy-done.46) | copy-start | bytes 49156
  722.4 91.7 %copy-start.61 = (f32[256]{0:T(256)S(1)}, f32[256]{0:T(256)}, u32[]{:S(2)}) copy-start(f32[256]{0:T(256)} %copy-done.60) | copy-start | bytes 3076
  722.4 91.7 %copy-start.70 = (f32[256]{0:T(256)S(1)}, f32[256]{0:T(256)}, u32[]{:S(2)}) copy-start(f32[256]{0:T(256)} %copy-done.69) | copy-start | bytes 3076
  722.4 93.2 %copy-start.7 = (f32[256,2048]{1,0:T(8,128)S(1)}, f32[256,2048]{1,0:T(8,128)}, u32[]{:S(2)}) copy-start(f32[256,2048]{1,0:T(8,128)} %copy-done.6) | copy-start | bytes 6291460
  722.4 93.2 %copy-start.14 = (bf16[32,64,128]{2,1,0:T(8,128)(2,1)S(1)}, bf16[32,64,128]{2,1,0:T(8,128)(2,1)}, u32[]{:S(2)}) copy-start(bf16[32,64,128]{2,1,0:T(8,128)(2,1)} %get-tuple-element.68) | copy-start | bytes 1572868
  722.4 93.2 %copy-start.57 = (f32[2048,1]{0,1:T(1,128)S(1)}, f32[2048,1]{0,1:T(1,128)}, u32[]{:S(2)}) copy-start(f32[2048,1]{0,1:T(1,128)} %copy-done.56) | copy-start | bytes 24580
  722.5 93.2 %copy-start.72 = (f32[256]{0:T(256)S(1)}, f32[256]{0:T(256)}, u32[]{:S(2)}) copy-start(f32[256]{0:T(256)} %copy-done.71) | copy-start | bytes 3076
  837.4 88.8 %copy-start.19 = (f32[256,512]{1,0:T(8,128)S(1)}, f32[256,512]{1,0:T(8,128)}, u32[]{:S(2)}) copy-start(f32[256,512]{1,0:T(8,128)} %copy-done.18) | copy-start | bytes 1572868
  837.4 88.8 %copy-start.21 = (f32[256,512]{1,0:T(8,128)S(1)}, f32[256,512]{1,0:T(8,128)}, u32[]{:S(2)}) copy-start(f32[256,512]{1,0:T(8,128)} %copy-done.20) | copy-start | bytes 1572868
  837.4 90.3 %copy-start.9 = (bf16[256,2048]{1,0:T(8,128)(2,1)S(1)}, bf16[256,2048]{1,0:T(8,128)(2,1)}, u32[]{:S(2)}) copy-start(bf16[256,2048]{1,0:T(8,128)(2,1)} %copy-done.8) | copy-start | bytes 3145732
  1048.2 9.8 copy-start.59
  1048.2 9.8 copy-start.63
  1060.7 115.2 %all-to-all-start.2 = ((bf16[16,64,352]{2,1,0:T(8,128)(2,1)}), bf16[16,64,352]{2,1,0:T(8,128)(2,1)}, u32[]{:S(2)}, u32[]{:S(2)}) async-start(bf16[16,64,352]{2,1,0:T(8,128)(2,1)} %reshape.753), calls=%async_computation.4 | async-start | bytes 1572864 | tf_op jit(solution)/shard_map/all_to_all | solution.py:1135
  1105.1 49.6 %copy-start.68 = (f32[2,128]{1,0:T(2,128)S(1)}, f32[2,128]{1,0:T(2,128)}, u32[]{:S(2)}) copy-start(f32[2,128]{1,0:T(2,128)} %copy-done.67) | copy-start | bytes 3076
  1105.1 49.6 %copy-start.74 = (f32[256]{0:T(256)S(1)}, f32[256]{0:T(256)}, u32[]{:S(2)}) copy-start(f32[256]{0:T(256)} %get-tuple-element.203) | copy-start | bytes 3076
  1105.1 49.7 %copy-start.66 = (f32[256]{0:T(256)S(1)}, f32[256]{0:T(256)}, u32[]{:S(2)}) copy-start(f32[256]{0:T(256)} %copy-done.64) | copy-start | bytes 3076
  (47 other events, 244.1 us)
Sparse Core Ops, SparseCore 0:
  190.1 88.4 all-gather.4
  369.2 74.9 all-gather.6
  537.9 180.0 reduce-scatter.2
  837.5 155.2 reduce-scatter.4

commit v5 on v4

--- a/solution.py
+++ b/solution.py
@@ -988,9 +988,6 @@
     expert_gate, expert_up = joined(fetched[0], 0), joined(fetched[1], 0)
     expert_down = joined(fetched[2], 1)
     padded = -(-mine // 128) * 128
-    shared_in = jnp.pad(
-        joined(fetched[3], 0).reshape(D, 2, mine), ((0, 0), (0, 0), (0, padded - mine))
-    ).reshape(D, 2 * padded)
     shared_out_weight = jnp.pad(joined(fetched[4], 0), ((0, padded - mine), (0, 0)))
     total_rows = n_expert * rows
     capacity = (9 * tokens * TOP + 8 * experts_count - 1) // (8 * experts_count)
@@ -1006,7 +1003,6 @@
     picked_bool = place == jnp.arange(slots, dtype=jnp.int32)[None, :, None]
     picked = picked_bool.astype(jnp.bfloat16)
     picked_float = picked_bool.astype(jnp.float32)
-    shared_pre = low(dot(all_normed, shared_in))
     gate_rows = lax.dynamic_index_in_dim(all_probs, lane, 1, keepdims=False)
     gate_slots = jnp.sum(
         picked_float * gate_rows.reshape(groups, 1, group_rows), axis=2
@@ -1025,6 +1021,11 @@
     arrived = to_slots(all_normed)
     gate_pre = low(dot(arrived, expert_gate))
     up_pre = low(dot(arrived, expert_up))
+    parts_in, gate_pre = lax.optimization_barrier((fetched[3], gate_pre))
+    shared_in = jnp.pad(
+        joined(parts_in, 0).reshape(D, 2, mine), ((0, 0), (0, 0), (0, padded - mine))
+    ).reshape(D, 2 * padded)
+    shared_pre = low(dot(all_normed, shared_in))
     expert_act = low(silu_product(wide(gate_pre), wide(up_pre)))
     expert_out = lax.optimization_barrier(low(dot(expert_act, expert_down)))
     shared_act = low(silu_product(wide(shared_pre[:, :padded]), wide(shared_pre[:, padded:])))

time: 1200 us -> 1210 us (level)
  no operation moved by 1% of the time
where the time goes in v5:
time: 1210 us; the launch traced here: 1200 us
  Pallas kernels  672 us (56%)
  matrix products  285 us (24%)
  other arithmetic  92.4 us (8%)
  local copies, waits for them, and re-layouts  82.1 us (7%)
  starting transfers between devices  32 us (3%)
  waiting for transfers between devices  17.5 us (1%)
  between operations  15.5 us (1%)
    pallas_call x3, Pallas kernels, gather(): pl.pallas_call(functools.partial(gather_kernel, items, sizes), out_shape=...  264 us
    pallas_call x3, Pallas kernels, scatter(): pl.pallas_call(functools.partial(scatter_kernel, items, sizes), out_shape...  249 us
    dot_general x10, matrix products, transposed_left(): lax.dot_general(left, right, (((0,), (0,)), ((), ())), preferred_element_...  95.2 us
    dot_general x9, matrix products, transposed_right(): lax.dot_general(left, right, (((1,), (1,)), ((), ())), preferred_element_...  90.1 us
    pallas_call x1, Pallas kernels, attention_backward(): pl.pallas_call(functools.partial(attend_back_kernel, tokens, span, scale)...  88.8 us
    dot_general x8, matrix products, dot(): return jnp.dot(a, b, preferred_element_type=jnp.float32)  75.8 us
    pallas_call x1, Pallas kernels, attention_forward(): pl.pallas_call(functools.partial(attend_kernel, tokens, span, scale), gri...  37.1 us
    pallas_call x2, Pallas kernels, combine(): pl.pallas_call(combine_kernel, grid=(groups // step,), out_shape=jax.Shap...  33.4 us
  transfers between devices with their start and end apart: 17, of which 1 were waited for; matrix products, arithmetic and copies ran while one was open for 33% of the time, Pallas kernels for 41%

profile of v5, /device:TPU:0, one launch (start us, length us, event | category | flops | bytes accessed | tf_op | source)
XLA Modules:
  0.0 1196.8 jit_solution(9230108446341653133)
XLA Ops:
  15.9 118.4 %shard_map.297 = (bf16[32,2,32,3072]{3,2,1,0:T(8,128)(2,1)}, bf16[32,64,576]{2,1,0:T(8,128)(2,1)}, bf16[32,16,4096]{2,1,0:T(8,128)(2,1)}, bf16[32,2,32,2048]{3,2,1,0:T(8,128)(2,1)}, bf16[32,64,128]{2,1,0:T(8,128)(2,1)}) custom-call(bf16[2,32,3072]{2,1,0:T(8,128)(2,1)} %pad_maximum_fusion.16.refs_0_, bf16[64,576]{1,0:T(8,128)(2,1)} %refs_1_.1, ...), custom_call_target="tpu_custom_call" | custom-call | bytes 1753088 | tf_op jit(solution)/shard_map/pallas_call | solution.py:276
  135.6 2.5 slice_convert_fusion.3
  138.8 2.8 fusion.105
  143.9 46.0 %shard_map.298 = (bf16[16,256,640]{2,1,0:T(8,128)(2,1)}, s32[16,8,256]{2,1,0:T(8,128)}) custom-call(bf16[256,640]{1,0:T(8,128)(2,1)} %maximum_maximum_fusion.refs_0_, s32[8,256]{1,0:T(8,128)} %pad.30.refs_1_), custom_call_target="tpu_custom_call" | custom-call | bytes 335872 | tf_op jit(solution)/shard_map/pallas_call | solution.py:276
  197.4 4.0 all-to-all-start
  209.1 2.7 copy.158.bias
  213.6 6.8 fusion.104
  222.7 37.1 %shard_map.299 = bf16[256,2048]{1,0:T(8,128)(2,1)} custom-call(bf16[256,2048]{1,0:T(8,128)(2,1)} %slice.248.qn, bf16[256,512]{1,0:T(8,128)(2,1)} %get-tuple-element.238.qa, bf16[256,512]{1,0:T(8,128)(2,1)} %get-tuple-element.237.qb, bf16[16,256,640]{2,1,0:T(8,128)(2,1)} %get-tuple-element.76.line, bf16[512,4096]{1,0:T(8,128)(2,1)} %bitcast.246, ...), custom_call_target="tpu_custom_call" | custom-call | flops 1000000000 | bytes 1000000 | tf_op jit(solution)/shard_map/pallas_call | solution.py:737
  259.8 6.6 multiply_reduce_fusion.2
  269.7 99.4 %shard_map.300 = (bf16[16,4,64,2048]{3,2,1,0:T(8,128)(2,1)}, f32[16,16,256]{2,1,0:T(8,128)}) custom-call(bf16[4,64,2048]{2,1,0:T(8,128)(2,1)} %bitcast.240, f32[16,256]{1,0:T(8,128)} %fusion.95.refs_1_), custom_call_target="tpu_custom_call" | custom-call | bytes 1064960 | tf_op jit(solution)/shard_map/pallas_call | solution.py:276
  371.3 11.4 convolution_convert_fusion.9
  388.3 17.4 %collective-permute-done = bf16[1024,352]{0,1:T(8,128)(2,1)S(1)} collective-permute-done((bf16[1024,352]{0,1:T(8,128)(2,1)}, bf16[1024,352]{0,1:T(8,128)(2,1)S(1)}, u32[]{:S(2)}, u32[]{:S(2)}) %collective-permute-start) | collective-permute-done | bytes 720928 | tf_op jit(solution)/shard_map/ppermute | solution.py:535
  405.7 2.3 broadcast_select_fusion.5
  410.5 13.1 %convolution_convert_fusion.6 = bf16[1792,1408]{1,0:T(8,128)(2,1)} fusion(bf16[1792,2048]{1,0:T(8,128)(2,1)S(1)} %bitcast.232, bf16[1024,1408]{1,0:T(8,128)(2,1)S(1)} %get-tuple-element.231, bf16[1024,1408]{1,0:T(8,128)(2,1)S(1)} %get-tuple-element.230), kind=kOutput, calls=%fused_computation.27 | convolution fusion | flops 10348822528 | bytes 18153472 | tf_op jit(solution)/shard_map/dot_general | solution.py:529
  428.2 3.2 broadcast_select_fusion.3
  431.7 7.0 broadcast_select_fusion.1
  438.7 13.1 %convolution_convert_fusion.5 = bf16[1792,1408]{1,0:T(8,128)(2,1)} fusion(bf16[1792,2048]{1,0:T(8,128)(2,1)S(1)} %bitcast.235, bf16[1024,1408]{1,0:T(8,128)(2,1)S(1)} %get-tuple-element.233, bf16[1024,1408]{1,0:T(8,128)(2,1)S(1)} %get-tuple-element.232), kind=kOutput, calls=%fused_computation.26 | convolution fusion | flops 10348822528 | bytes 18153472 | tf_op jit(solution)/shard_map/dot_general | solution.py:529
  451.8 18.8 %convolution_convert_fusion.4 = bf16[1792,2048]{1,0:T(8,128)(2,1)} fusion(bf16[1408,1024]{1,0:T(8,128)(2,1)} %get-tuple-element.235, bf16[1408,1024]{1,0:T(8,128)(2,1)} %get-tuple-element.234, bf16[1792,1408]{1,0:T(8,128)(2,1)} %convolution_convert_fusion.5, bf16[1792,1408]{1,0:T(8,128)(2,1)} %convolution_convert_fusion.6), kind=kOutput, calls=%fused_computation.25 | convolution fusion | flops 10370154496 | bytes 23199744 | tf_op jit(solution)/shard_map/dot_general | solution.py:529
  470.6 14.0 %convolution_convert_fusion.8 = bf16[4096,512]{1,0:T(8,128)(2,1)} fusion(bf16[4096,2048]{1,0:T(8,128)(2,1)} %bitcast.214, bf16[2048,512]{0,1:T(8,128)(2,1)S(1)} %bitcast.205), kind=kOutput, calls=%fused_computation.34 | convolution fusion | flops 8592031744 | bytes 23068672 | tf_op jit(solution)/shard_map/dot_general | solution.py:529
  484.6 6.4 convolution_convert_fusion.14
  491.1 6.4 convolution_convert_fusion.13
  497.5 7.1 fusion.2
  505.8 7.5 fusion
  513.2 5.9 fusion.45
  519.2 5.8 fusion.16
  525.1 14.8 %shard_map.301 = bf16[4096,2048]{1,0:T(8,128)(2,1)} custom-call(bf16[16,256,112]{2,1,0:T(8,128)(2,1)S(1)} %copy-done, bf16[16,112,2048]{2,1,0:T(8,128)(2,1)} %bitcast.218, bf16[4096,256]{1,0:T(8,128)(2,1)S(1)} %get-tuple-element.236.left, bf16[256,2048]{1,0:T(8,128)(2,1)S(1)} %fusion.36.right), custom_call_target="tpu_custom_call" | custom-call | flops 6174015488 | bytes 33554432 | tf_op jit(solution)/shard_map/pallas_call | solution.py:805
  539.9 5.9 fusion.106
  545.9 6.6 fusion.107
  555.2 13.0 %convolution_convert_fusion.11 = bf16[2048,512]{1,0:T(8,128)(2,1)S(1)} fusion(bf16[4096,2048]{1,0:T(8,128)(2,1)S(1)} %bitcast.217, bf16[4096,256]{1,0:T(8,128)(2,1)} %get-tuple-element.223, bf16[4096,256]{1,0:T(8,128)(2,1)} %get-tuple-element.222), kind=kOutput, calls=%fused_computation.59 | convolution fusion | flops 8599371776 | bytes 23068672 | tf_op jit(solution)/shard_map/dot_general | solution.py:72
  570.8 6.2 all-to-all-start.1
  577.1 22.4 %convolution_convert_fusion.7 = bf16[1408,2048]{1,0:T(8,128)(2,1)S(1)} fusion(f32[1792]{0:T(1024)S(1)} %mul.443, bf16[1792,1024]{1,0:T(8,128)(2,1)} %bitcast.223, bf16[1792,1024]{1,0:T(8,128)(2,1)} %bitcast.220, bf16[1792,1408]{1,0:T(8,128)(2,1)} %convolution_convert_fusion.5, bf16[1792,1408]{1,0:T(8,128)(2,1)} %convolution_convert_fusion.6), kind=kOutput, calls=%fused_computation.28 | convolution fusion | flops 10379853824 | bytes 23206912 | tf_op jit(solution)/shard_map/dot_general | solution.py:72
  599.5 3.2 constant_dynamic-slice_fusion.2
  604.3 22.5 %fusion.9 = (bf16[1792,1408]{1,0:T(8,128)(2,1)}, f32[1792,1408]{1,0:T(8,128)}) fusion(bf16[1792,1408]{1,0:T(8,128)(2,1)} %convolution_convert_fusion.6, bf16[1792,1408]{1,0:T(8,128)(2,1)} %convolution_convert_fusion.5, bf16[1408,1024]{1,0:T(8,128)(2,1)} %get-tuple-element.235, bf16[1408,1024]{1,0:T(8,128)(2,1)S(1)} %copy-done.33, f32[1792]{0:T(1024)S(1)} %mul.443, ...), kind=kOutput, calls=%fused_computation.20 | convolution fusion | flops 10401120256 | bytes 38345728 | tf_op jit(solution)/shard_map/dot_general | solution.py:78
  626.8 18.3 %convolution_convert_fusion.2 = bf16[2048,1408]{1,0:T(8,128)(2,1)S(1)} fusion(bf16[1792,2048]{1,0:T(8,128)(2,1)} %bitcast.228, f32[1792,1408]{1,0:T(8,128)} %get-tuple-element.278, bf16[1792,1408]{1,0:T(8,128)(2,1)} %convolution_convert_fusion.6), kind=kOutput, calls=%fused_computation.23 | convolution fusion | flops 10355310592 | bytes 28246016 | tf_op jit(solution)/shard_map/dot_general | solution.py:72
  645.2 3.4 constant_dynamic-slice_fusion.4
  649.7 14.5 %convolution_convert_fusion.3 = bf16[2048,1408]{1,0:T(8,128)(2,1)S(1)} fusion(bf16[1792,2048]{1,0:T(8,128)(2,1)} %bitcast.229, bf16[1792,1408]{1,0:T(8,128)(2,1)S(1)} %copy-done.81), kind=kOutput, calls=%fused_computation.24 | convolution fusion | flops 10337648640 | bytes 18153472 | tf_op jit(solution)/shard_map/dot_general | solution.py:72
  664.2 3.3 constant_dynamic-slice_fusion.6
  668.5 2.3 pad_maximum_fusion.4.left
  671.2 14.3 %fusion.18 = f32[1792,2048]{1,0:T(8,128)} fusion(bf16[1792,1408]{1,0:T(8,128)(2,1)S(1)} %copy-done.81, bf16[1024,1408]{1,0:T(8,128)(2,1)S(1)} %copy-done.30, bf16[1024,1408]{1,0:T(8,128)(2,1)S(1)} %copy-done.28), kind=kOutput, calls=%fused_computation.55 | convolution fusion | flops 10346299392 | bytes 25493504 | tf_op jit(solution)/shard_map/dot_general | solution.py:78
  685.6 20.4 %add_convert_fusion = bf16[1792,2048]{1,0:T(8,128)(2,1)} fusion(f32[1792,2048]{1,0:T(8,128)} %fusion.18, bf16[1024,1408]{1,0:T(8,128)(2,1)} %copy-done.32, bf16[1024,1408]{1,0:T(8,128)(2,1)} %copy-done.31, f32[1792,1408]{1,0:T(8,128)} %get-tuple-element.278, bf16[1792,1408]{1,0:T(8,128)(2,1)} %convolution_convert_fusion.6), kind=kOutput, calls=%fused_computation.10 | convolution fusion | flops 10371301376 | bytes 42926080 | tf_op jit(solution)/shard_map/dot_general | solution.py:78
  706.0 18.6 %shard_map.302 = bf16[4096,2048]{1,0:T(8,128)(2,1)} custom-call(bf16[16,256,112]{2,1,0:T(8,128)(2,1)S(1)} %copy-done.1, bf16[16,112,2048]{2,1,0:T(8,128)(2,1)} %bitcast.293, bf16[4096,512]{1,0:T(8,128)(2,1)} %pad_maximum_fusion.4.left, bf16[512,2048]{1,0:T(8,128)(2,1)S(1)} %bitcast.206), custom_call_target="tpu_custom_call" | custom-call | flops 10468982784 | bytes 33554432 | tf_op jit(solution)/shard_map/pallas_call | solution.py:805
  724.6 91.5 %shard_map.303 = f32[4,64,2048]{2,1,0:T(8,128)} custom-call(bf16[16,4,64,2048]{3,2,1,0:T(8,128)(2,1)} %bitcast.226), custom_call_target="tpu_custom_call" | custom-call | tf_op jit(solution)/shard_map/pallas_call | solution.py:485
  817.7 4.2 multiply_reduce_fusion
  822.0 4.4 fusion.22
  826.4 6.8 convolution_convert_fusion.12.grad
  833.2 2.4 convolution_convert_fusion.1
  835.6 3.9 fusion.98
  839.6 88.8 %shard_map.304 = (bf16[256,2048]{1,0:T(8,128)(2,1)}, f32[256,512]{1,0:T(8,128)}, f32[256,512]{1,0:T(8,128)}, bf16[16,256,640]{2,1,0:T(8,128)(2,1)}, bf16[512,4096]{1,0:T(8,128)(2,1)}) custom-call(bf16[256,2048]{1,0:T(8,128)(2,1)} %slice.248.qn, bf16[256,512]{1,0:T(8,128)(2,1)} %get-tuple-element.238.qa, bf16[256,512]{1,0:T(8,128)(2,1)} %get-tuple-element.237.qb, ...), custom_call_target="tpu_custom_call" | custom-call | flops 60000002048 | bytes 30000000 | tf_op jit(solution)/shard_map/pallas_call | solution.py:761
  929.8 7.9 convolution_convert_fusion
  937.8 112.3 %shard_map.305 = (f32[256,640]{1,0:T(8,128)}, f32[64,3072]{1,0:T(8,128)}, f32[16,4096]{1,0:T(8,128)}) custom-call(bf16[16,256,640]{2,1,0:T(8,128)(2,1)} %get-tuple-element.104.refs_0_, bf16[32,64,3072]{2,1,0:T(8,128)(2,1)} %bitcast.212, bf16[32,16,4096]{2,1,0:T(8,128)(2,1)} %bitcast.250), custom_call_target="tpu_custom_call" | custom-call | tf_op jit(solution)/shard_map/pallas_call | solution.py:485
  1050.1 2.8 add_convert_fusion.1
  1055.0 3.7 reshape.753
  1062.6 11.1 all-to-all-start.2
  1081.5 2.6 pad_maximum_fusion.13
  1084.1 2.5 reshape.751
  1090.8 4.3 copy.173
  1095.2 7.1 fusion.40
  1102.3 3.2 fusion.30
  1107.6 45.1 %shard_map.306 = (f32[64,576]{1,0:T(8,128)}, f32[64,128]{1,0:T(8,128)}, f32[64,1024]{1,0:T(8,128)}) custom-call(bf16[32,64,576]{2,1,0:T(8,128)(2,1)} %bitcast.236, bf16[32,64,128]{2,1,0:T(8,128)(2,1)} %bitcast.267, bf16[32,64,1024]{2,1,0:T(8,128)(2,1)} %bitcast.227), custom_call_target="tpu_custom_call" | custom-call | tf_op jit(solution)/shard_map/pallas_call | solution.py:485
  1157.3 3.4 fusion.23
  1160.7 5.1 add_bitcast_fusion.2
  1165.8 5.1 add_bitcast_fusion.1
  1172.8 5.6 add_bitcast_fusion
  1178.4 3.6 reshape.761
  (351 shorter events, 98.4 us)
Async XLA Ops:
  7.2 477.4 %all-gather.5.cloned.1.call-start = ((), (), s32[]{:S(2)}) async-start(), calls=%async_computation.7 | async-start | bytes 8912896 | tf_op jit(solution)/shard_map/all_gather | solution.py:513
  11.3 201.9 %copy-start.65 = (f32[2,128]{1,0:T(2,128)}, f32[2,128]{1,0:T(2,128)S(1)}, u32[]{:S(2)}) copy-start(f32[2,128]{1,0:T(2,128)S(1)} %fusion.31) | copy-start | bytes 3076
  13.2 125.2 %copy-start.4 = (bf16[1,2,128,2048]{3,2,1,0:T(8,128)(2,1)S(1)}, bf16[1,2,128,2048]{3,2,1,0:T(8,128)(2,1)}, u32[]{:S(2)}) copy-start(bf16[1,2,128,2048]{3,2,1,0:T(8,128)(2,1)} %param.18) | copy-start | bytes 3145732
  138.4 74.9 %copy-start.50 = (f32[2048,1]{0,1:T(1,128)}, f32[2048,1]{0,1:T(1,128)S(1)}, u32[]{:S(2)}) copy-start(f32[2048,1]{0,1:T(1,128)S(1)} %copy.192) | copy-start | bytes 24580
  138.7 51.7 %copy-start.46 = (bf16[64,2816]{1,0:T(8,128)(2,1)S(1)}, bf16[64,2816]{1,0:T(8,128)(2,1)}, u32[]{:S(2)}) copy-start(bf16[64,2816]{1,0:T(8,128)(2,1)} %param.30) | copy-start | bytes 1081348
  138.8 53.5 %copy-start.47 = (bf16[64,2816]{1,0:T(8,128)(2,1)S(1)}, bf16[64,2816]{1,0:T(8,128)(2,1)}, u32[]{:S(2)}) copy-start(bf16[64,2816]{1,0:T(8,128)(2,1)} %param.31) | copy-start | bytes 1081348
  141.7 54.1 %copy-start.71 = (f32[256]{0:T(256)}, f32[256]{0:T(256)S(1)}, u32[]{:S(2)}) copy-start(f32[256]{0:T(256)S(1)} %multiply_reduce_fusion.5) | copy-start | bytes 3076
  141.7 54.1 %copy-start.60 = (f32[256]{0:T(256)}, f32[256]{0:T(256)S(1)}, u32[]{:S(2)}) copy-start(f32[256]{0:T(256)S(1)} %fusion.79) | copy-start | bytes 3076
  142.8 62.5 %copy-start.40 = (f32[128,32]{1,0:T(8,128)}, f32[128,32]{1,0:T(8,128)S(1)}, u32[]{:S(2)}) copy-start(f32[128,32]{1,0:T(8,128)S(1)} %get-tuple-element.271) | copy-start | bytes 49156
  142.8 62.6 %copy-start.42 = (f32[128,32]{1,0:T(8,128)}, f32[128,32]{1,0:T(8,128)S(1)}, u32[]{:S(2)}) copy-start(f32[128,32]{1,0:T(8,128)S(1)} %get-tuple-element.272) | copy-start | bytes 49156
  189.9 194.7 %collective-permute-start.4 = (bf16[88,2048]{1,0:T(8,128)(2,1)}, bf16[88,2048]{1,0:T(8,128)(2,1)}, u32[]{:S(2)}, u32[]{:S(2)}) collective-permute-start(bf16[88,2048]{1,0:T(8,128)(2,1)} %param.32), channel_id=1, source_target_pairs={{0,16},{16,0},{1,17},{17,1},{2,18},{18,2},{3,19},{19,3},{4,20},{20... | collective-permute-start | bytes 1081352 | tf_op jit(solution)/shard_map/ppermute | solution.py:535
  191.7 13.2 %copy-start.77 = (s32[1,2,6]{2,1,0:T(2,128)S(1)}, s32[1,2,6]{2,1,0:T(2,128)}, u32[]{:S(2)}) copy-start(s32[1,2,6]{2,1,0:T(2,128)} %param.20) | copy-start | bytes 148
  197.4 187.3 %all-to-all-start = ((bf16[16,64,352]{2,1,0:T(8,128)(2,1)}), bf16[16,64,352]{2,1,0:T(8,128)(2,1)S(1)}, u32[]{:S(2)}, u32[]{:S(2)}) async-start(bf16[16,64,352]{2,1,0:T(8,128)(2,1)} %reshape.725), calls=%async_computation | async-start | bytes 1572864 | tf_op jit(solution)/shard_map/all_to_all | solution.py:917
  201.3 289.7 %all-gather.7.cloned.1.call-start = ((), (), s32[]{:S(2)}) async-start(), calls=%async_computation.8 | async-start | bytes 8912896 | tf_op jit(solution)/shard_map/all_gather | solution.py:513
  201.6 204.1 %collective-permute-start.1 = (bf16[1024,1408]{1,0:T(8,128)(2,1)}, bf16[1024,1408]{1,0:T(8,128)(2,1)}, u32[]{:S(2)}, u32[]{:S(2)}) collective-permute-start(bf16[1024,1408]{1,0:T(8,128)(2,1)} %bitcast.251), channel_id=1, source_target_pairs={{0,16},{16,0},{1,17},{17,1},{2,18},{18,2},{3,19},{19,3},{4,20},{20... | collective-permute-start | bytes 8650760 | tf_op jit(solution)/shard_map/ppermute | solution.py:535
  202.9 202.8 %collective-permute-start.2 = (bf16[1024,1408]{1,0:T(8,128)(2,1)}, bf16[1024,1408]{1,0:T(8,128)(2,1)}, u32[]{:S(2)}, u32[]{:S(2)}) collective-permute-start(bf16[1024,1408]{1,0:T(8,128)(2,1)} %bitcast.253), channel_id=1, source_target_pairs={{0,16},{16,0},{1,17},{17,1},{2,18},{18,2},{3,19},{19,3},{4,20},{20... | collective-permute-start | bytes 8650760 | tf_op jit(solution)/shard_map/ppermute | solution.py:535
  203.7 202.0 %collective-permute-start.3 = (bf16[1408,1024]{1,0:T(8,128)(2,1)}, bf16[1408,1024]{1,0:T(8,128)(2,1)}, u32[]{:S(2)}, u32[]{:S(2)}) collective-permute-start(bf16[1408,1024]{1,0:T(8,128)(2,1)} %bitcast.255), channel_id=1, source_target_pairs={{0,16},{16,0},{1,17},{17,1},{2,18},{18,2},{3,19},{19,3},{4,20},{20... | collective-permute-start | bytes 8650760 | tf_op jit(solution)/shard_map/ppermute | solution.py:535
  205.7 15.9 %copy-start.18 = (f32[256,512]{1,0:T(8,128)}, f32[256,512]{1,0:T(8,128)S(1)}, u32[]{:S(2)}) copy-start(f32[256,512]{1,0:T(8,128)S(1)} %copy.152) | copy-start | bytes 1572868
  206.0 15.6 %copy-start.20 = (f32[256,512]{1,0:T(8,128)}, f32[256,512]{1,0:T(8,128)S(1)}, u32[]{:S(2)}) copy-start(f32[256,512]{1,0:T(8,128)S(1)} %copy.150) | copy-start | bytes 1572868
  213.3 53.2 %copy-start.54 = (f32[2048,1]{0,1:T(1,128)}, f32[2048,1]{0,1:T(1,128)S(1)}, u32[]{:S(2)}) copy-start(f32[2048,1]{0,1:T(1,128)S(1)} %copy.193) | copy-start | bytes 24580
  259.8 8.2 copy-start.13
  266.4 116.2 %copy-start.74 = (f32[256]{0:T(256)}, f32[256]{0:T(256)S(1)}, u32[]{:S(2)}) copy-start(f32[256]{0:T(256)S(1)} %get-tuple-element.273) | copy-start | bytes 3076
  266.4 102.9 %copy-start.53 = (s32[16,8,256]{2,1,0:T(8,128)S(1)}, s32[16,8,256]{2,1,0:T(8,128)}, u32[]{:S(2)}) copy-start(s32[16,8,256]{2,1,0:T(8,128)} %get-tuple-element.79) | copy-start | bytes 393220
  266.5 102.9 %copy-start.69 = (f32[256]{0:T(256)}, f32[256]{0:T(256)S(1)}, u32[]{:S(2)}) copy-start(f32[256]{0:T(256)S(1)} %fusion.80) | copy-start | bytes 3076
  369.1 452.9 %reduce-scatter.3.cloned.1.call-start = ((), (), s32[]{:S(2)}) async-start(), calls=%async_computation.5 | async-start | bytes 17825792 | tf_op jit(solution)/shard_map/reduce_scatter | solution.py:517
  385.8 19.9 %copy-start.24 = (bf16[1,1024,1408]{2,1,0:T(8,128)(2,1)S(1)}, bf16[1,1024,1408]{2,1,0:T(8,128)(2,1)}, u32[]{:S(2)}) copy-start(bf16[1,1024,1408]{2,1,0:T(8,128)(2,1)} %param.33) | copy-start | bytes 8650756
  385.8 19.9 %collective-permute-start = (bf16[1024,352]{0,1:T(8,128)(2,1)}, bf16[1024,352]{0,1:T(8,128)(2,1)S(1)}, u32[]{:S(2)}, u32[]{:S(2)}) collective-permute-start(bf16[1024,352]{0,1:T(8,128)(2,1)} %copy.162), channel_id=1, source_target_pairs={{0,16},{16,0},{1,17},{17,1},{2,18},{18,2},{3,19},{19,3},{4,20},{20... | collective-permute-start | bytes 2162696 | tf_op jit(solution)/shard_map/ppermute | solution.py:535
  388.2 22.3 %slice-start.6 = ((s8[7340032]{0:T(1024)(128)(4,1)}), s8[4194304]{0:T(1024)(128)(4,1)S(1)}, s32[]{:S(2)}) async-start(s8[7340032]{0:T(1024)(128)(4,1)} %bitcast.230), calls=%async_computation.15 | async-start | bytes 8388608
  388.3 22.2 %slice-start.7 = ((s8[7340032]{0:T(1024)(128)(4,1)}), s8[3145728]{0:T(1024)(128)(4,1)S(1)}, s32[]{:S(2)}) async-start(s8[7340032]{0:T(1024)(128)(4,1)} %bitcast.230), calls=%async_computation.16 | async-start | bytes 6291456
  428.2 42.4 %copy-start.2 = (bf16[2048,2,256]{0,2,1:T(8,128)(2,1)}, bf16[2048,2,256]{0,2,1:T(8,128)(2,1)S(1)}, u32[]{:S(2)}) copy-start(bf16[2048,2,256]{0,2,1:T(8,128)(2,1)S(1)} %pad.31) | copy-start | bytes 6291460
  428.2 10.5 slice-start.8
  505.8 13.4 %slice-start = ((s8[8388608]{0:T(1024)(128)(4,1)}), s8[4194304]{0:T(1024)(128)(4,1)S(1)}, s32[]{:S(2)}) async-start(s8[8388608]{0:T(1024)(128)(4,1)} %bitcast.209), calls=%async_computation.9 | async-start | bytes 8388608
  539.9 15.3 %slice-start.2 = ((s8[16777216]{0:T(1024)(128)(4,1)}), s8[4194304]{0:T(1024)(128)(4,1)S(1)}, s32[]{:S(2)}) async-start(s8[16777216]{0:T(1024)(128)(4,1)} %bitcast.215), calls=%async_computation.11 | async-start | bytes 8388608
  539.9 15.2 %slice-start.3 = ((s8[16777216]{0:T(1024)(128)(4,1)}), s8[4194304]{0:T(1024)(128)(4,1)S(1)}, s32[]{:S(2)}) async-start(s8[16777216]{0:T(1024)(128)(4,1)} %bitcast.215), calls=%async_computation.12 | async-start | bytes 8388608
  545.8 9.3 slice-start.4
  545.9 9.3 slice-start.5
  553.5 496.6 %collective-permute-start.8 = (bf16[88,2048]{1,0:T(8,128)(2,1)}, bf16[88,2048]{1,0:T(8,128)(2,1)}, u32[]{:S(2)}, u32[]{:S(2)}) collective-permute-start(bf16[88,2048]{1,0:T(8,128)(2,1)} %get-tuple-element.257), channel_id=1, source_target_pairs={{0,16},{16,0},{1,17},{17,1},{2,18},{18,2},{3,19},{19,3},{4,20},{20... | collective-permute-start | bytes 1081352 | tf_op jit(solution)/shard_map/ppermute | solution.py:555
  569.6 480.4 %collective-permute-start.9 = (bf16[1024,512]{1,0:T(8,128)(2,1)}, bf16[1024,512]{1,0:T(8,128)(2,1)}, u32[]{:S(2)}, u32[]{:S(2)}) collective-permute-start(bf16[1024,512]{1,0:T(8,128)(2,1)} %get-tuple-element.241), channel_id=1, source_target_pairs={{0,16},{16,0},{1,17},{17,1},{2,18},{18,2},{3,19},{19,3},{4,20},{20... | collective-permute-start | bytes 3145736 | tf_op jit(solution)/shard_map/ppermute | solution.py:555
  570.8 245.3 %all-to-all-start.1 = ((f32[16,1,256]{2,1,0:T(1,128)}), f32[16,1,256]{2,1,0:T(1,128)}, u32[]{:S(2)}, u32[]{:S(2)}) async-start(f32[16,1,256]{2,1,0:T(1,128)} %all_to_all.15), calls=%async_computation.2 | async-start | bytes 32768 | tf_op jit(solution)/shard_map/all_to_all | solution.py:1044
  577.1 609.9 %reduce-scatter.5.cloned.1.call-start = ((), (), s32[]{:S(2)}) async-start(), calls=%async_computation.6 | async-start | bytes 4325376 | tf_op jit(solution)/shard_map/reduce_scatter | solution.py:1098
  602.7 447.4 %collective-permute-start.7 = (bf16[1408,1024]{1,0:T(8,128)(2,1)}, bf16[1408,1024]{1,0:T(8,128)(2,1)}, u32[]{:S(2)}, u32[]{:S(2)}) collective-permute-start(bf16[1408,1024]{1,0:T(8,128)(2,1)} %get-tuple-element.224), channel_id=1, source_target_pairs={{0,16},{16,0},{1,17},{17,1},{2,18},{18,2},{3,19},{19,3},{4,20},{20... | collective-permute-start | bytes 8650760 | tf_op jit(solution)/shard_map/ppermute | solution.py:555
  648.6 401.5 %collective-permute-start.6 = (bf16[1024,1408]{1,0:T(8,128)(2,1)}, bf16[1024,1408]{1,0:T(8,128)(2,1)}, u32[]{:S(2)}, u32[]{:S(2)}) collective-permute-start(bf16[1024,1408]{1,0:T(8,128)(2,1)} %get-tuple-element.226), channel_id=1, source_target_pairs={{0,16},{16,0},{1,17},{17,1},{2,18},{18,2},{3,19},{19,3},{4,20},{20... | collective-permute-start | bytes 8650760 | tf_op jit(solution)/shard_map/ppermute | solution.py:555
  667.5 382.6 %collective-permute-start.5 = (bf16[1024,1408]{1,0:T(8,128)(2,1)}, bf16[1024,1408]{1,0:T(8,128)(2,1)}, u32[]{:S(2)}, u32[]{:S(2)}) collective-permute-start(bf16[1024,1408]{1,0:T(8,128)(2,1)} %get-tuple-element.228), channel_id=1, source_target_pairs={{0,16},{16,0},{1,17},{17,1},{2,18},{18,2},{3,19},{19,3},{4,20},{20... | collective-permute-start | bytes 8650760 | tf_op jit(solution)/shard_map/ppermute | solution.py:555
  685.6 20.4 %copy-start.1 = (bf16[16,256,112]{2,1,0:T(8,128)(2,1)S(1)}, bf16[16,256,112]{2,1,0:T(8,128)(2,1)}, u32[]{:S(2)}) copy-start(bf16[16,256,112]{2,1,0:T(8,128)(2,1)} %fusion.35.picked) | copy-start | bytes 2752516
  685.6 20.4 %copy-start.3 = (bf16[2048,2,256]{0,2,1:T(8,128)(2,1)S(1)}, bf16[2048,2,256]{0,2,1:T(8,128)(2,1)}, u32[]{:S(2)}) copy-start(bf16[2048,2,256]{0,2,1:T(8,128)(2,1)} %copy-done.2) | copy-start | bytes 6291460
  724.6 91.6 %copy-start.45 = (f32[256,16]{0,1:T(8,128)S(1)}, f32[256,16]{0,1:T(8,128)}, u32[]{:S(2)}) copy-start(f32[256,16]{0,1:T(8,128)} %copy-done.44) | copy-start | bytes 49156
  724.6 91.6 %copy-start.59 = (f32[256]{0:T(256)S(1)}, f32[256]{0:T(256)}, u32[]{:S(2)}) copy-start(f32[256]{0:T(256)} %copy-done.58) | copy-start | bytes 3076
  724.6 91.6 %copy-start.68 = (f32[256]{0:T(256)S(1)}, f32[256]{0:T(256)}, u32[]{:S(2)}) copy-start(f32[256]{0:T(256)} %copy-done.67) | copy-start | bytes 3076
  724.6 93.1 %copy-start.7 = (f32[256,2048]{1,0:T(8,128)S(1)}, f32[256,2048]{1,0:T(8,128)}, u32[]{:S(2)}) copy-start(f32[256,2048]{1,0:T(8,128)} %copy-done.6) | copy-start | bytes 6291460
  724.6 93.1 %copy-start.14 = (bf16[32,64,128]{2,1,0:T(8,128)(2,1)S(1)}, bf16[32,64,128]{2,1,0:T(8,128)(2,1)}, u32[]{:S(2)}) copy-start(bf16[32,64,128]{2,1,0:T(8,128)(2,1)} %get-tuple-element.71) | copy-start | bytes 1572868
  724.6 93.1 %copy-start.55 = (f32[2048,1]{0,1:T(1,128)S(1)}, f32[2048,1]{0,1:T(1,128)}, u32[]{:S(2)}) copy-start(f32[2048,1]{0,1:T(1,128)} %copy-done.54) | copy-start | bytes 24580
  724.6 93.1 %copy-start.70 = (f32[256]{0:T(256)S(1)}, f32[256]{0:T(256)}, u32[]{:S(2)}) copy-start(f32[256]{0:T(256)} %copy-done.69) | copy-start | bytes 3076
  839.5 88.8 %copy-start.19 = (f32[256,512]{1,0:T(8,128)S(1)}, f32[256,512]{1,0:T(8,128)}, u32[]{:S(2)}) copy-start(f32[256,512]{1,0:T(8,128)} %copy-done.18) | copy-start | bytes 1572868
  839.5 88.8 %copy-start.21 = (f32[256,512]{1,0:T(8,128)S(1)}, f32[256,512]{1,0:T(8,128)}, u32[]{:S(2)}) copy-start(f32[256,512]{1,0:T(8,128)} %copy-done.20) | copy-start | bytes 1572868
  839.5 90.3 %copy-start.9 = (bf16[256,2048]{1,0:T(8,128)(2,1)S(1)}, bf16[256,2048]{1,0:T(8,128)(2,1)}, u32[]{:S(2)}) copy-start(bf16[256,2048]{1,0:T(8,128)(2,1)} %copy-done.8) | copy-start | bytes 3145732
  929.8 8.0 copy-start.38
  1050.0 8.7 copy-start.41
  1050.0 8.7 copy-start.43
  1050.0 9.8 copy-start.57
  1050.0 9.8 copy-start.61
  1062.6 115.9 %all-to-all-start.2 = ((bf16[16,64,352]{2,1,0:T(8,128)(2,1)}), bf16[16,64,352]{2,1,0:T(8,128)(2,1)}, u32[]{:S(2)}, u32[]{:S(2)}) async-start(bf16[16,64,352]{2,1,0:T(8,128)(2,1)} %reshape.753), calls=%async_computation.4 | async-start | bytes 1572864 | tf_op jit(solution)/shard_map/all_to_all | solution.py:1136
  1107.6 49.7 %copy-start.66 = (f32[2,128]{1,0:T(2,128)S(1)}, f32[2,128]{1,0:T(2,128)}, u32[]{:S(2)}) copy-start(f32[2,128]{1,0:T(2,128)} %copy-done.65) | copy-start | bytes 3076
  1107.6 49.7 %copy-start.72 = (f32[256]{0:T(256)S(1)}, f32[256]{0:T(256)}, u32[]{:S(2)}) copy-start(f32[256]{0:T(256)} %get-tuple-element.209) | copy-start | bytes 3076
  1107.6 49.7 %copy-start.64 = (f32[256]{0:T(256)S(1)}, f32[256]{0:T(256)}, u32[]{:S(2)}) copy-start(f32[256]{0:T(256)} %copy-done.62) | copy-start | bytes 3076
  (46 other events, 217.1 us)
Sparse Core Ops, SparseCore 0:
  190.1 88.4 all-gather.4
  369.2 74.9 all-gather.6
  540.0 179.1 reduce-scatter.2
  839.6 154.9 reduce-scatter.4
